TPU v7x, 512 devices: a whole 4x4x16 slice. The times are simulated.
512 devices in a mesh: ctx: 32 (over y, x, core), chan: 16 (over z).
Axes of the slice: x: 4, y: 4, z: 16, core: 2. Of those that a mesh axis runs over, the one named last changes fastest.
Arguments:
- value_branch: bfloat16 [192, 262144], P(None, ('ctx', 'chan')), may hold values from -6 to 6
- key_branch: bfloat16 [192, 262144], P(None, ('ctx', 'chan')), may hold values from -6 to 6
- gate_branch: bfloat16 [192, 262144], P(None, ('ctx', 'chan')), may hold values from -6 to 6
- skip_gain: float32 [192], replicated, may hold values from -4 to 4
- spectra: float32 [2, 192, 32, 8192], P(None, 'chan', 'ctx'), may hold values from -6 to 6
Outputs:
- gated_output: bfloat16 [192, 262144], P(None, ('ctx', 'chan'))
All inputs are finite; a program needn't handle non-finite values.
Results may differ from a plain program's by a relative error of at most 0.0054.
Values may be sent and summed in bfloat16 or wider, within the bound.
No kernel may reach another device: no remote copies, remote signals or barrier semaphores. Data moves between devices by JAX's collectives and lax.ppermute only.
A program may use at most 64 MiB of HBM per device.

v0:
```python
import math

import jax
import jax.numpy as jnp
from jax import lax
from jax.sharding import PartitionSpec as P

two_pi = 2.0 * math.pi
first_factor = 128
highest = lax.Precision.HIGHEST


def reversed_bits(numbers, bit_count):
    result = numbers * 0
    for bit_number in range(bit_count):
        result = result + (numbers >> bit_number & 1) * (1 << bit_count - 1 - bit_number)
    return result


def phase_pair(radians):
    return (jnp.cos(radians), jnp.sin(radians))


def block_table(length_of, direction):
    counter = jnp.arange(length_of, dtype=jnp.int32)
    product = counter[:, None] * counter[None, :] % length_of
    cosine, sine = phase_pair(direction * two_pi / length_of * product.astype(jnp.float32))
    upper_rows = jnp.stack([cosine, -sine], axis=1)
    lower_rows = jnp.stack([sine, cosine], axis=1)
    return jnp.stack([upper_rows, lower_rows], axis=0)


def complex_mul(signal, factor):
    factor_real, factor_imag = factor
    return jnp.stack(
        [
            signal[0] * factor_real - signal[1] * factor_imag,
            signal[0] * factor_imag + signal[1] * factor_real,
        ]
    )


def forward_local(signal):
    channel_count, seq_length = (signal.shape[1], signal.shape[2])
    second_factor = seq_length // first_factor
    blocked = signal.reshape(2, channel_count, first_factor, second_factor)
    section_one = jnp.einsum(
        "orca,cxaq->oxrq", block_table(first_factor, -1.0), blocked, precision=highest
    )
    column = jnp.arange(first_factor, dtype=jnp.int32)[:, None]
    within = jnp.arange(second_factor, dtype=jnp.int32)[None, :]
    twiddle = phase_pair(-two_pi / seq_length * (column * within).astype(jnp.float32))
    section_two = complex_mul(section_one, twiddle)
    section_three = jnp.einsum(
        "peoq,oxrq->pxer", block_table(second_factor, -1.0), section_two, precision=highest
    )
    return section_three.reshape(2, channel_count, seq_length)


def inverse_local(signal):
    channel_count, seq_length = (signal.shape[1], signal.shape[2])
    second_factor = seq_length // first_factor
    blocked = signal.reshape(2, channel_count, second_factor, first_factor)
    section_one = jnp.einsum(
        "pqoe,oxer->pxqr", block_table(second_factor, 1.0), blocked, precision=highest
    )
    within = jnp.arange(second_factor, dtype=jnp.int32)[:, None]
    column = jnp.arange(first_factor, dtype=jnp.int32)[None, :]
    twiddle = phase_pair(two_pi / seq_length * (within * column).astype(jnp.float32))
    section_two = complex_mul(section_one, twiddle)
    section_three = jnp.einsum(
        "paor,oxqr->pxaq", block_table(first_factor, 1.0), section_two, precision=highest
    )
    return section_three.reshape(2, channel_count, seq_length)


def body(value_branch, key_branch, gate_branch, skip_gain, spectra):
    carried = (key_branch.astype(jnp.float32) * value_branch.astype(jnp.float32)).astype(
        jnp.bfloat16
    )
    series = lax.all_to_all(carried, "chan", split_axis=0, concat_axis=1, tiled=True)
    channel_count, seq_length = series.shape
    ctx_count = lax.axis_size("ctx")
    bit_count = ctx_count.bit_length() - 1
    device = lax.axis_index("ctx")
    total_length = seq_length * ctx_count
    counter = jnp.arange(ctx_count, dtype=jnp.int32)
    target = reversed_bits(counter, bit_count)
    blocks = lax.all_to_all(
        series.reshape(channel_count, 1, seq_length), "ctx", split_axis=2, concat_axis=1, tiled=True
    )
    matrix = jnp.stack(
        phase_pair(
            -two_pi
            / ctx_count
            * (target[:, None] * counter[None, :] % ctx_count).astype(jnp.float32)
        )
    )
    rows = jnp.einsum("ojp,xps->oxjs", matrix, blocks.astype(jnp.float32), precision=highest)
    received = lax.all_to_all(rows, "ctx", split_axis=2, concat_axis=3, tiled=True)
    signal = received.reshape(2, channel_count, seq_length)
    device_rank = reversed_bits(device, bit_count)
    positions = jnp.arange(seq_length, dtype=jnp.int32)
    radians = two_pi / total_length * (positions * device_rank).astype(jnp.float32)
    signal = complex_mul(signal, phase_pair(-radians))
    spectrum = forward_local(signal)
    shaped = complex_mul(spectrum, (spectra[0, :, 0, :], spectra[1, :, 0, :]))
    returned = complex_mul(inverse_local(shaped), phase_pair(radians))
    parts = lax.all_to_all(
        returned.reshape(2, channel_count, 1, seq_length),
        "ctx",
        split_axis=3,
        concat_axis=2,
        tiled=True,
    )
    cosine, sine = phase_pair(
        two_pi / ctx_count * (counter[:, None] * target[None, :] % ctx_count).astype(jnp.float32)
    )
    matrix = jnp.stack([cosine, -sine])
    summed = jnp.einsum("opj,oxjs->xps", matrix, parts, precision=highest) / total_length
    local_conv = summed.astype(jnp.bfloat16)
    convolved = lax.all_to_all(local_conv, "ctx", split_axis=1, concat_axis=2, tiled=True).reshape(
        channel_count, seq_length
    )
    tokens_conv = lax.all_to_all(convolved, "chan", split_axis=1, concat_axis=0, tiled=True)
    result = gate_branch.astype(jnp.float32) * (
        tokens_conv.astype(jnp.float32) + skip_gain[:, None] * carried.astype(jnp.float32)
    )
    return result.astype(jnp.bfloat16)


def solution(mesh):
    in_specs = (
        P(None, ("ctx", "chan")),
        P(None, ("ctx", "chan")),
        P(None, ("ctx", "chan")),
        P(),
        P(None, "chan", "ctx", None),
    )
    out_specs = P(None, ("ctx", "chan"))
    return jax.shard_map(body, mesh=mesh, in_specs=in_specs, out_specs=out_specs, check_vma=False)
```

profile of v0, /device:TPU:32, one launch (start us, length us, event | category | flops | bytes accessed | tf_op | source)
XLA Modules:
  0.0 260.7 jit_solution(2350406900538774972)
XLA Ops:
  0.0 1.1 multiply_convert_fusion.1
  1.1 0.7 all_to_all.24
  1.8 15.2 %all-to-all-start = ((bf16[16,12,512]{2,1,0:T(8,128)(2,1)}), bf16[16,12,512]{2,1,0:T(8,128)(2,1)S(1)}, u32[]{:S(2)}, u32[]{:S(2)}) async-start(bf16[16,12,512]{2,1,0:T(8,128)(2,1)} %all_to_all.24), calls=%async_computation | async-start | bytes 524288 | tf_op jit(solution)/shard_map/all_to_all | solution.py:81
  17.3 0.8 fusion.37
  18.2 1.2 fusion.82
  19.7 0.8 fusion.33
  20.7 0.8 fusion.39
  21.5 0.8 fusion.31
  22.2 12.7 %all-to-all-done = bf16[16,12,512]{2,1,0:T(8,128)(2,1)S(1)} async-done(((bf16[16,12,512]{2,1,0:T(8,128)(2,1)}), bf16[16,12,512]{2,1,0:T(8,128)(2,1)S(1)}, u32[]{:S(2)}, u32[]{:S(2)}) %all-to-all-start) | async-done | bytes 196640 | tf_op jit(solution)/shard_map/all_to_all | solution.py:81
  35.2 6.8 %copy.60 = bf16[12,1,8192]{0,1,2:T(2,128)(2,1)} copy(bf16[12,1,8192]{2,0,1:T(8,128)(2,1)S(1)} %reshape.821) | data formatting | bytes 393216 | tf_op jit(solution)/shard_map/reshape | solution.py:90
  42.0 0.5 broadcast.981
  42.5 45.2 %reduce = bf16[8192,12]{1,0:T(8,128)(2,1)S(1)} reduce(bf16[8192,1,12]{2,1,0:T(2,128)(2,1)} %bitcast.126, bf16[]{:T(256)} %broadcast.981), dimensions={1}, to_apply=%bitcast.119.reduce_sub_computation | reduce | bytes 393218
  87.7 4.8 %reshape.841 = bf16[32,2,1536]{2,1,0:T(2,128)(2,1)} reshape(bf16[8192,12]{1,0:T(8,128)(2,1)S(1)} %reduce) | data formatting | bytes 393216
  92.5 7.3 %all-to-all-start.1 = ((bf16[32,2,1536]{2,1,0:T(2,128)(2,1)}), bf16[32,2,1536]{2,1,0:T(2,128)(2,1)S(1)}, u32[]{:S(2)}, u32[]{:S(2)}) async-start(bf16[32,2,1536]{2,1,0:T(2,128)(2,1)} %reshape.841), calls=%async_computation.1 | async-start | bytes 393216 | tf_op jit(solution)/shard_map/all_to_all | solution.py:89
  99.8 0.7 fusion.58
  100.6 7.5 %all-to-all-done.1 = bf16[32,2,1536]{2,1,0:T(2,128)(2,1)S(1)} async-done(((bf16[32,2,1536]{2,1,0:T(2,128)(2,1)}), bf16[32,2,1536]{2,1,0:T(2,128)(2,1)S(1)}, u32[]{:S(2)}, u32[]{:S(2)}) %all-to-all-start.1) | async-done | bytes 196640 | tf_op jit(solution)/shard_map/all_to_all | solution.py:89
  108.0 8.8 %reshape.842 = bf16[8192,1,12]{2,1,0:T(2,128)(2,1)} reshape(bf16[32,2,1536]{2,1,0:T(2,128)(2,1)S(1)} %all-to-all-done.1) | data formatting | bytes 393216
  116.8 8.1 %copy.61 = bf16[12,1,8192]{2,0,1:T(8,128)(2,1)S(1)} copy(bf16[12,1,8192]{0,1,2:T(2,128)(2,1)} %bitcast.127) | data formatting | bytes 393216 | tf_op jit(solution)/shard_map/all_to_all | solution.py:89
  125.0 0.4 convolution_bitcast_fusion.4
  125.4 1.5 copy.62
  126.9 4.1 %all-to-all-start.2 = ((f32[2,12,32,256]{3,0,1,2:T(2,128)}), f32[2,12,32,256]{3,0,1,2:T(2,128)S(1)}, u32[]{:S(2)}, u32[]{:S(2)}) async-start(f32[2,12,32,256]{3,0,1,2:T(2,128)} %copy.62), calls=%async_computation.2 | async-start | bytes 1572864 | tf_op jit(solution)/shard_map/all_to_all | solution.py:100
  131.2 0.3 multiply_sine_fusion.1
  131.5 0.3 multiply_sine_fusion
  131.7 0.6 maximum_bitcast_fusion.21
  132.4 0.7 maximum_bitcast_fusion.23
  133.1 12.3 %all-to-all-done.2 = f32[2,12,32,256]{3,0,1,2:T(2,128)S(1)} async-done(((f32[2,12,32,256]{3,0,1,2:T(2,128)}), f32[2,12,32,256]{3,0,1,2:T(2,128)S(1)}, u32[]{:S(2)}, u32[]{:S(2)}) %all-to-all-start.2) | async-done | bytes 786464 | tf_op jit(solution)/shard_map/all_to_all | solution.py:100
  145.4 0.6 fusion.81
  147.0 0.9 multiply_subtract_fusion.4
  148.0 0.8 convolution_bitcast_fusion.3
  148.8 0.9 multiply_subtract_fusion.3
  149.7 1.7 convolution_bitcast_fusion.2
  151.6 0.9 convolution_bitcast_fusion.1
  152.6 0.8 convolution_bitcast_fusion
  153.8 0.5 squeeze.16
  154.6 0.5 squeeze.17
  155.1 0.7 multiply_subtract_fusion
  155.7 0.7 maximum_bitcast_fusion.8
  156.5 7.9 %copy.71 = f32[2,12,1,8192]{1,0,2,3:T(2,128)} copy(f32[2,12,1,8192]{3,0,1,2:T(2,128)S(1)} %maximum_bitcast_fusion.8) | data formatting | bytes 1572864 | tf_op jit(solution)/shard_map/reshape | solution.py:110
  164.3 15.1 %reshape.843 = f32[32,1,6144]{2,1,0:T(1,128)S(1)} reshape(f32[8192,1,2,12]{3,2,1,0:T(2,128)} %bitcast.124) | data formatting | bytes 1572864
  179.4 17.8 %all_to_all.71 = f32[32,1,6144]{2,1,0:T(1,128)S(1)} all-to-all(f32[32,1,6144]{2,1,0:T(1,128)S(1)} %reshape.843), channel_id=1, replica_groups=mesh['ctx'=32,'chan'=16] {'ctx'}, dimensions={0} | all-to-all | bytes 1572864 | tf_op jit(solution)/shard_map/all_to_all | solution.py:109
  197.3 0.5 broadcast.982
  197.8 2.5 reduce.1
  200.3 14.8 %reshape.844 = f32[8192,1,2,12]{3,2,1,0:T(2,128)} reshape(f32[32,6144]{1,0:T(8,128)S(1)} %reduce.1) | data formatting | bytes 1572864
  215.1 6.9 %copy.86 = f32[2,12,32,256]{3,2,0,1:T(8,128)S(1)} copy(f32[2,12,32,256]{1,0,3,2:T(2,128)} %bitcast.125) | data formatting | bytes 1572864 | tf_op jit(solution)/shard_map/all_to_all | solution.py:109
  222.1 0.6 fusion.2
  222.8 12.2 %all_to_all.72 = bf16[12,32,256]{2,0,1:T(8,128)(2,1)S(1)} all-to-all(bf16[12,32,256]{2,0,1:T(8,128)(2,1)S(1)} %copy.73), channel_id=1, replica_groups=mesh['ctx'=32,'chan'=16] {'ctx'}, dimensions={1} | all-to-all | bytes 393216 | tf_op jit(solution)/shard_map/all_to_all | solution.py:122
  235.2 24.5 %all_to_all.73 = bf16[12,16,512]{2,0,1:T(8,128)(2,1)S(1)} all-to-all(bf16[12,16,512]{2,0,1:T(8,128)(2,1)S(1)} %copy.75), channel_id=1, replica_groups=mesh['ctx'=32,'chan'=16] {'chan'}, dimensions={1} | all-to-all | bytes 393216 | tf_op jit(solution)/shard_map/all_to_all | solution.py:125
  259.9 0.8 multiply_convert_fusion
  (49 shorter events, 3.8 us)
Async XLA Ops:
  1.8 33.1 %all-to-all-start = ((bf16[16,12,512]{2,1,0:T(8,128)(2,1)}), bf16[16,12,512]{2,1,0:T(8,128)(2,1)S(1)}, u32[]{:S(2)}, u32[]{:S(2)}) async-start(bf16[16,12,512]{2,1,0:T(8,128)(2,1)} %all_to_all.24), calls=%async_computation | async-start | bytes 524288 | tf_op jit(solution)/shard_map/all_to_all | solution.py:81
  92.5 15.5 %all-to-all-start.1 = ((bf16[32,2,1536]{2,1,0:T(2,128)(2,1)}), bf16[32,2,1536]{2,1,0:T(2,128)(2,1)S(1)}, u32[]{:S(2)}, u32[]{:S(2)}) async-start(bf16[32,2,1536]{2,1,0:T(2,128)(2,1)} %reshape.841), calls=%async_computation.1 | async-start | bytes 393216 | tf_op jit(solution)/shard_map/all_to_all | solution.py:89
  126.9 18.5 %all-to-all-start.2 = ((f32[2,12,32,256]{3,0,1,2:T(2,128)}), f32[2,12,32,256]{3,0,1,2:T(2,128)S(1)}, u32[]{:S(2)}, u32[]{:S(2)}) async-start(f32[2,12,32,256]{3,0,1,2:T(2,128)} %copy.62), calls=%async_computation.2 | async-start | bytes 1572864 | tf_op jit(solution)/shard_map/all_to_all | solution.py:100
  146.5 3.2 %copy-start.2 = (f32[1,64,2,64]{3,1,2,0:T(8,128)S(1)}, f32[1,64,2,64]{3,1,2,0:T(8,128)}, u32[]{:S(2)}) copy-start(f32[1,64,2,64]{3,1,2,0:T(8,128)} %get-tuple-element.27) | copy-start | bytes 98308
  147.9 3.6 %copy-start = (f32[1,64,2,64]{3,1,2,0:T(8,128)S(1)}, f32[1,64,2,64]{3,1,2,0:T(8,128)}, u32[]{:S(2)}) copy-start(f32[1,64,2,64]{3,1,2,0:T(8,128)} %get-tuple-element.25) | copy-start | bytes 98308
  147.9 3.6 %copy-start.1 = (f32[1,64,2,64]{3,1,2,0:T(8,128)S(1)}, f32[1,64,2,64]{3,1,2,0:T(8,128)}, u32[]{:S(2)}) copy-start(f32[1,64,2,64]{3,1,2,0:T(8,128)} %get-tuple-element.26) | copy-start | bytes 98308
  148.0 4.5 %copy-start.6 = (f32[64,128]{1,0:T(8,128)S(1)}, f32[64,128]{1,0:T(8,128)}, u32[]{:S(2)}) copy-start(f32[64,128]{1,0:T(8,128)} %get-tuple-element.45) | copy-start | bytes 98308
  148.0 4.5 %copy-start.7 = (f32[64,128]{1,0:T(8,128)S(1)}, f32[64,128]{1,0:T(8,128)}, u32[]{:S(2)}) copy-start(f32[64,128]{1,0:T(8,128)} %get-tuple-element.46) | copy-start | bytes 98308
  152.6 2.5 copy-start.4
  152.6 2.5 copy-start.5
  215.1 6.9 %copy-start.8 = (f32[1,32,32]{2,1,0:T(8,128)S(1)}, f32[1,32,32]{2,1,0:T(8,128)}, u32[]{:S(2)}) copy-start(f32[1,32,32]{2,1,0:T(8,128)} %get-tuple-element.31) | copy-start | bytes 12292
  222.0 37.9 %copy-start.3 = (bf16[192,512]{1,0:T(8,128)(2,1)S(1)}, bf16[192,512]{1,0:T(8,128)(2,1)}, u32[]{:S(2)}) copy-start(bf16[192,512]{1,0:T(8,128)(2,1)} %param.7) | copy-start | bytes 589828
  222.0 37.9 %copy-start.9 = (f32[192]{0:T(256)S(1)}, f32[192]{0:T(256)}, u32[]{:S(2)}) copy-start(f32[192]{0:T(256)} %param.8) | copy-start | bytes 2308
where the time goes:
time: 262 us; the launch traced here: 261 us
  local copies, waits for them, and re-layouts  81.5 us (31%)
  other arithmetic  59.8 us (23%)
  blocking collectives  54.6 us (21%)
  waiting for transfers between devices  32.5 us (12%)
  starting transfers between devices  26.6 us (10%)
  matrix products  5.24 us (2%)
    unnamed x1, other arithmetic  45.2 us
    unnamed x26, local copies, waits for them, and re-layouts  44.1 us
    all_to_all x1, blocking collectives, body(): lax.all_to_all(convolved, 'chan', split_axis=1, concat_axis=0, tiled=True)  24.5 us
    all_to_all x1, blocking collectives, body(): lax.all_to_all(returned.reshape(2, channel_count, 1, seq_length), 'ctx',...  17.8 us
    all_to_all x1, starting transfers between devices, body(): lax.all_to_all(carried, 'chan', split_axis=0, concat_axis=1, tiled=True)  15.2 us
    all_to_all x1, waiting for transfers between devices, body(): lax.all_to_all(carried, 'chan', split_axis=0, concat_axis=1, tiled=True)  12.7 us
    all_to_all x1, waiting for transfers between devices, body(): lax.all_to_all(rows, 'ctx', split_axis=2, concat_axis=3, tiled=True)  12.3 us
    all_to_all x1, blocking collectives, body(): lax.all_to_all(local_conv, 'ctx', split_axis=1, concat_axis=2, tiled=True)  12.2 us
  transfers between devices with their start and end apart: 3, of which 3 were waited for; matrix products, arithmetic and copies ran while one was open for 3% of the time, Pallas kernels for 0%

commit v1 on v0

v1 whole, which is shorter than its diff:
```python
import math

import jax
import jax.numpy as jnp
import ml_dtypes
import numpy as np
from jax import lax
from jax.experimental import pallas as pl
from jax.experimental.pallas import tpu as pltpu
from jax.sharding import PartitionSpec as P

N_CTX = 32
N_CHAN = 16
CHANNELS = 192
GROUP = CHANNELS // N_CHAN
TOKENS = 512
SEQ = 8192
LENGTH = SEQ * N_CTX
LANES = 128
F32 = jnp.float32
BF16 = jnp.bfloat16
VMEM_LIMIT = 32 * 1024 * 1024


def rev5(number):
    return int(f"{number:05b}"[::-1], 2)


def c_add(a, b):
    im = a[1] if b[1] is None else (b[1] if a[1] is None else a[1] + b[1])
    return (a[0] + b[0], im)


def c_sub(a, b):
    if b[1] is None:
        im = a[1]
    else:
        im = -b[1] if a[1] is None else a[1] - b[1]
    return (a[0] - b[0], im)


def c_root(a, turn, sign):
    if turn == 0:
        return a
    if turn == 0.25:
        if a[1] is None:
            return (jnp.zeros_like(a[0]), sign * a[0])
        return (-sign * a[1], sign * a[0])
    cosine = math.cos(2 * math.pi * turn)
    sine = sign * math.sin(2 * math.pi * turn)
    if a[1] is None:
        return (a[0] * cosine, a[0] * sine)
    if turn in (0.125, 0.375):
        root = math.sqrt(0.5)
        s_c = 1.0 if cosine > 0 else -1.0
        s_s = 1.0 if sine > 0 else -1.0
        re = a[0] - a[1] if s_c * s_s > 0 else a[0] + a[1]
        im = a[0] + a[1] if s_c * s_s > 0 else a[1] - a[0]
        return (re * (s_c * root), im * (s_c * root))
    return (a[0] * cosine - a[1] * sine, a[0] * sine + a[1] * cosine)


def c_mul(a, re, im):
    return (a[0] * re - a[1] * im, a[0] * im + a[1] * re)


def fft_list(terms, sign):
    size = len(terms)
    if size == 1:
        return terms
    half = size // 2
    even = fft_list(terms[0::2], sign)
    odd = fft_list(terms[1::2], sign)
    odd = [c_root(term, index / size, sign) for index, term in enumerate(odd)]
    return [c_add(e, o) for e, o in zip(even, odd)] + [c_sub(e, o) for e, o in zip(even, odd)]


def halves_sum(x, sign_rows):
    return x * sign_rows + pltpu.roll(x, 4, 0)


def pack_kernel(key_ref, value_ref, out_ref, wide):
    low = lax.broadcasted_iota(jnp.int32, (8, LANES), 0) < 4
    for block in range(CHANNELS // 16):
        rows = slice(16 * block, 16 * block + 16)
        carried = (key_ref[rows, :].astype(F32) * value_ref[rows, :].astype(F32)).astype(BF16).astype(F32)
        for part in range(2):
            for upper in range(2):
                a = carried[8 * part : 8 * part + 8, 256 * upper : 256 * upper + 128]
                b = carried[8 * part : 8 * part + 8, 256 * upper + 128 : 256 * upper + 256]
                first = jnp.where(low, a, pltpu.roll(b, 4, 0))
                second = jnp.where(low, pltpu.roll(a, 4, 0), b)
                for offset, piece in enumerate((first, second)):
                    quad = 4 * block + 2 * part + offset
                    start = 24 * upper + 8 * (quad % 3)
                    wide[quad // 3, start : start + 8, :] = piece
    for target in range(N_CHAN):
        out_ref[target] = wide[target].astype(BF16)


def gate_kernel(conv_ref, key_ref, value_ref, gate_ref, skip_ref, out_ref, wide, flat):
    low = lax.broadcasted_iota(jnp.int32, (8, LANES), 0) < 4
    for source in range(N_CHAN):
        wide[source] = conv_ref[source].astype(F32)
    for block in range(CHANNELS // 8):
        for upper in range(2):
            pieces = []
            for offset in range(2):
                quad = 2 * block + offset
                start = 24 * upper + 8 * (quad % 3)
                pieces.append(wide[quad // 3, start : start + 8, :])
            first, second = pieces
            flat[8 * block : 8 * block + 8, 256 * upper : 256 * upper + 128] = jnp.where(
                low, first, pltpu.roll(second, 4, 0)
            )
            flat[8 * block : 8 * block + 8, 256 * upper + 128 : 256 * upper + 256] = jnp.where(
                low, pltpu.roll(first, 4, 0), second
            )
    for block in range(CHANNELS // 16):
        rows = slice(16 * block, 16 * block + 16)
        carried = (key_ref[rows, :].astype(F32) * value_ref[rows, :].astype(F32)).astype(BF16).astype(F32)
        total = flat[rows, :] + skip_ref[rows, :] * carried
        out_ref[rows, :] = (gate_ref[rows, :].astype(F32) * total).astype(BF16)


def blocks_forward_kernel(in_ref, out_ref, wide, result):
    for pair in range(N_CTX // 2):
        wide[pair] = in_ref[pair].astype(F32)
    for group in range(3):
        rows = [slice(24 * half + 8 * group, 24 * half + 8 * group + 8) for half in range(2)]
        terms = [(wide[p // 2, rows[p % 2], :], None) for p in range(N_CTX)]
        sums = fft_list(terms, -1)
        for residue in range(N_CTX):
            if residue <= N_CTX // 2:
                re, im = sums[residue]
                if im is None:
                    im = jnp.zeros_like(re)
            else:
                re, im = sums[N_CTX - residue]
                im = -im
            target = rev5(residue)
            result[target, 8 * group : 8 * group + 8, :] = re
            result[target, 24 + 8 * group : 32 + 8 * group, :] = im
    for target in range(N_CTX):
        out_ref[target] = result[target].astype(BF16)


def blocks_inverse_kernel(in_ref, out_ref, wide, result):
    for source in range(N_CTX):
        wide[source] = in_ref[source].astype(F32)
    for group in range(3):
        terms = []
        for residue in range(N_CTX):
            source = rev5(residue)
            terms.append(
                (
                    wide[source, 8 * group : 8 * group + 8, :],
                    wide[source, 24 + 8 * group : 32 + 8 * group, :],
                )
            )
        sums = fft_list(terms, 1)
        for p in range(N_CTX):
            start = 24 * (p % 2) + 8 * group
            result[p // 2, start : start + 8, :] = sums[p][0]
    for pair in range(N_CTX // 2):
        out_ref[pair] = result[pair].astype(BF16)


def split_dot(x, high, low):
    x_high = x.astype(BF16)
    x_low = (x - x_high.astype(F32)).astype(BF16)
    total = jnp.dot(x_high, high, preferred_element_type=F32)
    total += jnp.dot(x_low, high, preferred_element_type=F32)
    total += jnp.dot(x_high, low, preferred_element_type=F32)
    return total


def filter_kernel(in_ref, spectra_ref, near_ref, far_ref, matrix_ref, out_ref, wide, rows_ref):
    row = lax.broadcasted_iota(jnp.int32, (8, LANES), 0)
    low = row < 4
    sign_rows = jnp.where(low, 1.0, -1.0).astype(F32)
    for q in range(N_CTX):
        wide[q] = in_ref[q].astype(F32)

    def pair_phase(kq, sign):
        turn = 2 * math.pi * kq / 64
        return (
            jnp.where(low, 1.0, math.cos(turn)).astype(F32),
            jnp.where(low, 0.0, sign * math.sin(turn)).astype(F32),
        )

    for group in range(3):
        terms = []
        for q in range(N_CTX):
            term = (
                wide[q, 8 * group : 8 * group + 8, :],
                wide[q, 24 + 8 * group : 32 + 8 * group, :],
            )
            terms.append(c_mul(term, near_ref[0, q], near_ref[1, q]))
        sums = fft_list(terms, -1)
        for kq in range(N_CTX):
            term = sums[kq]
            if kq:
                term = c_mul(term, *pair_phase(kq, -1))
            term = (halves_sum(term[0], sign_rows), halves_sum(term[1], sign_rows))
            term = c_mul(term, far_ref[0, kq], far_ref[1, kq])
            start = 24 * kq + 8 * group
            rows_ref[start : start + 8, 0:LANES] = term[0]
            rows_ref[start : start + 8, LANES : 2 * LANES] = term[1]
    chunk = 192
    for index in range(768 // chunk):
        rows = slice(chunk * index, chunk * index + chunk)
        spectrum = split_dot(rows_ref[rows, :], matrix_ref[0], matrix_ref[1])
        re, im = spectrum[:, :LANES], spectrum[:, LANES:]
        response_re, response_im = spectra_ref[0, rows, :], spectra_ref[1, rows, :]
        shaped = jnp.concatenate(
            [re * response_re - im * response_im, re * response_im + im * response_re], axis=1
        )
        rows_ref[rows, :] = split_dot(shaped, matrix_ref[2], matrix_ref[3])
    for group in range(3):
        terms = []
        for kq in range(N_CTX):
            start = 24 * kq + 8 * group
            term = (rows_ref[start : start + 8, 0:LANES], rows_ref[start : start + 8, LANES : 2 * LANES])
            term = c_mul(term, far_ref[0, kq], -far_ref[1, kq])
            term = (halves_sum(term[0], sign_rows), halves_sum(term[1], sign_rows))
            if kq:
                term = c_mul(term, *pair_phase(kq, 1))
            terms.append(term)
        sums = fft_list(terms, 1)
        for q in range(N_CTX):
            term = c_mul(sums[q], near_ref[0, q], -near_ref[1, q])
            wide[q, 8 * group : 8 * group + 8, :] = term[0]
            wide[q, 24 + 8 * group : 32 + 8 * group, :] = term[1]
    for q in range(N_CTX):
        out_ref[q] = wide[q].astype(BF16)


def far_table():
    kq = np.arange(32)[:, None, None]
    h = (np.arange(8) // 4)[None, :, None]
    lane = np.arange(LANES)[None, None, :]
    angle = -2 * np.pi * ((lane * (kq + 32 * h)) % SEQ) / SEQ
    return np.stack([np.cos(angle), np.sin(angle)]).astype(np.float32)


def lane_matrices():
    counter = np.arange(LANES)
    angle = 2 * np.pi * ((counter[:, None] * counter[None, :]) % LANES) / LANES
    cosine, sine = np.cos(angle), np.sin(angle)
    forward = np.block([[cosine, -sine], [sine, cosine]])
    inverse = np.block([[cosine, sine], [-sine, cosine]]) / LENGTH
    parts = []
    for matrix in (forward, inverse):
        high = matrix.astype(ml_dtypes.bfloat16)
        parts += [high, (matrix - high.astype(np.float64)).astype(ml_dtypes.bfloat16)]
    return np.stack(parts)


def near_table(residue):
    q = lax.broadcasted_iota(jnp.int32, (N_CTX, 8, LANES), 0)
    h = lax.broadcasted_iota(jnp.int32, (N_CTX, 8, LANES), 1) // 4
    lane = lax.broadcasted_iota(jnp.int32, (N_CTX, 8, LANES), 2)
    angle = (-2 * math.pi / LENGTH) * ((256 * q + 128 * h + lane) * residue).astype(F32)
    return jnp.stack([jnp.cos(angle), jnp.sin(angle)])


def call(kernel, out_shape, scratch, *operands):
    return pl.pallas_call(
        kernel,
        out_shape=jax.ShapeDtypeStruct(*out_shape),
        in_specs=[pl.BlockSpec(memory_space=pltpu.VMEM)] * len(operands),
        out_specs=pl.BlockSpec(memory_space=pltpu.VMEM),
        scratch_shapes=[pltpu.VMEM(shape, F32) for shape in scratch],
        compiler_params=pltpu.CompilerParams(vmem_limit_bytes=VMEM_LIMIT),
    )(*operands)


def exchange(x, axis):
    return lax.all_to_all(x, axis, split_axis=0, concat_axis=0, tiled=True)


def body(value_branch, key_branch, gate_branch, skip_gain, spectra):
    device = lax.axis_index("ctx")
    residue = sum(((device >> bit) & 1) << (4 - bit) for bit in range(5))
    near = near_table(residue)
    far = jnp.asarray(far_table())
    matrices = jnp.asarray(lane_matrices())
    response = spectra.reshape(2, 3, 4, LANES, 2, 32).transpose(0, 5, 1, 4, 2, 3).reshape(2, 768, LANES)

    packed = call(pack_kernel, ((N_CHAN, 48, LANES), BF16), [(N_CHAN, 48, LANES)], key_branch, value_branch)
    series = exchange(packed, "chan").reshape(N_CTX, 24, LANES)
    blocks = exchange(series, "ctx").reshape(N_CTX // 2, 48, LANES)
    rows = call(
        blocks_forward_kernel,
        ((N_CTX, 48, LANES), BF16),
        [(N_CTX // 2, 48, LANES), (N_CTX, 48, LANES)],
        blocks,
    )
    received = exchange(rows, "ctx")
    returned = call(
        filter_kernel,
        ((N_CTX, 48, LANES), BF16),
        [(N_CTX, 48, LANES), (768, 2 * LANES)],
        received,
        response,
        near,
        far,
        matrices,
    )
    parts = exchange(returned, "ctx")
    local = call(
        blocks_inverse_kernel,
        ((N_CTX // 2, 48, LANES), BF16),
        [(N_CTX, 48, LANES), (N_CTX // 2, 48, LANES)],
        parts,
    )
    convolved = exchange(local.reshape(N_CTX, 24, LANES), "ctx").reshape(N_CHAN, 48, LANES)
    tokens = exchange(convolved, "chan")
    return call(
        gate_kernel,
        ((CHANNELS, TOKENS), BF16),
        [(N_CHAN, 48, LANES), (CHANNELS, TOKENS)],
        tokens,
        key_branch,
        value_branch,
        gate_branch,
        skip_gain[:, None],
    )


def solution(mesh):
    in_specs = (
        P(None, ("ctx", "chan")),
        P(None, ("ctx", "chan")),
        P(None, ("ctx", "chan")),
        P(),
        P(None, "chan", "ctx", None),
    )
    out_specs = P(None, ("ctx", "chan"))
    return jax.shard_map(body, mesh=mesh, in_specs=in_specs, out_specs=out_specs, check_vma=False)
```

time: 262 us -> 118 us (0.45)
  local copies, waits for them, and re-layouts: 81.5 us -> 10.8 us
  other arithmetic: 59.8 us -> 0.59 us
  starting transfers between devices: 26.6 us -> 16.7 us
  waiting for transfers between devices: 32.5 us -> 25.3 us
  matrix products: 5.24 us -> 0 us
  blocking collectives: 54.6 us -> 59.6 us
  Pallas kernels: 0 us -> 3.94 us
    unnamed x1 -> x0, other arithmetic: 45.2 us -> none
    unnamed x26 -> x19, local copies, waits for them, and re-layouts: 44.1 us -> 2.5 us
    all_to_all x8 -> x0, local copies, waits for them, and re-layouts: 16.6 us -> none  [the longest x1 8.13 us: body(): lax.all_to_all(series.reshape(channel_count, 1, seq_length), 'ctx', split...]
    reshape x3 -> x1, local copies, waits for them, and re-layouts: 14.8 us -> 4.05 us  [body(): spectra.reshape(2, 3, 4, LANES, 2, 32).transpose(0, 5, 1, 4, 2, 3)]
    all_to_all x3, starting transfers between devices: 26.6 us -> 16.7 us  [exchange(): return lax.all_to_all(x, axis, split_axis=0, concat_axis=0, tiled=True)]
    all_to_all x3, waiting for transfers between devices: 32.5 us -> 25.3 us  [exchange(): return lax.all_to_all(x, axis, split_axis=0, concat_axis=0, tiled=True)]
    dot_general x6 -> x0, matrix products: 5.24 us -> none  [the longest x1 1.71 us: forward_local(): jnp.einsum('peoq,oxrq->pxer', block_table(second_factor, -1.0), section_t...]
    all_to_all x3, blocking collectives: 54.6 us -> 59.6 us  [exchange(): return lax.all_to_all(x, axis, split_axis=0, concat_axis=0, tiled=True)]
  transfers between devices with their start and end apart: 3 -> 3, of which waited for: 3 -> 3; matrix products, arithmetic and copies ran while one was open for 3% -> 8% of each run, Pallas kernels for 0% -> 0%
where the time goes in v1:
time: 118 us; the launch traced here: 117 us
  blocking collectives  59.6 us (51%)
  waiting for transfers between devices  25.3 us (21%)
  starting transfers between devices  16.7 us (14%)
  local copies, waits for them, and re-layouts  10.8 us (9%)
  Pallas kernels  3.94 us (3%)
    all_to_all x3, blocking collectives, exchange(): return lax.all_to_all(x, axis, split_axis=0, concat_axis=0, tiled=True)  59.6 us
    all_to_all x3, waiting for transfers between devices, exchange(): return lax.all_to_all(x, axis, split_axis=0, concat_axis=0, tiled=True)  25.3 us
    all_to_all x3, starting transfers between devices, exchange(): return lax.all_to_all(x, axis, split_axis=0, concat_axis=0, tiled=True)  16.7 us
    transpose x1, local copies, waits for them, and re-layouts, body(): spectra.reshape(2, 3, 4, LANES, 2, 32).transpose(0, 5, 1, 4, 2, 3)  4.12 us
    reshape x1, local copies, waits for them, and re-layouts, body(): spectra.reshape(2, 3, 4, LANES, 2, 32).transpose(0, 5, 1, 4, 2, 3)  4.05 us
    pallas_call x5, Pallas kernels, call(): pl.pallas_call(kernel, out_shape=jax.ShapeDtypeStruct(*out_shape), in_spe...  3.94 us
    unnamed x19, local copies, waits for them, and re-layouts  2.5 us
  transfers between devices with their start and end apart: 3, of which 3 were waited for; matrix products, arithmetic and copies ran while one was open for 8% of the time, Pallas kernels for 0%

profile of v1, /device:TPU:32, one launch (start us, length us, event | category | flops | bytes accessed | tf_op | source)
XLA Modules:
  0.0 117.1 jit_solution(12998128924152334897)
XLA Ops:
  0.0 0.0 copy-start
  0.0 0.9 copy-done
  0.9 0.0 copy-start.2
  0.9 0.9 copy-done.2
  1.9 0.0 copy-start.7
  1.9 0.1 shard_map.73
  1.9 31.1 %all_to_all.30 = bf16[16,48,128]{2,1,0:T(8,128)(2,1)} all-to-all(bf16[16,48,128]{2,1,0:T(8,128)(2,1)S(1)} %shard_map.73), channel_id=1, replica_groups=mesh['ctx'=32,'chan'=16] {'chan'}, dimensions={0} | all-to-all | bytes 393216 | tf_op jit(solution)/shard_map/all_to_all | solution.py:280
  33.0 7.3 %all-to-all-start.1 = ((bf16[32,24,128]{2,1,0:T(8,128)(2,1)}), bf16[32,24,128]{2,1,0:T(8,128)(2,1)S(1)}, u32[]{:S(2)}, u32[]{:S(2)}) async-start(bf16[32,24,128]{2,1,0:T(8,128)(2,1)} %bitcast), calls=%async_computation.1 | async-start | bytes 393216 | tf_op jit(solution)/shard_map/all_to_all | solution.py:280
  40.4 8.2 %all-to-all-done.1 = bf16[32,24,128]{2,1,0:T(8,128)(2,1)S(1)} async-done(((bf16[32,24,128]{2,1,0:T(8,128)(2,1)}), bf16[32,24,128]{2,1,0:T(8,128)(2,1)S(1)}, u32[]{:S(2)}, u32[]{:S(2)}) %all-to-all-start.1) | async-done | bytes 196640 | tf_op jit(solution)/shard_map/all_to_all | solution.py:280
  48.5 1.0 shard_map.74
  49.5 3.9 %all-to-all-start.2 = ((bf16[32,48,128]{2,1,0:T(8,128)(2,1)}), bf16[32,48,128]{2,1,0:T(8,128)(2,1)S(1)}, u32[]{:S(2)}, u32[]{:S(2)}) async-start(bf16[32,48,128]{2,1,0:T(8,128)(2,1)} %shard_map.74), calls=%async_computation.2 | async-start | bytes 786432 | tf_op jit(solution)/shard_map/all_to_all | solution.py:280
  53.4 0.0 copy-done.7
  53.4 0.6 copy.9
  54.0 4.0 %reshape.52 = f32[2,3,4,128,2,32]{5,4,3,0,2,1:T(2,128)} reshape(f32[2,12,1,8192]{3,0,1,2:T(2,128)S(1)} %copy.9) | data formatting | bytes 1572864 | tf_op jit(solution)/shard_map/reshape | solution.py:289
  58.1 0.0 copy-start.4
  58.1 0.0 copy-start.5
  58.1 4.1 %copy.10 = f32[2,32,3,2,4,128]{5,4,3,2,1,0:T(4,128)S(1)} copy(f32[2,32,3,2,4,128]{1,3,5,0,4,2:T(2,128)} %bitcast.12) | data formatting | bytes 1572864 | tf_op jit(solution)/shard_map/transpose | solution.py:289
  62.2 0.0 copy-start.8
  62.2 0.0 copy-start.1
  62.2 0.0 copy-start.3
  62.3 0.0 copy-start.6
  62.3 0.6 fusion.1
  62.9 0.8 all-to-all-done.2.in_ref
  63.7 0.0 copy-done.4
  63.7 0.0 copy-done.5
  63.7 1.8 %shard_map.75 = bf16[32,48,128]{2,1,0:T(8,128)(2,1)S(1)} custom-call(bf16[32,48,128]{2,1,0:T(8,128)(2,1)S(1)} %all-to-all-done.2.in_ref, f32[2,768,128]{2,1,0:T(8,128)S(1)} %bitcast.9, f32[2,32,8,128]{3,2,1,0:T(8,128)S(1)} %pad_maximum_fusion.near_ref, f32[2,32,8,128]{3,2,1,0:T(8,128)S(1)} %copy-done.5, bf16[4,256,256]{2,1,0:T(8,128)(2,1)S(1)} %copy-done.4), custom_call_target="tpu_custom_call" | custom-call | tf_op jit(solution)/shard_map/pallas_call | solution.py:269
  65.5 16.7 %all_to_all.31.in_ref = bf16[32,48,128]{2,1,0:T(8,128)(2,1)S(1)} all-to-all(bf16[32,48,128]{2,1,0:T(8,128)(2,1)S(1)} %shard_map.75), channel_id=1, replica_groups=mesh['ctx'=32,'chan'=16] {'ctx'}, dimensions={0} | all-to-all | bytes 786432 | tf_op jit(solution)/shard_map/all_to_all | solution.py:280
  82.2 0.2 shard_map.76
  82.4 11.9 %all_to_all.32 = bf16[32,24,128]{2,1,0:T(8,128)(2,1)} all-to-all(bf16[32,24,128]{2,1,0:T(8,128)(2,1)S(1)} %bitcast.11), channel_id=1, replica_groups=mesh['ctx'=32,'chan'=16] {'ctx'}, dimensions={0} | all-to-all | bytes 393216 | tf_op jit(solution)/shard_map/all_to_all | solution.py:280
  94.3 5.5 %all-to-all-start.5 = ((bf16[16,48,128]{2,1,0:T(8,128)(2,1)}), bf16[16,48,128]{2,1,0:T(8,128)(2,1)S(1)}, u32[]{:S(2)}, u32[]{:S(2)}) async-start(bf16[16,48,128]{2,1,0:T(8,128)(2,1)} %bitcast.5), calls=%async_computation.5 | async-start | bytes 393216 | tf_op jit(solution)/shard_map/all_to_all | solution.py:280
  99.8 0.0 copy-done.8
  99.8 0.1 copy.11.skip_ref
  100.0 16.3 %all-to-all-done.5.conv_ref = bf16[16,48,128]{2,1,0:T(8,128)(2,1)S(1)} async-done(((bf16[16,48,128]{2,1,0:T(8,128)(2,1)}), bf16[16,48,128]{2,1,0:T(8,128)(2,1)S(1)}, u32[]{:S(2)}, u32[]{:S(2)}) %all-to-all-start.5) | async-done | bytes 196640 | tf_op jit(solution)/shard_map/all_to_all | solution.py:280
  116.3 0.0 copy-done.1
  116.3 0.0 copy-done.3
  116.3 0.0 copy-done.6
  116.3 0.9 shard_map.77
  (4 shorter events, 0.0 us)
Async XLA Ops:
  0.0 0.9 copy-start
  0.9 0.9 copy-start.2
  1.9 51.6 %copy-start.7 = (f32[2,12,1,8192]{3,2,1,0:T(1,128)S(1)}, f32[2,12,1,8192]{3,2,1,0:T(1,128)}, u32[]{:S(2)}) copy-start(f32[2,12,1,8192]{3,2,1,0:T(1,128)} %param.11) | copy-start | bytes 2359300
  33.0 15.5 %all-to-all-start.1 = ((bf16[32,24,128]{2,1,0:T(8,128)(2,1)}), bf16[32,24,128]{2,1,0:T(8,128)(2,1)S(1)}, u32[]{:S(2)}, u32[]{:S(2)}) async-start(bf16[32,24,128]{2,1,0:T(8,128)(2,1)} %bitcast), calls=%async_computation.1 | async-start | bytes 393216 | tf_op jit(solution)/shard_map/all_to_all | solution.py:280
  49.5 14.2 %all-to-all-start.2 = ((bf16[32,48,128]{2,1,0:T(8,128)(2,1)}), bf16[32,48,128]{2,1,0:T(8,128)(2,1)S(1)}, u32[]{:S(2)}, u32[]{:S(2)}) async-start(bf16[32,48,128]{2,1,0:T(8,128)(2,1)} %shard_map.74), calls=%async_computation.2 | async-start | bytes 786432 | tf_op jit(solution)/shard_map/all_to_all | solution.py:280
  58.1 5.6 %copy-start.4 = (bf16[4,256,256]{2,1,0:T(8,128)(2,1)S(1)}, bf16[4,256,256]{2,1,0:T(8,128)(2,1)}, u32[]{:S(2)}) copy-start(bf16[4,256,256]{2,1,0:T(8,128)(2,1)} %constant.42.clone.matrix_ref) | copy-start | bytes 1572868
  58.1 5.6 %copy-start.5 = (f32[2,32,8,128]{3,2,1,0:T(8,128)S(1)}, f32[2,32,8,128]{3,2,1,0:T(8,128)}, u32[]{:S(2)}) copy-start(f32[2,32,8,128]{3,2,1,0:T(8,128)} %constant.41.clone.far_ref) | copy-start | bytes 786436
  62.2 37.6 %copy-start.8 = (f32[192]{0:T(256)S(1)}, f32[192]{0:T(256)}, u32[]{:S(2)}) copy-start(f32[192]{0:T(256)} %param.10) | copy-start | bytes 2308
  62.2 54.0 %copy-start.1 = (bf16[192,512]{1,0:T(8,128)(2,1)S(1)}, bf16[192,512]{1,0:T(8,128)(2,1)}, u32[]{:S(2)}) copy-start(bf16[192,512]{1,0:T(8,128)(2,1)} %key_ref.3) | copy-start | bytes 589828
  62.2 54.0 %copy-start.3 = (bf16[192,512]{1,0:T(8,128)(2,1)S(1)}, bf16[192,512]{1,0:T(8,128)(2,1)}, u32[]{:S(2)}) copy-start(bf16[192,512]{1,0:T(8,128)(2,1)} %value_ref.3) | copy-start | bytes 589828
  62.3 54.0 %copy-start.6 = (bf16[192,512]{1,0:T(8,128)(2,1)S(1)}, bf16[192,512]{1,0:T(8,128)(2,1)}, u32[]{:S(2)}) copy-start(bf16[192,512]{1,0:T(8,128)(2,1)} %gate_ref.1) | copy-start | bytes 589828
  94.3 22.0 %all-to-all-start.5 = ((bf16[16,48,128]{2,1,0:T(8,128)(2,1)}), bf16[16,48,128]{2,1,0:T(8,128)(2,1)S(1)}, u32[]{:S(2)}, u32[]{:S(2)}) async-start(bf16[16,48,128]{2,1,0:T(8,128)(2,1)} %bitcast.5), calls=%async_computation.5 | async-start | bytes 393216 | tf_op jit(solution)/shard_map/all_to_all | solution.py:280

commit v2 on v0

v2 whole, which is shorter than its diff:
```python
import math

import jax
import jax.numpy as jnp
import ml_dtypes
import numpy as np
from jax import lax
from jax.experimental import pallas as pl
from jax.experimental.pallas import tpu as pltpu
from jax.sharding import PartitionSpec as P

N_CTX = 32
N_CHAN = 16
CHANNELS = 192
GROUP = CHANNELS // N_CHAN
TOKENS = 512
SEQ = 8192
LENGTH = SEQ * N_CTX
LANES = 128
HALF = 16
ROWS = SEQ // LANES
F32 = jnp.float32
BF16 = jnp.bfloat16
VMEM_LIMIT = 32 * 1024 * 1024


def rev4(number):
    return int(f"{number:04b}"[::-1], 2)


def c_root(a, turn, sign):
    if turn == 0:
        return a
    if turn == 0.25:
        return (-a[1], a[0]) if sign > 0 else (a[1], -a[0])
    cosine = math.cos(2 * math.pi * turn)
    sine = sign * math.sin(2 * math.pi * turn)
    return (a[0] * cosine - a[1] * sine, a[0] * sine + a[1] * cosine)


def c_mul(a, re, im):
    return (a[0] * re - a[1] * im, a[0] * im + a[1] * re)


def fft_list(terms, sign):
    size = len(terms)
    if size == 1:
        return terms
    even = fft_list(terms[0::2], sign)
    odd = fft_list(terms[1::2], sign)
    odd = [c_root(term, index / size, sign) for index, term in enumerate(odd)]
    return [(e[0] + o[0], e[1] + o[1]) for e, o in zip(even, odd)] + [
        (e[0] - o[0], e[1] - o[1]) for e, o in zip(even, odd)
    ]


def product_kernel(key_ref, value_ref, out_ref, flat, wide):
    for block in range(CHANNELS // 16):
        rows = slice(16 * block, 16 * block + 16)
        product = key_ref[rows, :].astype(F32) * value_ref[rows, :].astype(F32)
        flat[rows, :] = product
    for target in range(N_CHAN):
        for quarter in range(4):
            wide[target, GROUP * quarter : GROUP * quarter + GROUP, :] = flat[
                GROUP * target : GROUP * target + GROUP, LANES * quarter : LANES * quarter + LANES
            ]
    for target in range(N_CHAN):
        out_ref[target] = wide[target].astype(BF16)


def fan_out_kernel(in_ref, out_ref, wide):
    for source in range(N_CHAN):
        wide[48 * source : 48 * source + 48, :] = in_ref[source].astype(F32)
    for channel in range(GROUP):
        series = wide[pl.ds(channel, ROWS, stride=GROUP), :].astype(BF16)
        out_ref[channel] = series
        out_ref[HALF + channel] = series
    for channel in range(GROUP, HALF):
        empty = jnp.zeros((ROWS, LANES), BF16)
        out_ref[channel] = empty
        out_ref[HALF + channel] = empty


def join_kernel(in_ref, out_ref, wide):
    for channel in range(GROUP):
        total = in_ref[channel].astype(F32) + in_ref[HALF + channel].astype(F32)
        wide[pl.ds(channel, ROWS, stride=GROUP), :] = total
    for target in range(N_CHAN):
        out_ref[target] = wide[48 * target : 48 * target + 48, :].astype(BF16)


def gate_kernel(conv_ref, key_ref, value_ref, gate_ref, skip_ref, out_ref, wide, flat):
    for source in range(N_CHAN):
        wide[source] = conv_ref[source].astype(F32)
    for source in range(N_CHAN):
        for quarter in range(4):
            flat[GROUP * source : GROUP * source + GROUP, LANES * quarter : LANES * quarter + LANES] = wide[
                source, GROUP * quarter : GROUP * quarter + GROUP, :
            ]
    for block in range(CHANNELS // 16):
        rows = slice(16 * block, 16 * block + 16)
        carried = (key_ref[rows, :].astype(F32) * value_ref[rows, :].astype(F32)).astype(BF16).astype(F32)
        total = flat[rows, :] + skip_ref[rows, :] * carried
        out_ref[rows, :] = (gate_ref[rows, :].astype(F32) * total).astype(BF16)


def spectra_kernel(place_ref, in_ref, out_ref):
    place = place_ref[0]
    for channel in range(GROUP):
        slot = place ^ channel
        parts = []
        for part in range(2):
            turned = in_ref[part, channel].T
            parts.append(jnp.concatenate([turned[:64, :], turned[64:, :]], axis=1))
        out_ref[slot] = jnp.concatenate(parts, axis=0).astype(BF16)
    for channel in range(GROUP, HALF):
        out_ref[place ^ channel] = jnp.zeros((2 * ROWS, LANES), BF16)


def split(x):
    high = x.astype(BF16)
    return high, (x - high.astype(F32)).astype(BF16)


def dot(a, b):
    return jnp.dot(a, b, preferred_element_type=F32)


def filter_kernel(
    place_ref, in_ref, spectra_ref, parity_ref, block_ref, lane_ref, row_matrix_ref, lane_matrix_ref, out_ref, real, pair
):
    place = place_ref[0]
    odd = place_ref[1]
    sign = jnp.where(odd == 0, 1.0, -1.0).astype(F32)

    def entry_phase(index, rows):
        cosine = jnp.where(odd == 0, 1.0, math.cos(math.pi * index / HALF)).astype(F32)
        sine = jnp.where(odd == 0, 0.0, -math.sin(math.pi * index / HALF)).astype(F32)
        re, im = parity_ref[0, rows, :], parity_ref[1, rows, :]
        re = jnp.where(odd == 0, 1.0, re)
        im = jnp.where(odd == 0, 0.0, im)
        return (re * cosine - im * sine, re * sine + im * cosine)

    for index in range(HALF):
        real[index] = in_ref[index].astype(F32) + sign * in_ref[HALF + index].astype(F32)
    for group in range(ROWS // 8):
        rows = slice(8 * group, 8 * group + 8)
        terms = []
        for index in range(HALF):
            phase = entry_phase(index, rows)
            term = real[index, rows, :]
            terms.append((term * phase[0], term * phase[1]))
        for kp, term in enumerate(fft_list(terms, -1)):
            if kp:
                term = c_mul(term, block_ref[0, kp, rows, :], block_ref[1, kp, rows, :])
            pair[kp, 8 * group : 8 * group + 8, :] = term[0]
            pair[kp, ROWS + 8 * group : ROWS + 8 * group + 8, :] = term[1]
    lane_re, lane_im = lane_ref[0], lane_ref[1]
    for kp in range(HALF):
        high, low = split(pair[kp])
        mixed = dot(row_matrix_ref[0], jnp.concatenate([high, low, high], axis=0))
        term = c_mul((mixed[:ROWS], mixed[ROWS:]), lane_re, lane_im)
        high, low = split(jnp.concatenate(term, axis=1))
        spectrum = dot(high, lane_matrix_ref[0]) + (dot(low, lane_matrix_ref[0]) + dot(high, lane_matrix_ref[1]))
        response = spectra_ref[place ^ rev4(kp)].astype(F32)
        term = c_mul((spectrum[:, :LANES], spectrum[:, LANES:]), response[:ROWS], response[ROWS:])
        high, low = split(jnp.concatenate(term, axis=1))
        mixed = dot(high, lane_matrix_ref[2]) + (dot(low, lane_matrix_ref[2]) + dot(high, lane_matrix_ref[3]))
        term = c_mul((mixed[:, :LANES], mixed[:, LANES:]), lane_re, -lane_im)
        high, low = split(jnp.concatenate(term, axis=0))
        pair[kp] = dot(row_matrix_ref[1], jnp.concatenate([high, low, high], axis=0))
    for group in range(ROWS // 8):
        rows = slice(8 * group, 8 * group + 8)
        terms = []
        for kp in range(HALF):
            term = (pair[kp, 8 * group : 8 * group + 8, :], pair[kp, ROWS + 8 * group : ROWS + 8 * group + 8, :])
            if kp:
                term = c_mul(term, block_ref[0, kp, rows, :], -block_ref[1, kp, rows, :])
            terms.append(term)
        for index, term in enumerate(fft_list(terms, 1)):
            phase = entry_phase(index, rows)
            real[index, rows, :] = term[0] * phase[0] + term[1] * phase[1]
    for index in range(HALF):
        total = real[index]
        out_ref[index] = total.astype(BF16)
        out_ref[HALF + index] = (sign * total).astype(BF16)


def phases(numerator, denominator):
    angle = -2 * np.pi * (numerator % denominator) / denominator
    return np.cos(angle), np.sin(angle)


def tables():
    row, lane = np.arange(ROWS), np.arange(LANES)
    offset = (LANES * row[:, None] + lane[None, :])[None]
    kp = np.arange(HALF)[:, None, None]
    parity = np.stack(phases(offset[0], LENGTH)).astype(np.float32)
    block = np.stack(phases(2 * kp * offset, LENGTH)).astype(np.float32)
    lane_phase = np.stack(phases(row[:, None] * lane[None, :], SEQ)).astype(np.float32)

    def parts(matrix):
        high = matrix.astype(ml_dtypes.bfloat16)
        return high, (matrix - high.astype(np.float64)).astype(ml_dtypes.bfloat16)

    cosine, sine = phases(row[:, None] * row[None, :], ROWS)
    row_matrices = []
    for flip in (1, -1):
        high, low = parts(np.block([[cosine, -flip * sine], [flip * sine, cosine]]))
        row_matrices.append(np.concatenate([high, high, low], axis=1))
    order = np.concatenate([np.arange(0, LANES, 2), np.arange(1, LANES, 2)])
    cosine, sine = phases(lane[:, None] * order[None, :], LANES)
    forward = np.block([[cosine, sine], [-sine, cosine]])
    inverse = np.block([[cosine.T, -sine.T], [sine.T, cosine.T]]) / LENGTH
    lane_matrices = [*parts(forward), *parts(inverse)]
    return parity, block, lane_phase, np.stack(row_matrices), np.stack(lane_matrices)


def call(kernel, out_shape, scratch, *operands, scalars=0):
    return pl.pallas_call(
        kernel,
        out_shape=jax.ShapeDtypeStruct(*out_shape),
        in_specs=[pl.BlockSpec(memory_space=pltpu.SMEM)] * scalars
        + [pl.BlockSpec(memory_space=pltpu.VMEM)] * (len(operands) - scalars),
        out_specs=pl.BlockSpec(memory_space=pltpu.VMEM),
        scratch_shapes=[pltpu.VMEM(shape, F32) for shape in scratch],
        compiler_params=pltpu.CompilerParams(vmem_limit_bytes=VMEM_LIMIT),
    )(*operands)


def apply_filter(place, series, response, **kwargs):
    return call(
        filter_kernel,
        ((N_CTX, ROWS, LANES), BF16),
        [(HALF, ROWS, LANES), (HALF, 2 * ROWS, LANES)],
        place,
        series,
        response,
        *(jnp.asarray(table) for table in tables()),
        scalars=1,
        **kwargs,
    )


def exchange(x, axis):
    return lax.all_to_all(x, axis, split_axis=0, concat_axis=0, tiled=True)


def spread_spectra(blocks):
    for bit in (3, 2, 1, 0):
        shape = blocks.shape
        view = blocks.reshape(HALF >> (bit + 1), 2, 1 << bit, *shape[1:])
        pairs = [(device, device ^ (1 << bit)) for device in range(N_CTX)]
        there = lax.ppermute(view[:, 1], "ctx", pairs)
        blocks = jnp.stack([view[:, 0], there], axis=1).reshape(shape)
    return blocks


def body(value_branch, key_branch, gate_branch, skip_gain, spectra):
    device = lax.axis_index("ctx")
    place = jnp.stack([device & 15, device >> 4])

    packed = call(
        product_kernel, ((N_CHAN, 48, LANES), BF16), [(CHANNELS, TOKENS), (N_CHAN, 48, LANES)], key_branch, value_branch
    )
    packed, spectra = lax.optimization_barrier((packed, spectra))
    response = call(
        spectra_kernel,
        ((HALF, 2 * ROWS, LANES), BF16),
        [],
        place,
        spectra.reshape(2, GROUP, ROWS, LANES),
        scalars=1,
    )
    response = spread_spectra(response)
    gathered = exchange(packed, "chan")
    sent = call(fan_out_kernel, ((N_CTX, ROWS, LANES), BF16), [(N_CHAN * 48, LANES)], gathered)
    series = exchange(sent, "ctx")
    parts = exchange(apply_filter(place, series, response), "ctx")
    joined = call(join_kernel, ((N_CHAN, 48, LANES), BF16), [(N_CHAN * 48, LANES)], parts)
    tokens = exchange(joined, "chan")
    return call(
        gate_kernel,
        ((CHANNELS, TOKENS), BF16),
        [(N_CHAN, 48, LANES), (CHANNELS, TOKENS)],
        tokens,
        key_branch,
        value_branch,
        gate_branch,
        skip_gain[:, None],
    )


def solution(mesh):
    in_specs = (
        P(None, ("ctx", "chan")),
        P(None, ("ctx", "chan")),
        P(None, ("ctx", "chan")),
        P(),
        P(None, "chan", "ctx", None),
    )
    out_specs = P(None, ("ctx", "chan"))
    return jax.shard_map(body, mesh=mesh, in_specs=in_specs, out_specs=out_specs, check_vma=False)
```

time: 262 us -> 118 us (0.45)
  local copies, waits for them, and re-layouts: 81.5 us -> 3.97 us
  other arithmetic: 59.8 us -> 0.28 us
  blocking collectives: 54.6 us -> 15.2 us
  Pallas kernels: 0 us -> 15 us
  starting transfers between devices: 26.6 us -> 38.7 us
  waiting for transfers between devices: 32.5 us -> 43.8 us
  matrix products: 5.24 us -> 0 us
    unnamed x1, other arithmetic: 45.2 us -> 0.05 us
    unnamed x26 -> x24, local copies, waits for them, and re-layouts: 44.1 us -> 3.69 us
    all_to_all x3 -> x1, blocking collectives: 54.6 us -> 15.2 us  [exchange(): return lax.all_to_all(x, axis, split_axis=0, concat_axis=0, tiled=True)]
    all_to_all x8 -> x0, local copies, waits for them, and re-layouts: 16.6 us -> none  [the longest x1 8.13 us: body(): lax.all_to_all(series.reshape(channel_count, 1, seq_length), 'ctx', split...]
    pallas_call x0 -> x6, Pallas kernels: none -> 15 us  [call(): pl.pallas_call(kernel, out_shape=jax.ShapeDtypeStruct(*out_shape), in_spe...]
    reshape x3 -> x0, local copies, waits for them, and re-layouts: 14.8 us -> none  [the longest x1 7.88 us: body(): returned.reshape(2, channel_count, 1, seq_length)]
    ppermute x0 -> x4, starting transfers between devices: none -> 13.2 us  [spread_spectra(): there = lax.ppermute(view[:, 1], 'ctx', pairs)]
    ppermute x0 -> x4, waiting for transfers between devices: none -> 7.69 us  [spread_spectra(): there = lax.ppermute(view[:, 1], 'ctx', pairs)]
  transfers between devices with their start and end apart: 3 -> 7, of which waited for: 3 -> 5; matrix products, arithmetic and copies ran while one was open for 3% -> 0% of each run, Pallas kernels for 0% -> 1%
where the time goes in v2:
time: 118 us; the launch traced here: 117 us
  waiting for transfers between devices  43.8 us (37%)
  starting transfers between devices  38.7 us (33%)
  blocking collectives  15.2 us (13%)
  Pallas kernels  15 us (13%)
  local copies, waits for them, and re-layouts  3.97 us (3%)
    all_to_all x3, waiting for transfers between devices, exchange(): return lax.all_to_all(x, axis, split_axis=0, concat_axis=0, tiled=True)  36.1 us
    all_to_all x3, starting transfers between devices, exchange(): return lax.all_to_all(x, axis, split_axis=0, concat_axis=0, tiled=True)  25.5 us
    all_to_all x1, blocking collectives, exchange(): return lax.all_to_all(x, axis, split_axis=0, concat_axis=0, tiled=True)  15.2 us
    pallas_call x6, Pallas kernels, call(): pl.pallas_call(kernel, out_shape=jax.ShapeDtypeStruct(*out_shape), in_spe...  15 us
    ppermute x4, starting transfers between devices, spread_spectra(): there = lax.ppermute(view[:, 1], 'ctx', pairs)  13.2 us
    ppermute x4, waiting for transfers between devices, spread_spectra(): there = lax.ppermute(view[:, 1], 'ctx', pairs)  7.69 us
    unnamed x24, local copies, waits for them, and re-layouts  3.69 us
  transfers between devices with their start and end apart: 7, of which 5 were waited for; matrix products, arithmetic and copies ran while one was open for 0% of the time, Pallas kernels for 1%

profile of v2, /device:TPU:32, one launch (start us, length us, event | category | flops | bytes accessed | tf_op | source)
XLA Modules:
  0.0 117.2 jit_solution(18020492316138143551)
XLA Ops:
  0.0 0.9 copy-done.2
  0.9 0.0 copy-start.4
  0.9 0.9 copy-done.4
  1.9 0.8 shard_map.100
  2.6 0.1 pad_add_fusion.place_ref
  2.7 0.0 copy-start.1
  2.7 1.1 copy-done.1
  3.8 1.0 shard_map.102
  4.8 3.5 %collective-permute-start = (bf16[1,8,128,128]{3,2,1,0:T(8,128)(2,1)S(1)}, bf16[1,8,128,128]{3,2,1,0:T(8,128)(2,1)S(1)}, u32[]{:S(2)}, u32[]{:S(2)}) collective-permute-start(bf16[1,8,128,128]{3,2,1,0:T(8,128)(2,1)S(1)} %get-tuple-element.16), channel_id=1, source_target_pairs={{0,128},{16,144},{32,160},{48,176},{64,192},{80,208},{96,224},{112... | collective-permute-start | bytes 786440 | tf_op jit(solution)/shard_map/ppermute | solution.py:254
  8.3 6.4 %collective-permute-done = bf16[1,8,128,128]{3,2,1,0:T(8,128)(2,1)S(1)} collective-permute-done((bf16[1,8,128,128]{3,2,1,0:T(8,128)(2,1)S(1)}, bf16[1,8,128,128]{3,2,1,0:T(8,128)(2,1)S(1)}, u32[]{:S(2)}, u32[]{:S(2)}) %collective-permute-start) | collective-permute-done | bytes 262176 | tf_op jit(solution)/shard_map/ppermute | solution.py:254
  14.8 4.9 %collective-permute-start.1 = (bf16[2,4,128,128]{3,2,1,0:T(8,128)(2,1)S(1)}, bf16[2,4,128,128]{3,2,1,0:T(8,128)(2,1)S(1)}, u32[]{:S(2)}, u32[]{:S(2)}) collective-permute-start(bf16[2,4,128,128]{3,2,1,0:T(8,128)(2,1)S(1)} %get-tuple-element.14), channel_id=1, source_target_pairs={{0,64},{16,80},{32,96},{48,112},{64,0},{80,16},{96,32},{112,48},{1... | collective-permute-start | bytes 786440 | tf_op jit(solution)/shard_map/ppermute | solution.py:254
  19.8 15.2 %all-to-all-start = ((bf16[16,48,128]{2,1,0:T(8,128)(2,1)}), bf16[16,48,128]{2,1,0:T(8,128)(2,1)S(1)}, u32[]{:S(2)}, u32[]{:S(2)}) async-start(bf16[16,48,128]{2,1,0:T(8,128)(2,1)} %shard_map.100), calls=%async_computation | async-start | bytes 393216 | tf_op jit(solution)/shard_map/all_to_all | solution.py:246
  35.0 0.0 collective-permute-done.1
  35.0 0.1 pad_maximum_fusion
  35.1 2.5 %collective-permute-start.2 = (bf16[4,2,128,128]{3,2,0,1:T(8,128)(2,1)S(1)}, bf16[4,2,128,128]{3,2,0,1:T(8,128)(2,1)S(1)}, u32[]{:S(2)}, u32[]{:S(2)}) collective-permute-start(bf16[4,2,128,128]{3,2,0,1:T(8,128)(2,1)S(1)} %get-tuple-element.12), channel_id=1, source_target_pairs={{0,32},{16,48},{32,0},{48,16},{64,96},{80,112},{96,64},{112,80},{1... | collective-permute-start | bytes 786440 | tf_op jit(solution)/shard_map/ppermute | solution.py:254
  37.7 12.8 %all-to-all-done.in_ref = bf16[16,48,128]{2,1,0:T(8,128)(2,1)S(1)} async-done(((bf16[16,48,128]{2,1,0:T(8,128)(2,1)}), bf16[16,48,128]{2,1,0:T(8,128)(2,1)S(1)}, u32[]{:S(2)}, u32[]{:S(2)}) %all-to-all-start) | async-done | bytes 196640 | tf_op jit(solution)/shard_map/all_to_all | solution.py:246
  50.5 0.9 shard_map.101
  51.3 5.4 %all-to-all-start.1 = ((bf16[32,64,128]{2,1,0:T(8,128)(2,1)}), bf16[32,64,128]{2,1,0:T(8,128)(2,1)S(1)}, u32[]{:S(2)}, u32[]{:S(2)}) async-start(bf16[32,64,128]{2,1,0:T(8,128)(2,1)} %shard_map.101), calls=%async_computation.1 | async-start | bytes 1048576 | tf_op jit(solution)/shard_map/all_to_all | solution.py:246
  56.8 0.0 collective-permute-done.2
  56.8 0.1 pad_maximum_fusion.1
  56.9 0.0 copy-start
  56.9 2.3 %collective-permute-start.3 = (bf16[8,1,128,128]{3,2,0,1:T(8,128)(2,1)S(1)}, bf16[8,1,128,128]{3,2,0,1:T(8,128)(2,1)S(1)}, u32[]{:S(2)}, u32[]{:S(2)}) collective-permute-start(bf16[8,1,128,128]{3,2,0,1:T(8,128)(2,1)S(1)} %get-tuple-element.10), channel_id=1, source_target_pairs={{0,16},{16,0},{32,48},{48,32},{64,80},{80,64},{96,112},{112,96},{1... | collective-permute-start | bytes 786440 | tf_op jit(solution)/shard_map/ppermute | solution.py:254
  59.2 1.2 %collective-permute-done.3 = bf16[8,1,128,128]{3,2,0,1:T(8,128)(2,1)S(1)} collective-permute-done((bf16[8,1,128,128]{3,2,0,1:T(8,128)(2,1)S(1)}, bf16[8,1,128,128]{3,2,0,1:T(8,128)(2,1)S(1)}, u32[]{:S(2)}, u32[]{:S(2)}) %collective-permute-start.3) | collective-permute-done | bytes 262176 | tf_op jit(solution)/shard_map/ppermute | solution.py:254
  60.5 0.0 copy-start.6
  60.5 0.0 copy-start.9
  60.5 0.0 copy-start.10
  60.5 0.1 pad_maximum_fusion.2
  60.6 8.0 %all-to-all-done.1.in_ref = bf16[32,64,128]{2,1,0:T(8,128)(2,1)S(1)} async-done(((bf16[32,64,128]{2,1,0:T(8,128)(2,1)}), bf16[32,64,128]{2,1,0:T(8,128)(2,1)S(1)}, u32[]{:S(2)}, u32[]{:S(2)}) %all-to-all-start.1) | async-done | bytes 524320 | tf_op jit(solution)/shard_map/all_to_all | solution.py:246
  68.6 0.0 copy-done
  68.6 0.0 copy-done.6
  68.6 0.0 copy-done.7
  68.6 0.0 copy-done.9
  68.6 0.0 copy-done.10
  68.6 10.8 %shard_map.103 = bf16[32,64,128]{2,1,0:T(8,128)(2,1)S(1)} custom-call(s32[2]{0:T(128)S(1)} %pad_add_fusion.place_ref, bf16[32,64,128]{2,1,0:T(8,128)(2,1)S(1)} %all-to-all-done.1.in_ref, bf16[16,128,128]{2,1,0:T(8,128)(2,1)S(1)} %bitcast.28, f32[2,64,128]{2,1,0:T(8,128)S(1)} %copy-done.9, f32[2,16,64,128]{3,2,1,0:T(8,128)S(1)} %copy-done, ...), custom_call_target="tpu_custom_call" | custom-call | tf_op jit(solution)/shard_map/pallas_call | solution.py:220
  79.4 15.2 %all_to_all.20.in_ref = bf16[32,64,128]{2,1,0:T(8,128)(2,1)S(1)} all-to-all(bf16[32,64,128]{2,1,0:T(8,128)(2,1)S(1)} %shard_map.103), channel_id=1, replica_groups=mesh['ctx'=32,'chan'=16] {'ctx'}, dimensions={0} | all-to-all | bytes 1048576 | tf_op jit(solution)/shard_map/all_to_all | solution.py:246
  94.6 0.0 copy-start.8
  94.6 0.7 shard_map.104
  95.3 0.0 copy-start.3
  95.3 0.0 copy-start.5
  95.3 4.8 %all-to-all-start.3 = ((bf16[16,48,128]{2,1,0:T(8,128)(2,1)}), bf16[16,48,128]{2,1,0:T(8,128)(2,1)S(1)}, u32[]{:S(2)}, u32[]{:S(2)}) async-start(bf16[16,48,128]{2,1,0:T(8,128)(2,1)} %shard_map.104), calls=%async_computation.3 | async-start | bytes 393216 | tf_op jit(solution)/shard_map/all_to_all | solution.py:246
  100.2 0.0 copy-start.11
  100.2 0.7 copy-done.11
  100.9 0.1 copy.19.skip_ref
  101.0 15.3 %all-to-all-done.3.conv_ref = bf16[16,48,128]{2,1,0:T(8,128)(2,1)S(1)} async-done(((bf16[16,48,128]{2,1,0:T(8,128)(2,1)}), bf16[16,48,128]{2,1,0:T(8,128)(2,1)S(1)}, u32[]{:S(2)}, u32[]{:S(2)}) %all-to-all-start.3) | async-done | bytes 196640 | tf_op jit(solution)/shard_map/all_to_all | solution.py:246
  116.3 0.0 copy-done.8
  116.3 0.0 copy-done.3
  116.3 0.0 copy-done.5
  116.3 0.9 shard_map.105
  (7 shorter events, 0.2 us)
Async XLA Ops:
  0.0 0.9 copy-start.2
  0.9 0.9 copy-start.4
  2.7 1.1 copy-start.1
  4.8 9.9 %collective-permute-start = (bf16[1,8,128,128]{3,2,1,0:T(8,128)(2,1)S(1)}, bf16[1,8,128,128]{3,2,1,0:T(8,128)(2,1)S(1)}, u32[]{:S(2)}, u32[]{:S(2)}) collective-permute-start(bf16[1,8,128,128]{3,2,1,0:T(8,128)(2,1)S(1)} %get-tuple-element.16), channel_id=1, source_target_pairs={{0,128},{16,144},{32,160},{48,176},{64,192},{80,208},{96,224},{112... | collective-permute-start | bytes 786440 | tf_op jit(solution)/shard_map/ppermute | solution.py:254
  14.8 20.2 %collective-permute-start.1 = (bf16[2,4,128,128]{3,2,1,0:T(8,128)(2,1)S(1)}, bf16[2,4,128,128]{3,2,1,0:T(8,128)(2,1)S(1)}, u32[]{:S(2)}, u32[]{:S(2)}) collective-permute-start(bf16[2,4,128,128]{3,2,1,0:T(8,128)(2,1)S(1)} %get-tuple-element.14), channel_id=1, source_target_pairs={{0,64},{16,80},{32,96},{48,112},{64,0},{80,16},{96,32},{112,48},{1... | collective-permute-start | bytes 786440 | tf_op jit(solution)/shard_map/ppermute | solution.py:254
  19.8 30.7 %all-to-all-start = ((bf16[16,48,128]{2,1,0:T(8,128)(2,1)}), bf16[16,48,128]{2,1,0:T(8,128)(2,1)S(1)}, u32[]{:S(2)}, u32[]{:S(2)}) async-start(bf16[16,48,128]{2,1,0:T(8,128)(2,1)} %shard_map.100), calls=%async_computation | async-start | bytes 393216 | tf_op jit(solution)/shard_map/all_to_all | solution.py:246
  35.1 21.7 %collective-permute-start.2 = (bf16[4,2,128,128]{3,2,0,1:T(8,128)(2,1)S(1)}, bf16[4,2,128,128]{3,2,0,1:T(8,128)(2,1)S(1)}, u32[]{:S(2)}, u32[]{:S(2)}) collective-permute-start(bf16[4,2,128,128]{3,2,0,1:T(8,128)(2,1)S(1)} %get-tuple-element.12), channel_id=1, source_target_pairs={{0,32},{16,48},{32,0},{48,16},{64,96},{80,112},{96,64},{112,80},{1... | collective-permute-start | bytes 786440 | tf_op jit(solution)/shard_map/ppermute | solution.py:254
  51.3 17.2 %all-to-all-start.1 = ((bf16[32,64,128]{2,1,0:T(8,128)(2,1)}), bf16[32,64,128]{2,1,0:T(8,128)(2,1)S(1)}, u32[]{:S(2)}, u32[]{:S(2)}) async-start(bf16[32,64,128]{2,1,0:T(8,128)(2,1)} %shard_map.101), calls=%async_computation.1 | async-start | bytes 1048576 | tf_op jit(solution)/shard_map/all_to_all | solution.py:246
  56.9 11.7 %copy-start = (f32[2,16,64,128]{3,2,1,0:T(8,128)S(1)}, f32[2,16,64,128]{3,2,1,0:T(8,128)}, u32[]{:S(2)}) copy-start(f32[2,16,64,128]{3,2,1,0:T(8,128)} %constant.21.clone.block_ref) | copy-start | bytes 3145732
  56.9 3.6 %collective-permute-start.3 = (bf16[8,1,128,128]{3,2,0,1:T(8,128)(2,1)S(1)}, bf16[8,1,128,128]{3,2,0,1:T(8,128)(2,1)S(1)}, u32[]{:S(2)}, u32[]{:S(2)}) collective-permute-start(bf16[8,1,128,128]{3,2,0,1:T(8,128)(2,1)S(1)} %get-tuple-element.10), channel_id=1, source_target_pairs={{0,16},{16,0},{32,48},{48,32},{64,80},{80,64},{96,112},{112,96},{1... | collective-permute-start | bytes 786440 | tf_op jit(solution)/shard_map/ppermute | solution.py:254
  60.5 8.1 %copy-start.6 = (bf16[4,256,256]{2,1,0:T(8,128)(2,1)S(1)}, bf16[4,256,256]{2,1,0:T(8,128)(2,1)}, u32[]{:S(2)}) copy-start(bf16[4,256,256]{2,1,0:T(8,128)(2,1)} %constant.24.clone.lane_matrix_ref) | copy-start | bytes 1572868
  60.5 8.1 %copy-start.7 = (bf16[2,128,384]{2,1,0:T(8,128)(2,1)S(1)}, bf16[2,128,384]{2,1,0:T(8,128)(2,1)}, u32[]{:S(2)}) copy-start(bf16[2,128,384]{2,1,0:T(8,128)(2,1)} %constant.23.clone.row_matrix_ref) | copy-start | bytes 589828
  60.5 8.1 %copy-start.9 = (f32[2,64,128]{2,1,0:T(8,128)S(1)}, f32[2,64,128]{2,1,0:T(8,128)}, u32[]{:S(2)}) copy-start(f32[2,64,128]{2,1,0:T(8,128)} %constant.20.clone.parity_ref) | copy-start | bytes 196612
  60.5 8.1 %copy-start.10 = (f32[2,64,128]{2,1,0:T(8,128)S(1)}, f32[2,64,128]{2,1,0:T(8,128)}, u32[]{:S(2)}) copy-start(f32[2,64,128]{2,1,0:T(8,128)} %constant.22.clone.lane_ref) | copy-start | bytes 196612
  94.6 21.7 %copy-start.8 = (bf16[192,512]{1,0:T(8,128)(2,1)S(1)}, bf16[192,512]{1,0:T(8,128)(2,1)}, u32[]{:S(2)}) copy-start(bf16[192,512]{1,0:T(8,128)(2,1)} %gate_ref.1) | copy-start | bytes 589828
  95.3 21.0 %copy-start.3 = (bf16[192,512]{1,0:T(8,128)(2,1)S(1)}, bf16[192,512]{1,0:T(8,128)(2,1)}, u32[]{:S(2)}) copy-start(bf16[192,512]{1,0:T(8,128)(2,1)} %key_ref.3) | copy-start | bytes 589828
  95.3 21.0 %copy-start.5 = (bf16[192,512]{1,0:T(8,128)(2,1)S(1)}, bf16[192,512]{1,0:T(8,128)(2,1)}, u32[]{:S(2)}) copy-start(bf16[192,512]{1,0:T(8,128)(2,1)} %value_ref.3) | copy-start | bytes 589828
  95.3 21.0 %all-to-all-start.3 = ((bf16[16,48,128]{2,1,0:T(8,128)(2,1)}), bf16[16,48,128]{2,1,0:T(8,128)(2,1)S(1)}, u32[]{:S(2)}, u32[]{:S(2)}) async-start(bf16[16,48,128]{2,1,0:T(8,128)(2,1)} %shard_map.104), calls=%async_computation.3 | async-start | bytes 393216 | tf_op jit(solution)/shard_map/all_to_all | solution.py:246
  100.2 0.7 copy-start.11

commit v3 on v2

--- a/solution.py
+++ b/solution.py
@@ -18,6 +18,7 @@
 LENGTH = SEQ * N_CTX
 LANES = 128
 HALF = 16
+CLASSES = 4
 ROWS = SEQ // LANES
 F32 = jnp.float32
 BF16 = jnp.bfloat16
@@ -107,14 +108,17 @@
 def spectra_kernel(place_ref, in_ref, out_ref):
     place = place_ref[0]
     for channel in range(GROUP):
-        slot = place ^ channel
+        distance = place ^ channel
+        slot = (((distance >> 1) & 3) << 2) | ((distance >> 3) << 1) | (distance & 1)
         parts = []
         for part in range(2):
             turned = in_ref[part, channel].T
             parts.append(jnp.concatenate([turned[:64, :], turned[64:, :]], axis=1))
         out_ref[slot] = jnp.concatenate(parts, axis=0).astype(BF16)
     for channel in range(GROUP, HALF):
-        out_ref[place ^ channel] = jnp.zeros((2 * ROWS, LANES), BF16)
+        distance = place ^ channel
+        slot = (((distance >> 1) & 3) << 2) | ((distance >> 3) << 1) | (distance & 1)
+        out_ref[slot] = jnp.zeros((2 * ROWS, LANES), BF16)
 
 
 def split(x):
@@ -153,27 +157,42 @@
         for kp, term in enumerate(fft_list(terms, -1)):
             if kp:
                 term = c_mul(term, block_ref[0, kp, rows, :], block_ref[1, kp, rows, :])
-            pair[kp, 8 * group : 8 * group + 8, :] = term[0]
-            pair[kp, ROWS + 8 * group : ROWS + 8 * group + 8, :] = term[1]
+            columns = slice(LANES * kp, LANES * kp + LANES)
+            pair[8 * group : 8 * group + 8, columns] = term[0]
+            pair[ROWS + 8 * group : ROWS + 8 * group + 8, columns] = term[1]
     lane_re, lane_im = lane_ref[0], lane_ref[1]
-    for kp in range(HALF):
-        high, low = split(pair[kp])
+    for first in range(0, HALF, CLASSES):
+        columns = slice(LANES * first, LANES * (first + CLASSES))
+        high, low = split(pair[:, columns])
         mixed = dot(row_matrix_ref[0], jnp.concatenate([high, low, high], axis=0))
-        term = c_mul((mixed[:ROWS], mixed[ROWS:]), lane_re, lane_im)
-        high, low = split(jnp.concatenate(term, axis=1))
-        spectrum = dot(high, lane_matrix_ref[0]) + (dot(low, lane_matrix_ref[0]) + dot(high, lane_matrix_ref[1]))
-        response = spectra_ref[place ^ rev4(kp)].astype(F32)
-        term = c_mul((spectrum[:, :LANES], spectrum[:, LANES:]), response[:ROWS], response[ROWS:])
-        high, low = split(jnp.concatenate(term, axis=1))
-        mixed = dot(high, lane_matrix_ref[2]) + (dot(low, lane_matrix_ref[2]) + dot(high, lane_matrix_ref[3]))
-        term = c_mul((mixed[:, :LANES], mixed[:, LANES:]), lane_re, -lane_im)
-        high, low = split(jnp.concatenate(term, axis=0))
-        pair[kp] = dot(row_matrix_ref[1], jnp.concatenate([high, low, high], axis=0))
+        turned = []
+        for index in range(CLASSES):
+            lanes = slice(LANES * index, LANES * index + LANES)
+            term = c_mul((mixed[:ROWS, lanes], mixed[ROWS:, lanes]), lane_re, lane_im)
+            turned.append(jnp.concatenate(term, axis=1))
+        high, low = split(jnp.concatenate(turned, axis=0))
+        spectrum = dot(jnp.concatenate([high, low, high], axis=1), lane_matrix_ref[0])
+        shaped = []
+        for index in range(CLASSES):
+            rows = slice(ROWS * index, ROWS * index + ROWS)
+            response = spectra_ref[slot_of(place ^ rev4(first + index))].astype(F32)
+            term = c_mul((spectrum[rows, :LANES], spectrum[rows, LANES:]), response[:ROWS], response[ROWS:])
+            shaped.append(jnp.concatenate(term, axis=1))
+        high, low = split(jnp.concatenate(shaped, axis=0))
+        mixed = dot(jnp.concatenate([high, low, high], axis=1), lane_matrix_ref[1])
+        turned = []
+        for index in range(CLASSES):
+            rows = slice(ROWS * index, ROWS * index + ROWS)
+            term = c_mul((mixed[rows, :LANES], mixed[rows, LANES:]), lane_re, -lane_im)
+            turned.append(jnp.concatenate(term, axis=0))
+        high, low = split(jnp.concatenate(turned, axis=1))
+        pair[:, columns] = dot(row_matrix_ref[1], jnp.concatenate([high, low, high], axis=0))
     for group in range(ROWS // 8):
         rows = slice(8 * group, 8 * group + 8)
         terms = []
         for kp in range(HALF):
-            term = (pair[kp, 8 * group : 8 * group + 8, :], pair[kp, ROWS + 8 * group : ROWS + 8 * group + 8, :])
+            columns = slice(LANES * kp, LANES * kp + LANES)
+            term = (pair[8 * group : 8 * group + 8, columns], pair[ROWS + 8 * group : ROWS + 8 * group + 8, columns])
             if kp:
                 term = c_mul(term, block_ref[0, kp, rows, :], -block_ref[1, kp, rows, :])
             terms.append(term)
@@ -212,7 +231,10 @@
     cosine, sine = phases(lane[:, None] * order[None, :], LANES)
     forward = np.block([[cosine, sine], [-sine, cosine]])
     inverse = np.block([[cosine.T, -sine.T], [sine.T, cosine.T]]) / LENGTH
-    lane_matrices = [*parts(forward), *parts(inverse)]
+    lane_matrices = []
+    for matrix in (forward, inverse):
+        high, low = parts(matrix)
+        lane_matrices.append(np.concatenate([high, high, low], axis=0))
     return parity, block, lane_phase, np.stack(row_matrices), np.stack(lane_matrices)
 
 
@@ -232,7 +254,7 @@
     return call(
         filter_kernel,
         ((N_CTX, ROWS, LANES), BF16),
-        [(HALF, ROWS, LANES), (HALF, 2 * ROWS, LANES)],
+        [(HALF, ROWS, LANES), (2 * ROWS, HALF * LANES)],
         place,
         series,
         response,
@@ -246,14 +268,21 @@
     return lax.all_to_all(x, axis, split_axis=0, concat_axis=0, tiled=True)
 
 
+def slot_of(distance):
+    return ((distance >> 3) << 3) | ((distance & 1) << 2) | ((distance >> 1) & 3)
+
+
+def swap(pieces, distances):
+    there = [pieces[0]]
+    for piece, distance in zip(pieces[1:], distances[1:]):
+        there.append(lax.ppermute(piece, "ctx", [(device, device ^ distance) for device in range(N_CTX)]))
+    return there
+
+
 def spread_spectra(blocks):
-    for bit in (3, 2, 1, 0):
-        shape = blocks.shape
-        view = blocks.reshape(HALF >> (bit + 1), 2, 1 << bit, *shape[1:])
-        pairs = [(device, device ^ (1 << bit)) for device in range(N_CTX)]
-        there = lax.ppermute(view[:, 1], "ctx", pairs)
-        blocks = jnp.stack([view[:, 0], there], axis=1).reshape(shape)
-    return blocks
+    pieces = swap([blocks[4 * x : 4 * x + 4] for x in range(4)], (0, 2, 4, 6))
+    pieces = swap([jnp.stack([piece[other] for piece in pieces]) for other in range(4)], (0, 1, 8, 9))
+    return jnp.concatenate(pieces, axis=0)
 
 
 def body(value_branch, key_branch, gate_branch, skip_gain, spectra):

time: 118 us -> 115 us (0.975)
  starting transfers between devices: 38.7 us -> 45.4 us
  waiting for transfers between devices: 43.8 us -> 37.6 us
  Pallas kernels: 15 us -> 9.02 us
  blocking collectives: 15.2 us -> 17.6 us
    all_to_all x3, waiting for transfers between devices: 36.1 us -> 29 us  [exchange(): return lax.all_to_all(x, axis, split_axis=0, concat_axis=0, tiled=True)]
    pallas_call x6, Pallas kernels: 15 us -> 9.02 us  [call(): pl.pallas_call(kernel, out_shape=jax.ShapeDtypeStruct(*out_shape), in_spe...]
    ppermute x4 -> x6, starting transfers between devices: 13.2 us -> 18.1 us  [swap(): lax.ppermute(piece, 'ctx', [(device, device ^ distance) for device in ran...]
    all_to_all x1, blocking collectives: 15.2 us -> 17.6 us  [exchange(): return lax.all_to_all(x, axis, split_axis=0, concat_axis=0, tiled=True)]
    all_to_all x3, starting transfers between devices: 25.5 us -> 27.3 us  [exchange(): return lax.all_to_all(x, axis, split_axis=0, concat_axis=0, tiled=True)]
    ppermute x4 -> x6, waiting for transfers between devices: 7.69 us -> 8.61 us  [swap(): lax.ppermute(piece, 'ctx', [(device, device ^ distance) for device in ran...]
    unnamed x24 -> x26, local copies, waits for them, and re-layouts: 3.69 us -> 3.74 us
  transfers between devices with their start and end apart: 7 -> 9, of which waited for: 5 -> 4; matrix products, arithmetic and copies ran while one was open for 0% -> 0% of each run, Pallas kernels for 1% -> 1%
where the time goes in v3:
time: 115 us; the launch traced here: 114 us
  starting transfers between devices  45.4 us (39%)
  waiting for transfers between devices  37.6 us (33%)
  blocking collectives  17.6 us (15%)
  Pallas kernels  9.02 us (8%)
  local copies, waits for them, and re-layouts  3.96 us (3%)
    all_to_all x3, waiting for transfers between devices, exchange(): return lax.all_to_all(x, axis, split_axis=0, concat_axis=0, tiled=True)  29 us
    all_to_all x3, starting transfers between devices, exchange(): return lax.all_to_all(x, axis, split_axis=0, concat_axis=0, tiled=True)  27.3 us
    ppermute x6, starting transfers between devices, swap(): lax.ppermute(piece, 'ctx', [(device, device ^ distance) for device in ran...  18.1 us
    all_to_all x1, blocking collectives, exchange(): return lax.all_to_all(x, axis, split_axis=0, concat_axis=0, tiled=True)  17.6 us
    pallas_call x6, Pallas kernels, call(): pl.pallas_call(kernel, out_shape=jax.ShapeDtypeStruct(*out_shape), in_spe...  9.02 us
    ppermute x6, waiting for transfers between devices, swap(): lax.ppermute(piece, 'ctx', [(device, device ^ distance) for device in ran...  8.61 us
    unnamed x26, local copies, waits for them, and re-layouts  3.74 us
  transfers between devices with their start and end apart: 9, of which 4 were waited for; matrix products, arithmetic and copies ran while one was open for 0% of the time, Pallas kernels for 1%

profile of v3, /device:TPU:32, one launch (start us, length us, event | category | flops | bytes accessed | tf_op | source)
XLA Modules:
  0.0 114.0 jit_solution(16288947486530468716)
XLA Ops:
  0.0 0.9 copy-done.2
  0.9 0.0 copy-start.4
  0.9 0.9 copy-done.4
  1.9 0.8 shard_map.100
  2.6 0.1 pad_add_fusion.place_ref
  2.7 0.0 copy-start.1
  2.7 1.1 copy-done.1
  3.8 1.0 shard_map.102
  4.8 3.4 %collective-permute-start = (bf16[4,128,128]{2,1,0:T(8,128)(2,1)S(1)}, bf16[4,128,128]{2,1,0:T(8,128)(2,1)S(1)}, u32[]{:S(2)}, u32[]{:S(2)}) collective-permute-start(bf16[4,128,128]{2,1,0:T(8,128)(2,1)S(1)} %get-tuple-element.15), channel_id=1, source_target_pairs={{0,32},{16,48},{32,0},{48,16},{64,96},{80,112},{96,64},{112,80},{1... | collective-permute-start | bytes 393224 | tf_op jit(solution)/shard_map/ppermute | solution.py:278
  8.2 4.6 %collective-permute-start.1 = (bf16[4,128,128]{2,1,0:T(8,128)(2,1)S(1)}, bf16[4,128,128]{2,1,0:T(8,128)(2,1)S(1)}, u32[]{:S(2)}, u32[]{:S(2)}) collective-permute-start(bf16[4,128,128]{2,1,0:T(8,128)(2,1)S(1)} %get-tuple-element.14), channel_id=1, source_target_pairs={{0,64},{16,80},{32,96},{48,112},{64,0},{80,16},{96,32},{112,48},{1... | collective-permute-start | bytes 393224 | tf_op jit(solution)/shard_map/ppermute | solution.py:278
  12.9 2.4 %collective-permute-start.2 = (bf16[4,128,128]{2,1,0:T(8,128)(2,1)S(1)}, bf16[4,128,128]{2,1,0:T(8,128)(2,1)S(1)}, u32[]{:S(2)}, u32[]{:S(2)}) collective-permute-start(bf16[4,128,128]{2,1,0:T(8,128)(2,1)S(1)} %get-tuple-element.13), channel_id=1, source_target_pairs={{0,96},{16,112},{32,64},{48,80},{64,32},{80,48},{96,0},{112,16},{1... | collective-permute-start | bytes 393224 | tf_op jit(solution)/shard_map/ppermute | solution.py:278
  15.3 15.2 %all-to-all-start = ((bf16[16,48,128]{2,1,0:T(8,128)(2,1)}), bf16[16,48,128]{2,1,0:T(8,128)(2,1)S(1)}, u32[]{:S(2)}, u32[]{:S(2)}) async-start(bf16[16,48,128]{2,1,0:T(8,128)(2,1)} %shard_map.100), calls=%async_computation | async-start | bytes 393216 | tf_op jit(solution)/shard_map/all_to_all | solution.py:268
  30.5 0.0 collective-permute-done
  30.5 0.0 collective-permute-done.1
  30.6 0.0 collective-permute-done.2
  30.6 1.9 %collective-permute-start.3 = (bf16[4,128,128]{2,1,0:T(8,128)(2,1)S(1)}, bf16[4,128,128]{2,1,0:T(8,128)(2,1)S(1)}, u32[]{:S(2)}, u32[]{:S(2)}) collective-permute-start(bf16[4,128,128]{2,1,0:T(8,128)(2,1)S(1)} %pad_maximum_fusion), channel_id=1, source_target_pairs={{0,16},{16,0},{32,48},{48,32},{64,80},{80,64},{96,112},{112,96},{1... | collective-permute-start | bytes 393224 | tf_op jit(solution)/shard_map/ppermute | solution.py:278
  32.6 13.7 %all-to-all-done.in_ref = bf16[16,48,128]{2,1,0:T(8,128)(2,1)S(1)} async-done(((bf16[16,48,128]{2,1,0:T(8,128)(2,1)}), bf16[16,48,128]{2,1,0:T(8,128)(2,1)S(1)}, u32[]{:S(2)}, u32[]{:S(2)}) %all-to-all-start) | async-done | bytes 196640 | tf_op jit(solution)/shard_map/all_to_all | solution.py:268
  46.3 0.9 shard_map.101
  47.2 0.0 copy-start
  47.2 7.2 %all-to-all-start.1 = ((bf16[32,64,128]{2,1,0:T(8,128)(2,1)}), bf16[32,64,128]{2,1,0:T(8,128)(2,1)S(1)}, u32[]{:S(2)}, u32[]{:S(2)}) async-start(bf16[32,64,128]{2,1,0:T(8,128)(2,1)} %shard_map.101), calls=%async_computation.1 | async-start | bytes 1048576 | tf_op jit(solution)/shard_map/all_to_all | solution.py:268
  54.4 0.0 copy-start.6
  54.4 3.8 %collective-permute-start.4 = (bf16[4,128,128]{2,1,0:T(8,128)(2,1)S(1)}, bf16[4,128,128]{2,1,0:T(8,128)(2,1)S(1)}, u32[]{:S(2)}, u32[]{:S(2)}) collective-permute-start(bf16[4,128,128]{2,1,0:T(8,128)(2,1)S(1)} %pad_maximum_fusion.1), channel_id=1, source_target_pairs={{0,128},{16,144},{32,160},{48,176},{64,192},{80,208},{96,224},{112... | collective-permute-start | bytes 393224 | tf_op jit(solution)/shard_map/ppermute | solution.py:278
  58.3 1.9 %collective-permute-start.5 = (bf16[4,128,128]{2,1,0:T(8,128)(2,1)S(1)}, bf16[4,128,128]{2,1,0:T(8,128)(2,1)S(1)}, u32[]{:S(2)}, u32[]{:S(2)}) collective-permute-start(bf16[4,128,128]{2,1,0:T(8,128)(2,1)S(1)} %pad_maximum_fusion.2), channel_id=1, source_target_pairs={{0,144},{16,128},{32,176},{48,160},{64,208},{80,192},{96,240},{112... | collective-permute-start | bytes 393224 | tf_op jit(solution)/shard_map/ppermute | solution.py:278
  60.2 0.0 collective-permute-done.3
  60.2 0.0 copy-start.7
  60.2 6.1 %collective-permute-done.4 = bf16[4,128,128]{2,1,0:T(8,128)(2,1)S(1)} collective-permute-done((bf16[4,128,128]{2,1,0:T(8,128)(2,1)S(1)}, bf16[4,128,128]{2,1,0:T(8,128)(2,1)S(1)}, u32[]{:S(2)}, u32[]{:S(2)}) %collective-permute-start.4) | collective-permute-done | bytes 131104 | tf_op jit(solution)/shard_map/ppermute | solution.py:278
  66.3 0.0 copy-start.9
  66.3 0.0 copy-start.10
  66.4 2.5 %collective-permute-done.5 = bf16[4,128,128]{2,1,0:T(8,128)(2,1)S(1)} collective-permute-done((bf16[4,128,128]{2,1,0:T(8,128)(2,1)S(1)}, bf16[4,128,128]{2,1,0:T(8,128)(2,1)S(1)}, u32[]{:S(2)}, u32[]{:S(2)}) %collective-permute-start.5) | collective-permute-done | bytes 131104 | tf_op jit(solution)/shard_map/ppermute | solution.py:278
  68.9 0.0 all-to-all-done.1.in_ref
  68.9 0.0 copy-done
  68.9 0.0 copy-done.6
  68.9 0.0 copy-done.7
  69.0 0.0 copy-done.9
  69.0 0.0 copy-done.10
  69.0 4.8 %shard_map.103 = bf16[32,64,128]{2,1,0:T(8,128)(2,1)S(1)} custom-call(s32[2]{0:T(128)S(1)} %pad_add_fusion.place_ref, bf16[32,64,128]{2,1,0:T(8,128)(2,1)S(1)} %all-to-all-done.1.in_ref, bf16[16,128,128]{2,1,0:T(8,128)(2,1)S(1)} %constant_dynamic-update-slice_fusion.spectra_ref, f32[2,64,128]{2,1,0:T(8,128)S(1)} %copy-done.9, ...), custom_call_target="tpu_custom_call" | custom-call | tf_op jit(solution)/shard_map/pallas_call | solution.py:242
  73.8 17.6 %all_to_all.20.in_ref = bf16[32,64,128]{2,1,0:T(8,128)(2,1)S(1)} all-to-all(bf16[32,64,128]{2,1,0:T(8,128)(2,1)S(1)} %shard_map.103), channel_id=1, replica_groups=mesh['ctx'=32,'chan'=16] {'ctx'}, dimensions={0} | all-to-all | bytes 1048576 | tf_op jit(solution)/shard_map/all_to_all | solution.py:268
  91.4 0.0 copy-start.8
  91.4 0.7 shard_map.104
  92.2 0.0 copy-start.3
  92.2 4.9 %all-to-all-start.3 = ((bf16[16,48,128]{2,1,0:T(8,128)(2,1)}), bf16[16,48,128]{2,1,0:T(8,128)(2,1)S(1)}, u32[]{:S(2)}, u32[]{:S(2)}) async-start(bf16[16,48,128]{2,1,0:T(8,128)(2,1)} %shard_map.104), calls=%async_computation.3 | async-start | bytes 393216 | tf_op jit(solution)/shard_map/all_to_all | solution.py:268
  97.0 0.7 copy-done.11
  97.7 0.1 copy.11.skip_ref
  97.8 15.3 %all-to-all-done.3.conv_ref = bf16[16,48,128]{2,1,0:T(8,128)(2,1)S(1)} async-done(((bf16[16,48,128]{2,1,0:T(8,128)(2,1)}), bf16[16,48,128]{2,1,0:T(8,128)(2,1)S(1)}, u32[]{:S(2)}, u32[]{:S(2)}) %all-to-all-start.3) | async-done | bytes 196640 | tf_op jit(solution)/shard_map/all_to_all | solution.py:268
  113.1 0.0 copy-done.8
  113.2 0.0 copy-done.3
  113.2 0.0 copy-done.5
  113.2 0.9 shard_map.105
  (14 shorter events, 0.2 us)
Async XLA Ops:
  0.0 0.9 copy-start.2
  0.9 0.9 copy-start.4
  2.7 1.1 copy-start.1
  4.8 25.7 %collective-permute-start = (bf16[4,128,128]{2,1,0:T(8,128)(2,1)S(1)}, bf16[4,128,128]{2,1,0:T(8,128)(2,1)S(1)}, u32[]{:S(2)}, u32[]{:S(2)}) collective-permute-start(bf16[4,128,128]{2,1,0:T(8,128)(2,1)S(1)} %get-tuple-element.15), channel_id=1, source_target_pairs={{0,32},{16,48},{32,0},{48,16},{64,96},{80,112},{96,64},{112,80},{1... | collective-permute-start | bytes 393224 | tf_op jit(solution)/shard_map/ppermute | solution.py:278
  8.2 22.3 %collective-permute-start.1 = (bf16[4,128,128]{2,1,0:T(8,128)(2,1)S(1)}, bf16[4,128,128]{2,1,0:T(8,128)(2,1)S(1)}, u32[]{:S(2)}, u32[]{:S(2)}) collective-permute-start(bf16[4,128,128]{2,1,0:T(8,128)(2,1)S(1)} %get-tuple-element.14), channel_id=1, source_target_pairs={{0,64},{16,80},{32,96},{48,112},{64,0},{80,16},{96,32},{112,48},{1... | collective-permute-start | bytes 393224 | tf_op jit(solution)/shard_map/ppermute | solution.py:278
  12.9 17.7 %collective-permute-start.2 = (bf16[4,128,128]{2,1,0:T(8,128)(2,1)S(1)}, bf16[4,128,128]{2,1,0:T(8,128)(2,1)S(1)}, u32[]{:S(2)}, u32[]{:S(2)}) collective-permute-start(bf16[4,128,128]{2,1,0:T(8,128)(2,1)S(1)} %get-tuple-element.13), channel_id=1, source_target_pairs={{0,96},{16,112},{32,64},{48,80},{64,32},{80,48},{96,0},{112,16},{1... | collective-permute-start | bytes 393224 | tf_op jit(solution)/shard_map/ppermute | solution.py:278
  15.3 31.0 %all-to-all-start = ((bf16[16,48,128]{2,1,0:T(8,128)(2,1)}), bf16[16,48,128]{2,1,0:T(8,128)(2,1)S(1)}, u32[]{:S(2)}, u32[]{:S(2)}) async-start(bf16[16,48,128]{2,1,0:T(8,128)(2,1)} %shard_map.100), calls=%async_computation | async-start | bytes 393216 | tf_op jit(solution)/shard_map/all_to_all | solution.py:268
  30.6 29.6 %collective-permute-start.3 = (bf16[4,128,128]{2,1,0:T(8,128)(2,1)S(1)}, bf16[4,128,128]{2,1,0:T(8,128)(2,1)S(1)}, u32[]{:S(2)}, u32[]{:S(2)}) collective-permute-start(bf16[4,128,128]{2,1,0:T(8,128)(2,1)S(1)} %pad_maximum_fusion), channel_id=1, source_target_pairs={{0,16},{16,0},{32,48},{48,32},{64,80},{80,64},{96,112},{112,96},{1... | collective-permute-start | bytes 393224 | tf_op jit(solution)/shard_map/ppermute | solution.py:278
  47.2 21.8 %copy-start = (f32[2,16,64,128]{3,2,1,0:T(8,128)S(1)}, f32[2,16,64,128]{3,2,1,0:T(8,128)}, u32[]{:S(2)}) copy-start(f32[2,16,64,128]{3,2,1,0:T(8,128)} %constant.21.clone.block_ref) | copy-start | bytes 3145732
  47.2 21.8 %all-to-all-start.1 = ((bf16[32,64,128]{2,1,0:T(8,128)(2,1)}), bf16[32,64,128]{2,1,0:T(8,128)(2,1)S(1)}, u32[]{:S(2)}, u32[]{:S(2)}) async-start(bf16[32,64,128]{2,1,0:T(8,128)(2,1)} %shard_map.101), calls=%async_computation.1 | async-start | bytes 1048576 | tf_op jit(solution)/shard_map/all_to_all | solution.py:268
  54.4 14.6 %copy-start.6 = (bf16[2,768,256]{2,1,0:T(8,128)(2,1)S(1)}, bf16[2,768,256]{2,1,0:T(8,128)(2,1)}, u32[]{:S(2)}) copy-start(bf16[2,768,256]{2,1,0:T(8,128)(2,1)} %constant.24.clone.lane_matrix_ref) | copy-start | bytes 2359300
  54.4 11.9 %collective-permute-start.4 = (bf16[4,128,128]{2,1,0:T(8,128)(2,1)S(1)}, bf16[4,128,128]{2,1,0:T(8,128)(2,1)S(1)}, u32[]{:S(2)}, u32[]{:S(2)}) collective-permute-start(bf16[4,128,128]{2,1,0:T(8,128)(2,1)S(1)} %pad_maximum_fusion.1), channel_id=1, source_target_pairs={{0,128},{16,144},{32,160},{48,176},{64,192},{80,208},{96,224},{112... | collective-permute-start | bytes 393224 | tf_op jit(solution)/shard_map/ppermute | solution.py:278
  58.3 10.6 %collective-permute-start.5 = (bf16[4,128,128]{2,1,0:T(8,128)(2,1)S(1)}, bf16[4,128,128]{2,1,0:T(8,128)(2,1)S(1)}, u32[]{:S(2)}, u32[]{:S(2)}) collective-permute-start(bf16[4,128,128]{2,1,0:T(8,128)(2,1)S(1)} %pad_maximum_fusion.2), channel_id=1, source_target_pairs={{0,144},{16,128},{32,176},{48,160},{64,208},{80,192},{96,240},{112... | collective-permute-start | bytes 393224 | tf_op jit(solution)/shard_map/ppermute | solution.py:278
  60.2 8.7 %copy-start.7 = (bf16[2,128,384]{2,1,0:T(8,128)(2,1)S(1)}, bf16[2,128,384]{2,1,0:T(8,128)(2,1)}, u32[]{:S(2)}) copy-start(bf16[2,128,384]{2,1,0:T(8,128)(2,1)} %constant.23.clone.row_matrix_ref) | copy-start | bytes 589828
  66.3 2.6 %copy-start.9 = (f32[2,64,128]{2,1,0:T(8,128)S(1)}, f32[2,64,128]{2,1,0:T(8,128)}, u32[]{:S(2)}) copy-start(f32[2,64,128]{2,1,0:T(8,128)} %constant.20.clone.parity_ref) | copy-start | bytes 196612
  66.3 2.6 %copy-start.10 = (f32[2,64,128]{2,1,0:T(8,128)S(1)}, f32[2,64,128]{2,1,0:T(8,128)}, u32[]{:S(2)}) copy-start(f32[2,64,128]{2,1,0:T(8,128)} %constant.22.clone.lane_ref) | copy-start | bytes 196612
  91.4 21.7 %copy-start.8 = (bf16[192,512]{1,0:T(8,128)(2,1)S(1)}, bf16[192,512]{1,0:T(8,128)(2,1)}, u32[]{:S(2)}) copy-start(bf16[192,512]{1,0:T(8,128)(2,1)} %gate_ref.1) | copy-start | bytes 589828
  92.2 21.0 %copy-start.3 = (bf16[192,512]{1,0:T(8,128)(2,1)S(1)}, bf16[192,512]{1,0:T(8,128)(2,1)}, u32[]{:S(2)}) copy-start(bf16[192,512]{1,0:T(8,128)(2,1)} %key_ref.3) | copy-start | bytes 589828
  92.2 21.0 %copy-start.5 = (bf16[192,512]{1,0:T(8,128)(2,1)S(1)}, bf16[192,512]{1,0:T(8,128)(2,1)}, u32[]{:S(2)}) copy-start(bf16[192,512]{1,0:T(8,128)(2,1)} %value_ref.3) | copy-start | bytes 589828
  92.2 21.0 %all-to-all-start.3 = ((bf16[16,48,128]{2,1,0:T(8,128)(2,1)}), bf16[16,48,128]{2,1,0:T(8,128)(2,1)S(1)}, u32[]{:S(2)}, u32[]{:S(2)}) async-start(bf16[16,48,128]{2,1,0:T(8,128)(2,1)} %shard_map.104), calls=%async_computation.3 | async-start | bytes 393216 | tf_op jit(solution)/shard_map/all_to_all | solution.py:268
  97.0 0.7 copy-start.11

commit v4 on v3

--- a/solution.py
+++ b/solution.py
@@ -105,20 +105,13 @@
         out_ref[rows, :] = (gate_ref[rows, :].astype(F32) * total).astype(BF16)
 
 
-def spectra_kernel(place_ref, in_ref, out_ref):
-    place = place_ref[0]
+def spectra_kernel(in_ref, out_ref):
     for channel in range(GROUP):
-        distance = place ^ channel
-        slot = (((distance >> 1) & 3) << 2) | ((distance >> 3) << 1) | (distance & 1)
         parts = []
         for part in range(2):
             turned = in_ref[part, channel].T
             parts.append(jnp.concatenate([turned[:64, :], turned[64:, :]], axis=1))
-        out_ref[slot] = jnp.concatenate(parts, axis=0).astype(BF16)
-    for channel in range(GROUP, HALF):
-        distance = place ^ channel
-        slot = (((distance >> 1) & 3) << 2) | ((distance >> 3) << 1) | (distance & 1)
-        out_ref[slot] = jnp.zeros((2 * ROWS, LANES), BF16)
+        out_ref[channel] = jnp.concatenate(parts, axis=0).astype(BF16)
 
 
 def split(x):
@@ -131,9 +124,20 @@
 
 
 def filter_kernel(
-    place_ref, in_ref, spectra_ref, parity_ref, block_ref, lane_ref, row_matrix_ref, lane_matrix_ref, out_ref, real, pair
+    place_ref,
+    in_ref,
+    here_ref,
+    there_ref,
+    parity_ref,
+    block_ref,
+    lane_ref,
+    row_matrix_ref,
+    lane_matrix_ref,
+    out_ref,
+    real,
+    pair,
 ):
-    place = place_ref[0]
+    core = place_ref[0] & 1
     odd = place_ref[1]
     sign = jnp.where(odd == 0, 1.0, -1.0).astype(F32)
 
@@ -175,7 +179,8 @@
         shaped = []
         for index in range(CLASSES):
             rows = slice(ROWS * index, ROWS * index + ROWS)
-            response = spectra_ref[slot_of(place ^ rev4(first + index))].astype(F32)
+            source = rev4(first + index)
+            response = jnp.where(core == source % 2, here_ref[source // 2], there_ref[source // 2]).astype(F32)
             term = c_mul((spectrum[rows, :LANES], spectrum[rows, LANES:]), response[:ROWS], response[ROWS:])
             shaped.append(jnp.concatenate(term, axis=1))
         high, low = split(jnp.concatenate(shaped, axis=0))
@@ -250,17 +255,16 @@
     )(*operands)
 
 
-def apply_filter(place, series, response, **kwargs):
+def apply_filter(place, series, response):
     return call(
         filter_kernel,
         ((N_CTX, ROWS, LANES), BF16),
         [(HALF, ROWS, LANES), (2 * ROWS, HALF * LANES)],
         place,
         series,
-        response,
+        *response,
         *(jnp.asarray(table) for table in tables()),
         scalars=1,
-        **kwargs,
     )
 
 
@@ -268,21 +272,13 @@
     return lax.all_to_all(x, axis, split_axis=0, concat_axis=0, tiled=True)
 
 
-def slot_of(distance):
-    return ((distance >> 3) << 3) | ((distance & 1) << 2) | ((distance >> 1) & 3)
-
-
-def swap(pieces, distances):
-    there = [pieces[0]]
-    for piece, distance in zip(pieces[1:], distances[1:]):
-        there.append(lax.ppermute(piece, "ctx", [(device, device ^ distance) for device in range(N_CTX)]))
-    return there
-
-
-def spread_spectra(blocks):
-    pieces = swap([blocks[4 * x : 4 * x + 4] for x in range(4)], (0, 2, 4, 6))
-    pieces = swap([jnp.stack([piece[other] for piece in pieces]) for other in range(4)], (0, 1, 8, 9))
-    return jnp.concatenate(pieces, axis=0)
+def spread_spectra(blocks, place):
+    equal_core = [[16 * half + 2 * chip + core for chip in range(8)] for half in range(2) for core in range(2)]
+    blocks = lax.all_gather(blocks, "ctx", axis_index_groups=equal_core)
+    here = lax.dynamic_index_in_dim(blocks, place[0], 1, keepdims=False)
+    there = lax.dynamic_index_in_dim(blocks, place[0] ^ 1, 1, keepdims=False)
+    there = lax.ppermute(there, "ctx", [(device, device ^ 1) for device in range(N_CTX)])
+    return here, there
 
 
 def body(value_branch, key_branch, gate_branch, skip_gain, spectra):
@@ -294,14 +290,9 @@
     )
     packed, spectra = lax.optimization_barrier((packed, spectra))
     response = call(
-        spectra_kernel,
-        ((HALF, 2 * ROWS, LANES), BF16),
-        [],
-        place,
-        spectra.reshape(2, GROUP, ROWS, LANES),
-        scalars=1,
-    )
-    response = spread_spectra(response)
+        spectra_kernel, ((GROUP, 2 * ROWS, LANES), BF16), [], spectra.reshape(2, GROUP, ROWS, LANES)
+    )
+    response = spread_spectra(response, place)
     gathered = exchange(packed, "chan")
     sent = call(fan_out_kernel, ((N_CTX, ROWS, LANES), BF16), [(N_CHAN * 48, LANES)], gathered)
     series = exchange(sent, "ctx")

time: 115 us -> 139 us (1.21)
  blocking collectives: 17.6 us -> 48.3 us
  starting transfers between devices: 45.4 us -> 21.8 us
  between operations: 0.28 us -> 13.5 us
  local copies, waits for them, and re-layouts: 3.96 us -> 6.76 us
  waiting for transfers between devices: 37.6 us -> 39.7 us
    all_to_all x1 -> x2, blocking collectives: 17.6 us -> 48.3 us  [exchange(): return lax.all_to_all(x, axis, split_axis=0, concat_axis=0, tiled=True)]
    all_gather x0 -> x1, waiting for transfers between devices: none -> 22.1 us  [spread_spectra(): blocks = lax.all_gather(blocks, 'ctx', axis_index_groups=equal_core)]
    ppermute x6 -> x1, starting transfers between devices: 18.1 us -> 2.04 us  [spread_spectra(): lax.ppermute(there, 'ctx', [(device, device ^ 1) for device in range(N_CT...]
    all_to_all x3 -> x2, waiting for transfers between devices: 29 us -> 16 us  [exchange(): return lax.all_to_all(x, axis, split_axis=0, concat_axis=0, tiled=True)]
    all_to_all x3 -> x2, starting transfers between devices: 27.3 us -> 19.8 us  [exchange(): return lax.all_to_all(x, axis, split_axis=0, concat_axis=0, tiled=True)]
    ppermute x6 -> x1, waiting for transfers between devices: 8.61 us -> 1.63 us  [spread_spectra(): lax.ppermute(there, 'ctx', [(device, device ^ 1) for device in range(N_CT...]
    squeeze x0 -> x1, local copies, waits for them, and re-layouts: none -> 1.79 us  [spread_spectra(): there = lax.dynamic_index_in_dim(blocks, place[0] ^ 1, 1, keepdims=False)]
    unnamed x26 -> x24, local copies, waits for them, and re-layouts: 3.74 us -> 4.86 us
  transfers between devices with their start and end apart: 9 -> 4, of which waited for: 4 -> 3; matrix products, arithmetic and copies ran while one was open for 0% -> 1% of each run, Pallas kernels for 1% -> 1%
where the time goes in v4:
time: 139 us
  blocking collectives  48.3 us (35%)
  waiting for transfers between devices  39.7 us (29%)
  starting transfers between devices  21.8 us (16%)
  between operations  13.5 us (10%)
  Pallas kernels  8.51 us (6%)
  local copies, waits for them, and re-layouts  6.76 us (5%)
    all_to_all x2, blocking collectives, exchange(): return lax.all_to_all(x, axis, split_axis=0, concat_axis=0, tiled=True)  48.3 us
    all_gather x1, waiting for transfers between devices, spread_spectra(): blocks = lax.all_gather(blocks, 'ctx', axis_index_groups=equal_core)  22.1 us
    all_to_all x2, starting transfers between devices, exchange(): return lax.all_to_all(x, axis, split_axis=0, concat_axis=0, tiled=True)  19.8 us
    all_to_all x2, waiting for transfers between devices, exchange(): return lax.all_to_all(x, axis, split_axis=0, concat_axis=0, tiled=True)  16 us
    pallas_call x6, Pallas kernels, call(): pl.pallas_call(kernel, out_shape=jax.ShapeDtypeStruct(*out_shape), in_spe...  8.51 us
    unnamed x24, local copies, waits for them, and re-layouts  4.86 us
  transfers between devices with their start and end apart: 4, of which 3 were waited for; matrix products, arithmetic and copies ran while one was open for 1% of the time, Pallas kernels for 1%

profile of v4, /device:TPU:32, one launch (start us, length us, event | category | flops | bytes accessed | tf_op | source)
XLA Modules:
  0.0 138.7 jit_solution(74127151429657821)
XLA Ops:
  6.5 0.0 copy-start
  6.5 0.0 all-gather.3.cloned.1.call-start
  6.5 0.0 copy-start.2
  6.5 1.0 copy-done.2
  7.6 0.0 copy-start.4
  7.6 0.9 copy-done.4
  8.5 0.1 shard_map.100
  8.6 0.0 copy-start.1
  8.6 1.1 copy-done.1
  9.7 0.0 copy-start.6
  9.7 0.0 copy-start.7
  9.7 0.0 copy-start.9
  9.7 1.1 shard_map.102
  10.8 0.0 all-gather.3.cloned.1.call-update
  10.9 30.8 %all_to_all.20.in_ref = bf16[16,48,128]{2,1,0:T(8,128)(2,1)S(1)} all-to-all(bf16[16,48,128]{2,1,0:T(8,128)(2,1)S(1)} %shard_map.100), channel_id=1, replica_groups=mesh['ctx'=32,'chan'=16] {'chan'}, dimensions={0} | all-to-all | bytes 393216 | tf_op jit(solution)/shard_map/all_to_all | solution.py:272
  41.7 0.9 shard_map.101
  42.6 7.3 %all-to-all-start.1 = ((bf16[32,64,128]{2,1,0:T(8,128)(2,1)}), bf16[32,64,128]{2,1,0:T(8,128)(2,1)S(1)}, u32[]{:S(2)}, u32[]{:S(2)}) async-start(bf16[32,64,128]{2,1,0:T(8,128)(2,1)} %shard_map.101), calls=%async_computation.1 | async-start | bytes 1048576 | tf_op jit(solution)/shard_map/all_to_all | solution.py:272
  49.9 22.1 %all-gather.3.cloned.1.call-done = bf16[96,128,128]{2,1,0:T(8,128)(2,1)} async-done(((bf16[12,128,128]{2,1,0:T(8,128)(2,1)}), bf16[96,128,128]{2,1,0:T(8,128)(2,1)}) %all-gather.3.cloned.1.call-update) | async-done | bytes 3145744 | tf_op jit(solution)/shard_map/all_gather | solution.py:277
  72.0 0.0 copy-start.11
  72.0 1.8 %dynamic-slice_bitcast_fusion = (bf16[8,128,128]{2,1,0:T(8,128)(2,1)}, bf16[8,128,128]{2,1,0:T(8,128)(2,1)S(1)}) fusion(bf16[8,12,128,128]{3,2,1,0:T(8,128)(2,1)} %bitcast.14, s32[]{:T(128)S(6)} %select_n.8, s32[]{:T(128)S(6)} %select_n.7), kind=kLoop, calls=%fused_computation | loop fusion | bytes 1048584 | tf_op jit(solution)/shard_map/jit(dynamic_index_in_dim)/squeeze | solution.py:279
  73.8 0.0 copy-start.3
  73.8 0.0 copy-start.5
  73.8 2.0 %collective-permute-start = (bf16[8,128,128]{2,1,0:T(8,128)(2,1)}, bf16[8,128,128]{2,1,0:T(8,128)(2,1)S(1)}, u32[]{:S(2)}, u32[]{:S(2)}) collective-permute-start(bf16[8,128,128]{2,1,0:T(8,128)(2,1)} %get-tuple-element.9), channel_id=1, source_target_pairs={{0,16},{16,0},{32,48},{48,32},{64,80},{80,64},{96,112},{112,96},{1... | collective-permute-start | bytes 786440 | tf_op jit(solution)/shard_map/ppermute | solution.py:280
  75.9 0.1 pad_add_fusion.place_ref
  75.9 0.0 all-to-all-done.1.in_ref
  75.9 1.6 %collective-permute-done.there_ref = bf16[8,128,128]{2,1,0:T(8,128)(2,1)S(1)} collective-permute-done((bf16[8,128,128]{2,1,0:T(8,128)(2,1)}, bf16[8,128,128]{2,1,0:T(8,128)(2,1)S(1)}, u32[]{:S(2)}, u32[]{:S(2)}) %collective-permute-start) | collective-permute-done | bytes 262176 | tf_op jit(solution)/shard_map/ppermute | solution.py:280
  77.6 0.0 copy-done
  77.6 0.0 copy-done.6
  77.6 0.0 copy-done.7
  77.6 0.0 copy-done.9
  77.6 0.0 copy-start.10
  77.6 0.8 copy-done.10
  78.4 4.8 %shard_map.103 = bf16[32,64,128]{2,1,0:T(8,128)(2,1)S(1)} custom-call(s32[2]{0:T(128)S(1)} %pad_add_fusion.place_ref, bf16[32,64,128]{2,1,0:T(8,128)(2,1)S(1)} %all-to-all-done.1.in_ref, bf16[8,128,128]{2,1,0:T(8,128)(2,1)S(1)} %get-tuple-element.10.here_ref, bf16[8,128,128]{2,1,0:T(8,128)(2,1)S(1)} %collective-permute-done.there_ref, ...), custom_call_target="tpu_custom_call" | custom-call | tf_op jit(solution)/shard_map/pallas_call | solution.py:247
  83.2 17.5 %all_to_all.21.in_ref = bf16[32,64,128]{2,1,0:T(8,128)(2,1)S(1)} all-to-all(bf16[32,64,128]{2,1,0:T(8,128)(2,1)S(1)} %shard_map.103), channel_id=1, replica_groups=mesh['ctx'=32,'chan'=16] {'ctx'}, dimensions={0} | all-to-all | bytes 1048576 | tf_op jit(solution)/shard_map/all_to_all | solution.py:272
  100.7 0.7 shard_map.104
  101.5 12.5 %all-to-all-start.3 = ((bf16[16,48,128]{2,1,0:T(8,128)(2,1)}), bf16[16,48,128]{2,1,0:T(8,128)(2,1)S(1)}, u32[]{:S(2)}, u32[]{:S(2)}) async-start(bf16[16,48,128]{2,1,0:T(8,128)(2,1)} %shard_map.104), calls=%async_computation.3 | async-start | bytes 393216 | tf_op jit(solution)/shard_map/all_to_all | solution.py:272
  114.0 0.0 copy-done.11
  114.0 0.1 copy.18.skip_ref
  114.1 16.0 %all-to-all-done.3.conv_ref = bf16[16,48,128]{2,1,0:T(8,128)(2,1)S(1)} async-done(((bf16[16,48,128]{2,1,0:T(8,128)(2,1)}), bf16[16,48,128]{2,1,0:T(8,128)(2,1)S(1)}, u32[]{:S(2)}, u32[]{:S(2)}) %all-to-all-start.3) | async-done | bytes 196640 | tf_op jit(solution)/shard_map/all_to_all | solution.py:272
  130.1 0.0 copy-done.3
  130.1 0.0 copy-done.5
  130.1 0.0 copy-start.8
  130.1 0.9 copy-done.8
  131.0 0.9 shard_map.105
Async XLA Ops:
  6.5 71.0 %copy-start = (f32[2,16,64,128]{3,2,1,0:T(8,128)S(1)}, f32[2,16,64,128]{3,2,1,0:T(8,128)}, u32[]{:S(2)}) copy-start(f32[2,16,64,128]{3,2,1,0:T(8,128)} %constant.31.clone.block_ref) | copy-start | bytes 3145732
  6.5 65.5 %all-gather.3.cloned.1.call-start = ((), (), s32[]{:S(2)}) async-start(), calls=%async_computation.4 | async-start | bytes 3538944 | tf_op jit(solution)/shard_map/all_gather | solution.py:277
  6.5 1.0 copy-start.2
  7.6 0.9 copy-start.4
  8.6 1.1 copy-start.1
  9.7 67.9 %copy-start.6 = (bf16[2,768,256]{2,1,0:T(8,128)(2,1)S(1)}, bf16[2,768,256]{2,1,0:T(8,128)(2,1)}, u32[]{:S(2)}) copy-start(bf16[2,768,256]{2,1,0:T(8,128)(2,1)} %constant.34.clone.lane_matrix_ref) | copy-start | bytes 2359300
  9.7 67.9 %copy-start.7 = (bf16[2,128,384]{2,1,0:T(8,128)(2,1)S(1)}, bf16[2,128,384]{2,1,0:T(8,128)(2,1)}, u32[]{:S(2)}) copy-start(bf16[2,128,384]{2,1,0:T(8,128)(2,1)} %constant.33.clone.row_matrix_ref) | copy-start | bytes 589828
  9.7 67.9 %copy-start.9 = (f32[2,64,128]{2,1,0:T(8,128)S(1)}, f32[2,64,128]{2,1,0:T(8,128)}, u32[]{:S(2)}) copy-start(f32[2,64,128]{2,1,0:T(8,128)} %constant.30.clone.parity_ref) | copy-start | bytes 196612
  42.6 33.4 %all-to-all-start.1 = ((bf16[32,64,128]{2,1,0:T(8,128)(2,1)}), bf16[32,64,128]{2,1,0:T(8,128)(2,1)S(1)}, u32[]{:S(2)}, u32[]{:S(2)}) async-start(bf16[32,64,128]{2,1,0:T(8,128)(2,1)} %shard_map.101), calls=%async_computation.1 | async-start | bytes 1048576 | tf_op jit(solution)/shard_map/all_to_all | solution.py:272
  72.0 42.0 %copy-start.11 = (f32[192]{0:T(256)S(1)}, f32[192]{0:T(256)}, u32[]{:S(2)}) copy-start(f32[192]{0:T(256)} %param.13) | copy-start | bytes 2308
  73.8 56.3 %copy-start.3 = (bf16[192,512]{1,0:T(8,128)(2,1)S(1)}, bf16[192,512]{1,0:T(8,128)(2,1)}, u32[]{:S(2)}) copy-start(bf16[192,512]{1,0:T(8,128)(2,1)} %key_ref.3) | copy-start | bytes 589828
  73.8 56.3 %copy-start.5 = (bf16[192,512]{1,0:T(8,128)(2,1)S(1)}, bf16[192,512]{1,0:T(8,128)(2,1)}, u32[]{:S(2)}) copy-start(bf16[192,512]{1,0:T(8,128)(2,1)} %value_ref.3) | copy-start | bytes 589828
  73.8 3.8 %collective-permute-start = (bf16[8,128,128]{2,1,0:T(8,128)(2,1)}, bf16[8,128,128]{2,1,0:T(8,128)(2,1)S(1)}, u32[]{:S(2)}, u32[]{:S(2)}) collective-permute-start(bf16[8,128,128]{2,1,0:T(8,128)(2,1)} %get-tuple-element.9), channel_id=1, source_target_pairs={{0,16},{16,0},{32,48},{48,32},{64,80},{80,64},{96,112},{112,96},{1... | collective-permute-start | bytes 786440 | tf_op jit(solution)/shard_map/ppermute | solution.py:280
  77.6 0.8 copy-start.10
  101.5 28.6 %all-to-all-start.3 = ((bf16[16,48,128]{2,1,0:T(8,128)(2,1)}), bf16[16,48,128]{2,1,0:T(8,128)(2,1)S(1)}, u32[]{:S(2)}, u32[]{:S(2)}) async-start(bf16[16,48,128]{2,1,0:T(8,128)(2,1)} %shard_map.104), calls=%async_computation.3 | async-start | bytes 393216 | tf_op jit(solution)/shard_map/all_to_all | solution.py:272
  130.1 0.9 copy-start.8
Sparse Core Ops, SparseCore 0:
  11.0 60.9 all-gather.2

commit v5 on v4

--- a/solution.py
+++ b/solution.py
@@ -55,54 +55,76 @@
     ]
 
 
-def product_kernel(key_ref, value_ref, out_ref, flat, wide):
+def pack_kernel(key_ref, value_ref, out_ref, wide):
+    low = lax.broadcasted_iota(jnp.int32, (8, LANES), 0) < 4
     for block in range(CHANNELS // 16):
         rows = slice(16 * block, 16 * block + 16)
-        product = key_ref[rows, :].astype(F32) * value_ref[rows, :].astype(F32)
-        flat[rows, :] = product
-    for target in range(N_CHAN):
-        for quarter in range(4):
-            wide[target, GROUP * quarter : GROUP * quarter + GROUP, :] = flat[
-                GROUP * target : GROUP * target + GROUP, LANES * quarter : LANES * quarter + LANES
-            ]
+        carried = (key_ref[rows, :].astype(F32) * value_ref[rows, :].astype(F32)).astype(BF16).astype(F32)
+        for part in range(2):
+            for upper in range(2):
+                a = carried[8 * part : 8 * part + 8, 256 * upper : 256 * upper + 128]
+                b = carried[8 * part : 8 * part + 8, 256 * upper + 128 : 256 * upper + 256]
+                first = jnp.where(low, a, pltpu.roll(b, 4, 0))
+                second = jnp.where(low, pltpu.roll(a, 4, 0), b)
+                for offset, piece in enumerate((first, second)):
+                    quad = 4 * block + 2 * part + offset
+                    start = 24 * upper + 8 * (quad % 3)
+                    wide[quad // 3, start : start + 8, :] = piece
     for target in range(N_CHAN):
         out_ref[target] = wide[target].astype(BF16)
 
 
-def fan_out_kernel(in_ref, out_ref, wide):
-    for source in range(N_CHAN):
-        wide[48 * source : 48 * source + 48, :] = in_ref[source].astype(F32)
-    for channel in range(GROUP):
-        series = wide[pl.ds(channel, ROWS, stride=GROUP), :].astype(BF16)
-        out_ref[channel] = series
-        out_ref[HALF + channel] = series
-    for channel in range(GROUP, HALF):
-        empty = jnp.zeros((ROWS, LANES), BF16)
-        out_ref[channel] = empty
-        out_ref[HALF + channel] = empty
-
-
-def join_kernel(in_ref, out_ref, wide):
-    for channel in range(GROUP):
-        total = in_ref[channel].astype(F32) + in_ref[HALF + channel].astype(F32)
-        wide[pl.ds(channel, ROWS, stride=GROUP), :] = total
-    for target in range(N_CHAN):
-        out_ref[target] = wide[48 * target : 48 * target + 48, :].astype(BF16)
-
-
 def gate_kernel(conv_ref, key_ref, value_ref, gate_ref, skip_ref, out_ref, wide, flat):
+    low = lax.broadcasted_iota(jnp.int32, (8, LANES), 0) < 4
     for source in range(N_CHAN):
         wide[source] = conv_ref[source].astype(F32)
-    for source in range(N_CHAN):
-        for quarter in range(4):
-            flat[GROUP * source : GROUP * source + GROUP, LANES * quarter : LANES * quarter + LANES] = wide[
-                source, GROUP * quarter : GROUP * quarter + GROUP, :
-            ]
+    for block in range(CHANNELS // 8):
+        for upper in range(2):
+            pieces = []
+            for offset in range(2):
+                quad = 2 * block + offset
+                start = 24 * upper + 8 * (quad % 3)
+                pieces.append(wide[quad // 3, start : start + 8, :])
+            first, second = pieces
+            flat[8 * block : 8 * block + 8, 256 * upper : 256 * upper + 128] = jnp.where(
+                low, first, pltpu.roll(second, 4, 0)
+            )
+            flat[8 * block : 8 * block + 8, 256 * upper + 128 : 256 * upper + 256] = jnp.where(
+                low, pltpu.roll(first, 4, 0), second
+            )
     for block in range(CHANNELS // 16):
         rows = slice(16 * block, 16 * block + 16)
         carried = (key_ref[rows, :].astype(F32) * value_ref[rows, :].astype(F32)).astype(BF16).astype(F32)
         total = flat[rows, :] + skip_ref[rows, :] * carried
         out_ref[rows, :] = (gate_ref[rows, :].astype(F32) * total).astype(BF16)
+
+
+def fan_out_kernel(in_ref, blocks_ref, out_ref, wide):
+    for source in range(N_CHAN):
+        wide[48 * source : 48 * source + 48, :] = in_ref[source].astype(F32)
+    for channel in range(GROUP):
+        first = 8 * (channel // 4) + channel % 4
+        pieces = [wide[pl.ds(first + 4 * quarter, ROWS // 2, stride=24), :] for quarter in range(2)]
+        series = jnp.concatenate(pieces, axis=0).astype(BF16)
+        block = blocks_ref[channel]
+        for parity in range(2):
+            out_ref[HALF * parity + channel, 0:ROWS, :] = series
+            out_ref[HALF * parity + channel, ROWS : 3 * ROWS, :] = block
+    for channel in range(GROUP, HALF):
+        for parity in range(2):
+            out_ref[HALF * parity + channel] = jnp.zeros((3 * ROWS, LANES), BF16)
+
+
+def join_kernel(in_ref, out_ref, wide):
+    for channel in range(GROUP):
+        total = in_ref[channel].astype(F32) + in_ref[HALF + channel].astype(F32)
+        first = 8 * (channel // 4) + channel % 4
+        for quarter in range(2):
+            wide[pl.ds(first + 4 * quarter, ROWS // 2, stride=24), :] = total[
+                ROWS // 2 * quarter : ROWS // 2 * quarter + ROWS // 2
+            ]
+    for target in range(N_CHAN):
+        out_ref[target] = wide[48 * target : 48 * target + 48, :].astype(BF16)
 
 
 def spectra_kernel(in_ref, out_ref):
@@ -124,21 +146,9 @@
 
 
 def filter_kernel(
-    place_ref,
-    in_ref,
-    here_ref,
-    there_ref,
-    parity_ref,
-    block_ref,
-    lane_ref,
-    row_matrix_ref,
-    lane_matrix_ref,
-    out_ref,
-    real,
-    pair,
+    odd_ref, in_ref, parity_ref, block_ref, lane_ref, row_matrix_ref, lane_matrix_ref, out_ref, real, pair
 ):
-    core = place_ref[0] & 1
-    odd = place_ref[1]
+    odd = odd_ref[0]
     sign = jnp.where(odd == 0, 1.0, -1.0).astype(F32)
 
     def entry_phase(index, rows):
@@ -150,7 +160,7 @@
         return (re * cosine - im * sine, re * sine + im * cosine)
 
     for index in range(HALF):
-        real[index] = in_ref[index].astype(F32) + sign * in_ref[HALF + index].astype(F32)
+        real[index] = in_ref[index, 0:ROWS, :].astype(F32) + sign * in_ref[HALF + index, 0:ROWS, :].astype(F32)
     for group in range(ROWS // 8):
         rows = slice(8 * group, 8 * group + 8)
         terms = []
@@ -179,8 +189,7 @@
         shaped = []
         for index in range(CLASSES):
             rows = slice(ROWS * index, ROWS * index + ROWS)
-            source = rev4(first + index)
-            response = jnp.where(core == source % 2, here_ref[source // 2], there_ref[source // 2]).astype(F32)
+            response = in_ref[HALF * odd + rev4(first + index), ROWS : 3 * ROWS, :].astype(F32)
             term = c_mul((spectrum[rows, :LANES], spectrum[rows, LANES:]), response[:ROWS], response[ROWS:])
             shaped.append(jnp.concatenate(term, axis=1))
         high, low = split(jnp.concatenate(shaped, axis=0))
@@ -215,9 +224,14 @@
     return np.cos(angle), np.sin(angle)
 
 
+def row_order():
+    pair = np.arange(ROWS // 2)
+    return np.concatenate([2 * pair, 2 * pair + 1])
+
+
 def tables():
-    row, lane = np.arange(ROWS), np.arange(LANES)
-    offset = (LANES * row[:, None] + lane[None, :])[None]
+    row, lane, order = np.arange(ROWS), np.arange(LANES), row_order()
+    offset = (LANES * order[:, None] + lane[None, :])[None]
     kp = np.arange(HALF)[:, None, None]
     parity = np.stack(phases(offset[0], LENGTH)).astype(np.float32)
     block = np.stack(phases(2 * kp * offset, LENGTH)).astype(np.float32)
@@ -227,10 +241,10 @@
         high = matrix.astype(ml_dtypes.bfloat16)
         return high, (matrix - high.astype(np.float64)).astype(ml_dtypes.bfloat16)
 
-    cosine, sine = phases(row[:, None] * row[None, :], ROWS)
+    cosine, sine = phases(row[:, None] * order[None, :], ROWS)
     row_matrices = []
-    for flip in (1, -1):
-        high, low = parts(np.block([[cosine, -flip * sine], [flip * sine, cosine]]))
+    for matrix in (np.block([[cosine, -sine], [sine, cosine]]), np.block([[cosine.T, sine.T], [-sine.T, cosine.T]])):
+        high, low = parts(matrix)
         row_matrices.append(np.concatenate([high, high, low], axis=1))
     order = np.concatenate([np.arange(0, LANES, 2), np.arange(1, LANES, 2)])
     cosine, sine = phases(lane[:, None] * order[None, :], LANES)
@@ -255,14 +269,13 @@
     )(*operands)
 
 
-def apply_filter(place, series, response):
+def apply_filter(odd, received):
     return call(
         filter_kernel,
         ((N_CTX, ROWS, LANES), BF16),
         [(HALF, ROWS, LANES), (2 * ROWS, HALF * LANES)],
-        place,
-        series,
-        *response,
+        odd,
+        received,
         *(jnp.asarray(table) for table in tables()),
         scalars=1,
     )
@@ -272,31 +285,14 @@
     return lax.all_to_all(x, axis, split_axis=0, concat_axis=0, tiled=True)
 
 
-def spread_spectra(blocks, place):
-    equal_core = [[16 * half + 2 * chip + core for chip in range(8)] for half in range(2) for core in range(2)]
-    blocks = lax.all_gather(blocks, "ctx", axis_index_groups=equal_core)
-    here = lax.dynamic_index_in_dim(blocks, place[0], 1, keepdims=False)
-    there = lax.dynamic_index_in_dim(blocks, place[0] ^ 1, 1, keepdims=False)
-    there = lax.ppermute(there, "ctx", [(device, device ^ 1) for device in range(N_CTX)])
-    return here, there
-
-
 def body(value_branch, key_branch, gate_branch, skip_gain, spectra):
-    device = lax.axis_index("ctx")
-    place = jnp.stack([device & 15, device >> 4])
-
-    packed = call(
-        product_kernel, ((N_CHAN, 48, LANES), BF16), [(CHANNELS, TOKENS), (N_CHAN, 48, LANES)], key_branch, value_branch
-    )
-    packed, spectra = lax.optimization_barrier((packed, spectra))
-    response = call(
-        spectra_kernel, ((GROUP, 2 * ROWS, LANES), BF16), [], spectra.reshape(2, GROUP, ROWS, LANES)
-    )
-    response = spread_spectra(response, place)
+    odd = (lax.axis_index("ctx") >> 4)[None]
+    packed = call(pack_kernel, ((N_CHAN, 48, LANES), BF16), [(N_CHAN, 48, LANES)], key_branch, value_branch)
+    blocks = call(spectra_kernel, ((GROUP, 2 * ROWS, LANES), BF16), [], spectra.reshape(2, GROUP, ROWS, LANES))
     gathered = exchange(packed, "chan")
-    sent = call(fan_out_kernel, ((N_CTX, ROWS, LANES), BF16), [(N_CHAN * 48, LANES)], gathered)
-    series = exchange(sent, "ctx")
-    parts = exchange(apply_filter(place, series, response), "ctx")
+    sent = call(fan_out_kernel, ((N_CTX, 3 * ROWS, LANES), BF16), [(N_CHAN * 48, LANES)], gathered, blocks)
+    received = exchange(sent, "ctx")
+    parts = exchange(apply_filter(odd, received), "ctx")
     joined = call(join_kernel, ((N_CHAN, 48, LANES), BF16), [(N_CHAN * 48, LANES)], parts)
     tokens = exchange(joined, "chan")
     return call(

time: 139 us -> 110 us (0.79)
  blocking collectives: 48.3 us -> 14.9 us
  waiting for transfers between devices: 39.7 us -> 54.2 us
  between operations: 13.5 us -> 0.11 us
  starting transfers between devices: 21.8 us -> 28.2 us
  local copies, waits for them, and re-layouts: 6.76 us -> 4.06 us
    all_to_all x2 -> x3, waiting for transfers between devices: 16 us -> 54.2 us  [exchange(): return lax.all_to_all(x, axis, split_axis=0, concat_axis=0, tiled=True)]
    all_to_all x2 -> x1, blocking collectives: 48.3 us -> 14.9 us  [exchange(): return lax.all_to_all(x, axis, split_axis=0, concat_axis=0, tiled=True)]
    all_gather x1 -> x0, waiting for transfers between devices: 22.1 us -> none  [spread_spectra(): blocks = lax.all_gather(blocks, 'ctx', axis_index_groups=equal_core)]
    all_to_all x2 -> x3, starting transfers between devices: 19.8 us -> 28.2 us  [exchange(): return lax.all_to_all(x, axis, split_axis=0, concat_axis=0, tiled=True)]
    ppermute x1 -> x0, starting transfers between devices: 2.04 us -> none  [spread_spectra(): lax.ppermute(there, 'ctx', [(device, device ^ 1) for device in range(N_CT...]
    squeeze x1 -> x0, local copies, waits for them, and re-layouts: 1.79 us -> none  [spread_spectra(): there = lax.dynamic_index_in_dim(blocks, place[0] ^ 1, 1, keepdims=False)]
    ppermute x1 -> x0, waiting for transfers between devices: 1.63 us -> none  [spread_spectra(): lax.ppermute(there, 'ctx', [(device, device ^ 1) for device in range(N_CT...]
  transfers between devices with their start and end apart: 4 -> 3, of which waited for: 3 -> 3; matrix products, arithmetic and copies ran while one was open for 1% -> 0% of each run, Pallas kernels for 1% -> 0%
where the time goes in v5:
time: 110 us
  waiting for transfers between devices  54.2 us (49%)
  starting transfers between devices  28.2 us (26%)
  blocking collectives  14.9 us (14%)
  Pallas kernels  8.47 us (8%)
  local copies, waits for them, and re-layouts  4.06 us (4%)
    all_to_all x3, waiting for transfers between devices, exchange(): return lax.all_to_all(x, axis, split_axis=0, concat_axis=0, tiled=True)  54.2 us
    all_to_all x3, starting transfers between devices, exchange(): return lax.all_to_all(x, axis, split_axis=0, concat_axis=0, tiled=True)  28.2 us
    all_to_all x1, blocking collectives, exchange(): return lax.all_to_all(x, axis, split_axis=0, concat_axis=0, tiled=True)  14.9 us
    pallas_call x6, Pallas kernels, call(): pl.pallas_call(kernel, out_shape=jax.ShapeDtypeStruct(*out_shape), in_spe...  8.47 us
    unnamed x24, local copies, waits for them, and re-layouts  3.94 us
  transfers between devices with their start and end apart: 3, of which 3 were waited for; matrix products, arithmetic and copies ran while one was open for 0% of the time, Pallas kernels for 0%

profile of v5, /device:TPU:32, one launch (start us, length us, event | category | flops | bytes accessed | tf_op | source)
XLA Modules:
  0.0 109.9 jit_solution(9723592077605895356)
XLA Ops:
  0.0 0.0 copy-start.3
  0.0 0.9 copy-done.3
  0.9 0.0 copy-start.5
  0.9 0.9 copy-done.5
  1.9 0.7 shard_map.100
  2.6 15.2 %all-to-all-start = ((bf16[16,48,128]{2,1,0:T(8,128)(2,1)}), bf16[16,48,128]{2,1,0:T(8,128)(2,1)S(1)}, u32[]{:S(2)}, u32[]{:S(2)}) async-start(bf16[16,48,128]{2,1,0:T(8,128)(2,1)} %shard_map.100), calls=%async_computation | async-start | bytes 393216 | tf_op jit(solution)/shard_map/all_to_all | solution.py:285
  17.8 0.0 copy-start.2
  17.8 1.1 %copy-done.2 = f32[2,12,1,8192]{3,2,1,0:T(1,128)S(1)} copy-done((f32[2,12,1,8192]{3,2,1,0:T(1,128)S(1)}, f32[2,12,1,8192]{3,2,1,0:T(1,128)}, u32[]{:S(2)}) %copy-start.2) | copy-done | bytes 786456
  18.9 0.4 shard_map.101.blocks_ref
  19.4 14.3 %all-to-all-done.in_ref = bf16[16,48,128]{2,1,0:T(8,128)(2,1)S(1)} async-done(((bf16[16,48,128]{2,1,0:T(8,128)(2,1)}), bf16[16,48,128]{2,1,0:T(8,128)(2,1)S(1)}, u32[]{:S(2)}, u32[]{:S(2)}) %all-to-all-start) | async-done | bytes 196640 | tf_op jit(solution)/shard_map/all_to_all | solution.py:285
  33.6 1.4 %shard_map.102 = bf16[32,192,128]{2,1,0:T(8,128)(2,1)} custom-call(bf16[16,48,128]{2,1,0:T(8,128)(2,1)S(1)} %all-to-all-done.in_ref, bf16[12,128,128]{2,1,0:T(8,128)(2,1)S(1)} %shard_map.101.blocks_ref), custom_call_target="tpu_custom_call" | custom-call | tf_op jit(solution)/shard_map/pallas_call | solution.py:261
  35.0 0.0 copy-start
  35.0 0.0 copy-start.1
  35.0 0.0 copy-start.9
  35.0 0.0 copy-start.10
  35.1 7.5 %all-to-all-start.1 = ((bf16[32,192,128]{2,1,0:T(8,128)(2,1)}), bf16[32,192,128]{2,1,0:T(8,128)(2,1)S(1)}, u32[]{:S(2)}, u32[]{:S(2)}) async-start(bf16[32,192,128]{2,1,0:T(8,128)(2,1)} %shard_map.102), calls=%async_computation.1 | async-start | bytes 3145728 | tf_op jit(solution)/shard_map/all_to_all | solution.py:285
  42.5 23.9 %all-to-all-done.1.in_ref = bf16[32,192,128]{2,1,0:T(8,128)(2,1)S(1)} async-done(((bf16[32,192,128]{2,1,0:T(8,128)(2,1)}), bf16[32,192,128]{2,1,0:T(8,128)(2,1)S(1)}, u32[]{:S(2)}, u32[]{:S(2)}) %all-to-all-start.1) | async-done | bytes 1572896 | tf_op jit(solution)/shard_map/all_to_all | solution.py:285
  66.5 0.0 copy-done
  66.5 0.0 copy-done.1
  66.5 0.0 copy-done.9
  66.5 0.0 copy-done.10
  66.5 0.0 copy-start.7
  66.5 0.9 copy-done.7
  67.4 4.3 %shard_map.103 = bf16[32,64,128]{2,1,0:T(8,128)(2,1)S(1)} custom-call(s32[1]{0:T(128)} %bitcast.odd_ref, bf16[32,192,128]{2,1,0:T(8,128)(2,1)S(1)} %all-to-all-done.1.in_ref, f32[2,64,128]{2,1,0:T(8,128)S(1)} %copy-done.9, f32[2,16,64,128]{3,2,1,0:T(8,128)S(1)} %copy-done, f32[2,64,128]{2,1,0:T(8,128)S(1)} %copy-done.10, bf16[2,128,384]{2,1,0:T(8,128)(2,1)S(1)} %copy-done.7, ...), custom_call_target="tpu_custom_call" | custom-call | tf_op jit(solution)/shard_map/pallas_call | solution.py:261
  71.7 0.0 copy-start.11
  71.7 0.0 copy-start.4
  71.7 0.0 copy-start.6
  71.7 0.0 copy-start.8
  71.8 14.9 %all_to_all.20.in_ref = bf16[32,64,128]{2,1,0:T(8,128)(2,1)S(1)} all-to-all(bf16[32,64,128]{2,1,0:T(8,128)(2,1)S(1)} %shard_map.103), channel_id=1, replica_groups=mesh['ctx'=32,'chan'=16] {'ctx'}, dimensions={0} | all-to-all | bytes 1048576 | tf_op jit(solution)/shard_map/all_to_all | solution.py:285
  86.6 0.8 shard_map.104
  87.4 5.5 %all-to-all-start.3 = ((bf16[16,48,128]{2,1,0:T(8,128)(2,1)}), bf16[16,48,128]{2,1,0:T(8,128)(2,1)S(1)}, u32[]{:S(2)}, u32[]{:S(2)}) async-start(bf16[16,48,128]{2,1,0:T(8,128)(2,1)} %shard_map.104), calls=%async_computation.3 | async-start | bytes 393216 | tf_op jit(solution)/shard_map/all_to_all | solution.py:285
  93.0 0.0 copy-done.11
  93.0 0.1 copy.11.skip_ref
  93.1 16.0 %all-to-all-done.3.conv_ref = bf16[16,48,128]{2,1,0:T(8,128)(2,1)S(1)} async-done(((bf16[16,48,128]{2,1,0:T(8,128)(2,1)}), bf16[16,48,128]{2,1,0:T(8,128)(2,1)S(1)}, u32[]{:S(2)}, u32[]{:S(2)}) %all-to-all-start.3) | async-done | bytes 196640 | tf_op jit(solution)/shard_map/all_to_all | solution.py:285
  109.1 0.0 copy-done.4
  109.1 0.0 copy-done.6
  109.1 0.0 copy-done.8
  109.1 0.9 shard_map.105
Async XLA Ops:
  0.0 0.9 copy-start.3
  0.9 0.9 copy-start.5
  2.6 31.0 %all-to-all-start = ((bf16[16,48,128]{2,1,0:T(8,128)(2,1)}), bf16[16,48,128]{2,1,0:T(8,128)(2,1)S(1)}, u32[]{:S(2)}, u32[]{:S(2)}) async-start(bf16[16,48,128]{2,1,0:T(8,128)(2,1)} %shard_map.100), calls=%async_computation | async-start | bytes 393216 | tf_op jit(solution)/shard_map/all_to_all | solution.py:285
  17.8 1.1 %copy-start.2 = (f32[2,12,1,8192]{3,2,1,0:T(1,128)S(1)}, f32[2,12,1,8192]{3,2,1,0:T(1,128)}, u32[]{:S(2)}) copy-start(f32[2,12,1,8192]{3,2,1,0:T(1,128)} %param.14) | copy-start | bytes 2359300
  35.0 31.4 %copy-start = (f32[2,16,64,128]{3,2,1,0:T(8,128)S(1)}, f32[2,16,64,128]{3,2,1,0:T(8,128)}, u32[]{:S(2)}) copy-start(f32[2,16,64,128]{3,2,1,0:T(8,128)} %constant.19.clone.block_ref) | copy-start | bytes 3145732
  35.0 31.4 %copy-start.1 = (bf16[2,768,256]{2,1,0:T(8,128)(2,1)S(1)}, bf16[2,768,256]{2,1,0:T(8,128)(2,1)}, u32[]{:S(2)}) copy-start(bf16[2,768,256]{2,1,0:T(8,128)(2,1)} %constant.22.clone.lane_matrix_ref) | copy-start | bytes 2359300
  35.0 31.4 %copy-start.9 = (f32[2,64,128]{2,1,0:T(8,128)S(1)}, f32[2,64,128]{2,1,0:T(8,128)}, u32[]{:S(2)}) copy-start(f32[2,64,128]{2,1,0:T(8,128)} %constant.18.clone.parity_ref) | copy-start | bytes 196612
  35.0 31.4 %copy-start.10 = (f32[2,64,128]{2,1,0:T(8,128)S(1)}, f32[2,64,128]{2,1,0:T(8,128)}, u32[]{:S(2)}) copy-start(f32[2,64,128]{2,1,0:T(8,128)} %constant.20.clone.lane_ref) | copy-start | bytes 196612
  35.1 31.4 %all-to-all-start.1 = ((bf16[32,192,128]{2,1,0:T(8,128)(2,1)}), bf16[32,192,128]{2,1,0:T(8,128)(2,1)S(1)}, u32[]{:S(2)}, u32[]{:S(2)}) async-start(bf16[32,192,128]{2,1,0:T(8,128)(2,1)} %shard_map.102), calls=%async_computation.1 | async-start | bytes 3145728 | tf_op jit(solution)/shard_map/all_to_all | solution.py:285
  66.5 0.9 copy-start.7
  71.7 21.2 %copy-start.11 = (f32[192]{0:T(256)S(1)}, f32[192]{0:T(256)}, u32[]{:S(2)}) copy-start(f32[192]{0:T(256)} %param.13) | copy-start | bytes 2308
  71.7 37.3 %copy-start.4 = (bf16[192,512]{1,0:T(8,128)(2,1)S(1)}, bf16[192,512]{1,0:T(8,128)(2,1)}, u32[]{:S(2)}) copy-start(bf16[192,512]{1,0:T(8,128)(2,1)} %key_ref.3) | copy-start | bytes 589828
  71.7 37.3 %copy-start.6 = (bf16[192,512]{1,0:T(8,128)(2,1)S(1)}, bf16[192,512]{1,0:T(8,128)(2,1)}, u32[]{:S(2)}) copy-start(bf16[192,512]{1,0:T(8,128)(2,1)} %value_ref.3) | copy-start | bytes 589828
  71.7 37.3 %copy-start.8 = (bf16[192,512]{1,0:T(8,128)(2,1)S(1)}, bf16[192,512]{1,0:T(8,128)(2,1)}, u32[]{:S(2)}) copy-start(bf16[192,512]{1,0:T(8,128)(2,1)} %gate_ref.1) | copy-start | bytes 589828
  87.4 21.6 %all-to-all-start.3 = ((bf16[16,48,128]{2,1,0:T(8,128)(2,1)}), bf16[16,48,128]{2,1,0:T(8,128)(2,1)S(1)}, u32[]{:S(2)}, u32[]{:S(2)}) async-start(bf16[16,48,128]{2,1,0:T(8,128)(2,1)} %shard_map.104), calls=%async_computation.3 | async-start | bytes 393216 | tf_op jit(solution)/shard_map/all_to_all | solution.py:285

commit v6 on v5

v6 whole, which is shorter than its diff:
```python
import math

import jax
import jax.numpy as jnp
import ml_dtypes
import numpy as np
from jax import lax
from jax.experimental import pallas as pl
from jax.experimental.pallas import tpu as pltpu
from jax.sharding import PartitionSpec as P

N_CTX = 32
N_CHAN = 16
CHANNELS = 192
GROUP = CHANNELS // N_CHAN
TOKENS = 512
SEQ = 8192
LENGTH = SEQ * N_CTX
LANES = 128
HALF = 16
CLASSES = 8
ROWS = SEQ // LANES
WORK = ROWS // 2
CHIPS = [chip for chip in range(HALF) if (chip + chip // 4) % 4 != 3]
F32 = jnp.float32
BF16 = jnp.bfloat16
VMEM_LIMIT = 32 * 1024 * 1024


def rev5(number):
    return int(f"{number:05b}"[::-1], 2)


def c_root(a, turn, sign):
    if turn == 0:
        return a
    if turn == 0.25:
        return (-a[1], a[0]) if sign > 0 else (a[1], -a[0])
    cosine = math.cos(2 * math.pi * turn)
    sine = sign * math.sin(2 * math.pi * turn)
    return (a[0] * cosine - a[1] * sine, a[0] * sine + a[1] * cosine)


def c_mul(a, re, im):
    return (a[0] * re - a[1] * im, a[0] * im + a[1] * re)


def fft_list(terms, sign):
    size = len(terms)
    if size == 1:
        return terms
    even = fft_list(terms[0::2], sign)
    odd = fft_list(terms[1::2], sign)
    odd = [c_root(term, index / size, sign) for index, term in enumerate(odd)]
    return [(e[0] + o[0], e[1] + o[1]) for e, o in zip(even, odd)] + [
        (e[0] - o[0], e[1] - o[1]) for e, o in zip(even, odd)
    ]


def pack_kernel(key_ref, value_ref, out_ref, wide):
    low = lax.broadcasted_iota(jnp.int32, (8, LANES), 0) < 4
    for block in range(CHANNELS // 16):
        rows = slice(16 * block, 16 * block + 16)
        carried = (key_ref[rows, :].astype(F32) * value_ref[rows, :].astype(F32)).astype(BF16).astype(F32)
        for part in range(2):
            for upper in range(2):
                a = carried[8 * part : 8 * part + 8, 256 * upper : 256 * upper + 128]
                b = carried[8 * part : 8 * part + 8, 256 * upper + 128 : 256 * upper + 256]
                first = jnp.where(low, a, pltpu.roll(b, 4, 0))
                second = jnp.where(low, pltpu.roll(a, 4, 0), b)
                for offset, piece in enumerate((first, second)):
                    quad = 4 * block + 2 * part + offset
                    start = 24 * upper + 8 * (quad % 3)
                    wide[quad // 3, start : start + 8, :] = piece
    for target in range(N_CHAN):
        out_ref[target] = wide[target].astype(BF16)


def gate_kernel(conv_ref, key_ref, value_ref, gate_ref, skip_ref, out_ref, wide, flat):
    low = lax.broadcasted_iota(jnp.int32, (8, LANES), 0) < 4
    for source in range(N_CHAN):
        wide[source] = conv_ref[source].astype(F32)
    for block in range(CHANNELS // 8):
        for upper in range(2):
            pieces = []
            for offset in range(2):
                quad = 2 * block + offset
                start = 24 * upper + 8 * (quad % 3)
                pieces.append(wide[quad // 3, start : start + 8, :])
            first, second = pieces
            flat[8 * block : 8 * block + 8, 256 * upper : 256 * upper + 128] = jnp.where(
                low, first, pltpu.roll(second, 4, 0)
            )
            flat[8 * block : 8 * block + 8, 256 * upper + 128 : 256 * upper + 256] = jnp.where(
                low, pltpu.roll(first, 4, 0), second
            )
    for block in range(CHANNELS // 16):
        rows = slice(16 * block, 16 * block + 16)
        carried = (key_ref[rows, :].astype(F32) * value_ref[rows, :].astype(F32)).astype(BF16).astype(F32)
        total = flat[rows, :] + skip_ref[rows, :] * carried
        out_ref[rows, :] = (gate_ref[rows, :].astype(F32) * total).astype(BF16)


def fan_out_kernel(in_ref, blocks_ref, out_ref, wide):
    for source in range(N_CHAN):
        wide[48 * source : 48 * source + 48, :] = in_ref[source].astype(F32)
    for channel, chip in enumerate(CHIPS):
        first = 8 * (channel // 4) + channel % 4
        pieces = [wide[pl.ds(first + 4 * quarter, ROWS // 2, stride=24), :] for quarter in range(2)]
        series = jnp.concatenate(pieces, axis=0).astype(BF16)
        for core in range(2):
            out_ref[2 * chip + core, 0:ROWS, :] = series
            out_ref[2 * chip + core, ROWS : 2 * ROWS, :] = blocks_ref[2 * channel + core]
    for chip in range(HALF):
        if chip not in CHIPS:
            for core in range(2):
                out_ref[2 * chip + core] = jnp.zeros((2 * ROWS, LANES), BF16)


def join_kernel(in_ref, out_ref, wide):
    for channel, chip in enumerate(CHIPS):
        total = in_ref[2 * chip].astype(F32) + in_ref[2 * chip + 1].astype(F32)
        first = 8 * (channel // 4) + channel % 4
        for quarter in range(2):
            wide[pl.ds(first + 4 * quarter, ROWS // 2, stride=24), :] = total[
                ROWS // 2 * quarter : ROWS // 2 * quarter + ROWS // 2
            ]
    for target in range(N_CHAN):
        out_ref[target] = wide[48 * target : 48 * target + 48, :].astype(BF16)


def spectra_kernel(in_ref, out_ref, turned):
    for channel in range(GROUP):
        for part in range(2):
            turned[LANES * part : LANES * part + LANES, :] = in_ref[part, channel].T
        for core in range(2):
            parts = []
            for part in range(2):
                starts = [LANES * part + 64 * upper + core for upper in range(2)]
                halves = [turned[pl.ds(start, 32, stride=2), :] for start in starts]
                parts.append(jnp.concatenate(halves, axis=1))
            out_ref[2 * channel + core] = jnp.concatenate(parts, axis=0).astype(BF16)


def split(x):
    high = x.astype(BF16)
    return high, (x - high.astype(F32)).astype(BF16)


def dot(a, b):
    return jnp.dot(a, b, preferred_element_type=F32)


def filter_kernel(core_ref, in_ref, block_ref, lane_ref, row_matrix_ref, lane_matrix_ref, out_ref, real, pair):
    sign = jnp.where(core_ref[0] == 0, 1.0, -1.0).astype(F32)
    for index in range(N_CTX):
        real[index] = in_ref[index, 0:ROWS, :].astype(F32)

    def places(group):
        start = 32 * (group // 2) + 8 * (group % 2)
        return slice(start, start + 8), slice(start + 16, start + 24), 8 * group

    for group in range(WORK // 8):
        early, late, row = places(group)
        sums = fft_list([(real[p, early, :], sign * real[p, late, :]) for p in range(N_CTX)], -1)
        for residue in range(N_CTX):
            here, mirror = sums[residue], sums[-residue % N_CTX]
            first = (here[0] + mirror[0], here[1] - mirror[1])
            second = (here[1] + mirror[1], mirror[0] - here[0])
            second = c_root(second, residue / 64, -1)
            term = (first[0] + second[0], first[1] + second[1])
            rows = slice(row, row + 8)
            term = c_mul(term, block_ref[0, residue, rows, :], block_ref[1, residue, rows, :])
            columns = slice(LANES * residue, LANES * residue + LANES)
            pair[row : row + 8, columns] = term[0]
            pair[WORK + row : WORK + row + 8, columns] = term[1]
    lane_re, lane_im = lane_ref[0], lane_ref[1]
    for first in range(0, N_CTX, CLASSES):
        columns = slice(LANES * first, LANES * (first + CLASSES))
        high, low = split(pair[:, columns])
        mixed = dot(row_matrix_ref[0], jnp.concatenate([high, low, high], axis=0))
        turned = []
        for index in range(CLASSES):
            lanes = slice(LANES * index, LANES * index + LANES)
            term = c_mul((mixed[:WORK, lanes], mixed[WORK:, lanes]), lane_re, lane_im)
            turned.append(jnp.concatenate(term, axis=1))
        high, low = split(jnp.concatenate(turned, axis=0))
        spectrum = dot(jnp.concatenate([high, low, high], axis=1), lane_matrix_ref[0])
        shaped = []
        for index in range(CLASSES):
            rows = slice(WORK * index, WORK * index + WORK)
            response = in_ref[rev5(first + index), ROWS : 2 * ROWS, :].astype(F32)
            term = c_mul((spectrum[rows, :LANES], spectrum[rows, LANES:]), response[:WORK], response[WORK:])
            shaped.append(jnp.concatenate(term, axis=1))
        high, low = split(jnp.concatenate(shaped, axis=0))
        mixed = dot(jnp.concatenate([high, low, high], axis=1), lane_matrix_ref[1])
        turned = []
        for index in range(CLASSES):
            rows = slice(WORK * index, WORK * index + WORK)
            term = c_mul((mixed[rows, :LANES], mixed[rows, LANES:]), lane_re, -lane_im)
            turned.append(jnp.concatenate(term, axis=0))
        high, low = split(jnp.concatenate(turned, axis=1))
        pair[:, columns] = dot(row_matrix_ref[1], jnp.concatenate([high, low, high], axis=0))
    for group in range(WORK // 8):
        early, late, row = places(group)
        rows = slice(row, row + 8)
        evens, odds = [], []
        for residue in range(N_CTX):
            columns = slice(LANES * residue, LANES * residue + LANES)
            term = (pair[row : row + 8, columns], pair[WORK + row : WORK + row + 8, columns])
            term = c_mul(term, block_ref[0, residue, rows, :], -block_ref[1, residue, rows, :])
            evens.append(term)
            odds.append(c_root(term, residue / 64, 1))
        terms = []
        for residue in range(N_CTX):
            mirror = -residue % N_CTX
            even = (evens[residue][0] + evens[mirror][0], evens[residue][1] - evens[mirror][1])
            odd = (odds[residue][0] + odds[mirror][0], odds[residue][1] - odds[mirror][1])
            terms.append((even[0] - odd[1], even[1] + odd[0]))
        for p, term in enumerate(fft_list(terms, 1)):
            real[p, early, :] = term[0]
            real[p, late, :] = sign * term[1]
    for index in range(N_CTX):
        out_ref[index] = real[index].astype(BF16)


def phases(numerator, denominator):
    angle = -2 * np.pi * (numerator % denominator) / denominator
    return np.cos(angle), np.sin(angle)


def row_order():
    pair = np.arange(ROWS // 2)
    return np.concatenate([2 * pair, 2 * pair + 1])


def tables():
    row, lane = np.arange(WORK), np.arange(LANES)
    half = np.arange(WORK // 2)
    order = np.concatenate([2 * half, 2 * half + 1])
    offset = (LANES * order[:, None] + lane[None, :])[None]
    frequency = (np.arange(N_CTX)[None, :] + 32 * np.arange(2)[:, None])[:, :, None, None]
    block = np.stack(phases(offset * frequency, LENGTH), axis=1).astype(np.float32)
    lane_phase = np.stack(phases(row[:, None] * lane[None, :], 4096)).astype(np.float32)

    def parts(matrix):
        high = matrix.astype(ml_dtypes.bfloat16)
        return high, (matrix - high.astype(np.float64)).astype(ml_dtypes.bfloat16)

    cosine, sine = phases(row[:, None] * order[None, :], WORK)
    row_matrices = []
    for matrix in (np.block([[cosine, -sine], [sine, cosine]]), np.block([[cosine.T, sine.T], [-sine.T, cosine.T]])):
        high, low = parts(matrix)
        row_matrices.append(np.concatenate([high, high, low], axis=1))
    order = np.concatenate([np.arange(0, LANES, 2), np.arange(1, LANES, 2)])
    cosine, sine = phases(lane[:, None] * order[None, :], LANES)
    forward = np.block([[cosine, sine], [-sine, cosine]])
    inverse = np.block([[cosine.T, -sine.T], [sine.T, cosine.T]]) / (4 * LENGTH)
    lane_matrices = []
    for matrix in (forward, inverse):
        high, low = parts(matrix)
        lane_matrices.append(np.concatenate([high, high, low], axis=0))
    return block, lane_phase, np.stack(row_matrices), np.stack(lane_matrices)


def call(kernel, out_shape, scratch, *operands, scalars=0):
    return pl.pallas_call(
        kernel,
        out_shape=jax.ShapeDtypeStruct(*out_shape),
        in_specs=[pl.BlockSpec(memory_space=pltpu.SMEM)] * scalars
        + [pl.BlockSpec(memory_space=pltpu.VMEM)] * (len(operands) - scalars),
        out_specs=pl.BlockSpec(memory_space=pltpu.VMEM),
        scratch_shapes=[pltpu.VMEM(shape, F32) for shape in scratch],
        compiler_params=pltpu.CompilerParams(vmem_limit_bytes=VMEM_LIMIT),
    )(*operands)


def apply_filter(core, received):
    block, *others = (jnp.asarray(table) for table in tables())
    block = lax.dynamic_index_in_dim(block, core[0], 0, keepdims=False)
    return call(
        filter_kernel,
        ((N_CTX, ROWS, LANES), BF16),
        [(N_CTX, ROWS, LANES), (2 * WORK, N_CTX * LANES)],
        core,
        received,
        block,
        *others,
        scalars=1,
    )


def exchange(x, axis):
    return lax.all_to_all(x, axis, split_axis=0, concat_axis=0, tiled=True)


def body(value_branch, key_branch, gate_branch, skip_gain, spectra):
    core = (lax.axis_index("ctx") & 1)[None]
    packed = call(pack_kernel, ((N_CHAN, 48, LANES), BF16), [(N_CHAN, 48, LANES)], key_branch, value_branch)
    blocks = call(
        spectra_kernel,
        ((2 * GROUP, ROWS, LANES), BF16),
        [(2 * LANES, ROWS)],
        spectra.reshape(2, GROUP, ROWS, LANES),
    )
    gathered = exchange(packed, "chan")
    sent = call(fan_out_kernel, ((N_CTX, 2 * ROWS, LANES), BF16), [(N_CHAN * 48, LANES)], gathered, blocks)
    received = exchange(sent, "ctx")
    parts = exchange(apply_filter(core, received), "ctx")
    joined = call(join_kernel, ((N_CHAN, 48, LANES), BF16), [(N_CHAN * 48, LANES)], parts)
    tokens = exchange(joined, "chan")
    return call(
        gate_kernel,
        ((CHANNELS, TOKENS), BF16),
        [(N_CHAN, 48, LANES), (CHANNELS, TOKENS)],
        tokens,
        key_branch,
        value_branch,
        gate_branch,
        skip_gain[:, None],
    )


def solution(mesh):
    in_specs = (
        P(None, ("ctx", "chan")),
        P(None, ("ctx", "chan")),
        P(None, ("ctx", "chan")),
        P(),
        P(None, "chan", "ctx", None),
    )
    out_specs = P(None, ("ctx", "chan"))
    return jax.shard_map(body, mesh=mesh, in_specs=in_specs, out_specs=out_specs, check_vma=False)
```

time: 110 us -> 103 us (0.936)
  waiting for transfers between devices: 54.2 us -> 46 us
  local copies, waits for them, and re-layouts: 4.06 us -> 5.18 us
    all_to_all x3, waiting for transfers between devices: 54.2 us -> 46 us  [exchange(): return lax.all_to_all(x, axis, split_axis=0, concat_axis=0, tiled=True)]
    squeeze x0 -> x1, local copies, waits for them, and re-layouts: none -> 1.3 us  [apply_filter(): block = lax.dynamic_index_in_dim(block, core[0], 0, keepdims=False)]
    unnamed x24 -> x20, local copies, waits for them, and re-layouts: 3.94 us -> 3.76 us
  transfers between devices with their start and end apart: 3 -> 3, of which waited for: 3 -> 3; matrix products, arithmetic and copies ran while one was open for 0% -> 1% of each run, Pallas kernels for 0% -> 1%
where the time goes in v6:
time: 103 us
  waiting for transfers between devices  46 us (45%)
  starting transfers between devices  28.2 us (27%)
  blocking collectives  15.1 us (15%)
  Pallas kernels  8.22 us (8%)
  local copies, waits for them, and re-layouts  5.18 us (5%)
    all_to_all x3, waiting for transfers between devices, exchange(): return lax.all_to_all(x, axis, split_axis=0, concat_axis=0, tiled=True)  46 us
    all_to_all x3, starting transfers between devices, exchange(): return lax.all_to_all(x, axis, split_axis=0, concat_axis=0, tiled=True)  28.2 us
    all_to_all x1, blocking collectives, exchange(): return lax.all_to_all(x, axis, split_axis=0, concat_axis=0, tiled=True)  15.1 us
    pallas_call x6, Pallas kernels, call(): pl.pallas_call(kernel, out_shape=jax.ShapeDtypeStruct(*out_shape), in_spe...  8.22 us
    unnamed x20, local copies, waits for them, and re-layouts  3.76 us
  transfers between devices with their start and end apart: 3, of which 3 were waited for; matrix products, arithmetic and copies ran while one was open for 1% of the time, Pallas kernels for 1%

profile of v6, /device:TPU:32, one launch (start us, length us, event | category | flops | bytes accessed | tf_op | source)
XLA Modules:
  0.0 102.8 jit_solution(14055621997755629244)
XLA Ops:
  0.0 0.0 copy-start.2
  0.0 0.9 copy-done.2
  0.9 0.0 copy-start.4
  0.9 0.9 copy-done.4
  1.9 0.7 shard_map.91
  2.6 15.2 %all-to-all-start = ((bf16[16,48,128]{2,1,0:T(8,128)(2,1)}), bf16[16,48,128]{2,1,0:T(8,128)(2,1)S(1)}, u32[]{:S(2)}, u32[]{:S(2)}) async-start(bf16[16,48,128]{2,1,0:T(8,128)(2,1)} %shard_map.91), calls=%async_computation | async-start | bytes 393216 | tf_op jit(solution)/shard_map/all_to_all | solution.py:294
  17.8 0.0 copy-start
  17.8 1.1 %copy-done = f32[2,12,1,8192]{3,2,1,0:T(1,128)S(1)} copy-done((f32[2,12,1,8192]{3,2,1,0:T(1,128)S(1)}, f32[2,12,1,8192]{3,2,1,0:T(1,128)}, u32[]{:S(2)}) %copy-start) | copy-done | bytes 786456
  18.9 0.6 shard_map.92.blocks_ref
  19.6 14.0 %all-to-all-done.in_ref = bf16[16,48,128]{2,1,0:T(8,128)(2,1)S(1)} async-done(((bf16[16,48,128]{2,1,0:T(8,128)(2,1)}), bf16[16,48,128]{2,1,0:T(8,128)(2,1)S(1)}, u32[]{:S(2)}, u32[]{:S(2)}) %all-to-all-start) | async-done | bytes 196640 | tf_op jit(solution)/shard_map/all_to_all | solution.py:294
  33.6 1.1 %shard_map.93 = bf16[32,128,128]{2,1,0:T(8,128)(2,1)} custom-call(bf16[16,48,128]{2,1,0:T(8,128)(2,1)S(1)} %all-to-all-done.in_ref, bf16[24,64,128]{2,1,0:T(8,128)(2,1)S(1)} %shard_map.92.blocks_ref), custom_call_target="tpu_custom_call" | custom-call | tf_op jit(solution)/shard_map/pallas_call | solution.py:267
  34.8 0.0 copy-start.1
  34.8 0.0 copy-start.7
  34.8 7.5 %all-to-all-start.1 = ((bf16[32,128,128]{2,1,0:T(8,128)(2,1)}), bf16[32,128,128]{2,1,0:T(8,128)(2,1)S(1)}, u32[]{:S(2)}, u32[]{:S(2)}) async-start(bf16[32,128,128]{2,1,0:T(8,128)(2,1)} %shard_map.93), calls=%async_computation.1 | async-start | bytes 2097152 | tf_op jit(solution)/shard_map/all_to_all | solution.py:294
  42.2 1.3 %dynamic-slice_bitcast_fusion.block_ref = f32[2,32,32,128]{3,2,1,0:T(8,128)S(1)} fusion(f32[2,2,32,32,128]{4,3,2,1,0:T(8,128)} %constant.22.clone, s32[]{:T(128)S(6)} %select_n.4), kind=kLoop, calls=%fused_computation | loop fusion | bytes 2097156 | tf_op jit(solution)/shard_map/jit(dynamic_index_in_dim)/squeeze | solution.py:280
  43.5 16.0 %all-to-all-done.1.in_ref = bf16[32,128,128]{2,1,0:T(8,128)(2,1)S(1)} async-done(((bf16[32,128,128]{2,1,0:T(8,128)(2,1)}), bf16[32,128,128]{2,1,0:T(8,128)(2,1)S(1)}, u32[]{:S(2)}, u32[]{:S(2)}) %all-to-all-start.1) | async-done | bytes 1048608 | tf_op jit(solution)/shard_map/all_to_all | solution.py:294
  59.6 0.0 copy-done.1
  59.6 0.0 copy-done.7
  59.6 0.0 copy-start.8
  59.6 0.8 copy-done.8
  60.3 0.0 copy-start.9
  60.3 0.0 copy-start.3
  60.3 0.0 copy-start.5
  60.3 0.0 copy-start.6
  60.3 4.1 %shard_map.94 = bf16[32,64,128]{2,1,0:T(8,128)(2,1)S(1)} custom-call(s32[1]{0:T(128)} %bitcast.core_ref, bf16[32,128,128]{2,1,0:T(8,128)(2,1)S(1)} %all-to-all-done.1.in_ref, f32[2,32,32,128]{3,2,1,0:T(8,128)S(1)} %dynamic-slice_bitcast_fusion.block_ref, f32[2,32,128]{2,1,0:T(8,128)S(1)} %copy-done.8, bf16[2,64,192]{2,1,0:T(8,128)(2,1)S(1)} %copy-done.7, ...), custom_call_target="tpu_custom_call" | custom-call | tf_op jit(solution)/shard_map/pallas_call | solution.py:267
  64.4 15.1 %all_to_all.20.in_ref = bf16[32,64,128]{2,1,0:T(8,128)(2,1)S(1)} all-to-all(bf16[32,64,128]{2,1,0:T(8,128)(2,1)S(1)} %shard_map.94), channel_id=1, replica_groups=mesh['ctx'=32,'chan'=16] {'ctx'}, dimensions={0} | all-to-all | bytes 1048576 | tf_op jit(solution)/shard_map/all_to_all | solution.py:294
  79.5 0.8 shard_map.95
  80.3 5.5 %all-to-all-start.3 = ((bf16[16,48,128]{2,1,0:T(8,128)(2,1)}), bf16[16,48,128]{2,1,0:T(8,128)(2,1)S(1)}, u32[]{:S(2)}, u32[]{:S(2)}) async-start(bf16[16,48,128]{2,1,0:T(8,128)(2,1)} %shard_map.95), calls=%async_computation.3 | async-start | bytes 393216 | tf_op jit(solution)/shard_map/all_to_all | solution.py:294
  85.8 0.0 copy-done.9
  85.9 0.1 copy.10.skip_ref
  86.0 16.0 %all-to-all-done.3.conv_ref = bf16[16,48,128]{2,1,0:T(8,128)(2,1)S(1)} async-done(((bf16[16,48,128]{2,1,0:T(8,128)(2,1)}), bf16[16,48,128]{2,1,0:T(8,128)(2,1)S(1)}, u32[]{:S(2)}, u32[]{:S(2)}) %all-to-all-start.3) | async-done | bytes 196640 | tf_op jit(solution)/shard_map/all_to_all | solution.py:294
  102.0 0.0 copy-done.3
  102.0 0.0 copy-done.5
  102.0 0.0 copy-done.6
  102.0 0.9 shard_map.96
Async XLA Ops:
  0.0 0.9 copy-start.2
  0.9 0.9 copy-start.4
  2.6 31.0 %all-to-all-start = ((bf16[16,48,128]{2,1,0:T(8,128)(2,1)}), bf16[16,48,128]{2,1,0:T(8,128)(2,1)S(1)}, u32[]{:S(2)}, u32[]{:S(2)}) async-start(bf16[16,48,128]{2,1,0:T(8,128)(2,1)} %shard_map.91), calls=%async_computation | async-start | bytes 393216 | tf_op jit(solution)/shard_map/all_to_all | solution.py:294
  17.8 1.1 %copy-start = (f32[2,12,1,8192]{3,2,1,0:T(1,128)S(1)}, f32[2,12,1,8192]{3,2,1,0:T(1,128)}, u32[]{:S(2)}) copy-start(f32[2,12,1,8192]{3,2,1,0:T(1,128)} %param.13) | copy-start | bytes 2359300
  34.8 24.8 %copy-start.1 = (bf16[2,768,256]{2,1,0:T(8,128)(2,1)S(1)}, bf16[2,768,256]{2,1,0:T(8,128)(2,1)}, u32[]{:S(2)}) copy-start(bf16[2,768,256]{2,1,0:T(8,128)(2,1)} %constant.25.clone.lane_matrix_ref) | copy-start | bytes 2359300
  34.8 24.8 %copy-start.7 = (bf16[2,64,192]{2,1,0:T(8,128)(2,1)S(1)}, bf16[2,64,192]{2,1,0:T(8,128)(2,1)}, u32[]{:S(2)}) copy-start(bf16[2,64,192]{2,1,0:T(8,128)(2,1)} %constant.24.clone.row_matrix_ref) | copy-start | bytes 147460
  34.8 24.8 %all-to-all-start.1 = ((bf16[32,128,128]{2,1,0:T(8,128)(2,1)}), bf16[32,128,128]{2,1,0:T(8,128)(2,1)S(1)}, u32[]{:S(2)}, u32[]{:S(2)}) async-start(bf16[32,128,128]{2,1,0:T(8,128)(2,1)} %shard_map.93), calls=%async_computation.1 | async-start | bytes 2097152 | tf_op jit(solution)/shard_map/all_to_all | solution.py:294
  59.6 0.8 copy-start.8
  60.3 25.5 %copy-start.9 = (f32[192]{0:T(256)S(1)}, f32[192]{0:T(256)}, u32[]{:S(2)}) copy-start(f32[192]{0:T(256)} %param.12) | copy-start | bytes 2308
  60.3 41.6 %copy-start.3 = (bf16[192,512]{1,0:T(8,128)(2,1)S(1)}, bf16[192,512]{1,0:T(8,128)(2,1)}, u32[]{:S(2)}) copy-start(bf16[192,512]{1,0:T(8,128)(2,1)} %key_ref.3) | copy-start | bytes 589828
  60.3 41.6 %copy-start.5 = (bf16[192,512]{1,0:T(8,128)(2,1)S(1)}, bf16[192,512]{1,0:T(8,128)(2,1)}, u32[]{:S(2)}) copy-start(bf16[192,512]{1,0:T(8,128)(2,1)} %value_ref.3) | copy-start | bytes 589828
  60.3 41.6 %copy-start.6 = (bf16[192,512]{1,0:T(8,128)(2,1)S(1)}, bf16[192,512]{1,0:T(8,128)(2,1)}, u32[]{:S(2)}) copy-start(bf16[192,512]{1,0:T(8,128)(2,1)} %gate_ref.1) | copy-start | bytes 589828
  80.3 21.6 %all-to-all-start.3 = ((bf16[16,48,128]{2,1,0:T(8,128)(2,1)}), bf16[16,48,128]{2,1,0:T(8,128)(2,1)S(1)}, u32[]{:S(2)}, u32[]{:S(2)}) async-start(bf16[16,48,128]{2,1,0:T(8,128)(2,1)} %shard_map.95), calls=%async_computation.3 | async-start | bytes 393216 | tf_op jit(solution)/shard_map/all_to_all | solution.py:294

commit v7 on v6

--- a/solution.py
+++ b/solution.py
@@ -18,13 +18,13 @@
 LENGTH = SEQ * N_CTX
 LANES = 128
 HALF = 16
-CLASSES = 8
 ROWS = SEQ // LANES
 WORK = ROWS // 2
 CHIPS = [chip for chip in range(HALF) if (chip + chip // 4) % 4 != 3]
 F32 = jnp.float32
 BF16 = jnp.bfloat16
 VMEM_LIMIT = 32 * 1024 * 1024
+WHOLE_VMEM = 64 * 1024 * 1024 - 256 * 1024
 
 
 def rev5(number):
@@ -57,9 +57,22 @@
     ]
 
 
-def pack_kernel(key_ref, value_ref, out_ref, wide):
+def start(copy):
+    copy.start()
+    return copy
+
+
+def pack_kernel(key_far, value_far, out_far, key_ref, value_ref, wide, out_ref, arrived, left):
     low = lax.broadcasted_iota(jnp.int32, (8, LANES), 0) < 4
+    fetches, sends = [], []
+    for half in range(2):
+        rows = pl.ds(half * CHANNELS // 2, CHANNELS // 2)
+        for index, (far, near) in enumerate(((key_far, key_ref), (value_far, value_ref))):
+            fetches.append(start(pltpu.make_async_copy(far.at[rows], near.at[rows], arrived.at[half, index])))
     for block in range(CHANNELS // 16):
+        if block % 6 == 0:
+            fetches[block // 3].wait()
+            fetches[block // 3 + 1].wait()
         rows = slice(16 * block, 16 * block + 16)
         carried = (key_ref[rows, :].astype(F32) * value_ref[rows, :].astype(F32)).astype(BF16).astype(F32)
         for part in range(2):
@@ -70,23 +83,30 @@
                 second = jnp.where(low, pltpu.roll(a, 4, 0), b)
                 for offset, piece in enumerate((first, second)):
                     quad = 4 * block + 2 * part + offset
-                    start = 24 * upper + 8 * (quad % 3)
-                    wide[quad // 3, start : start + 8, :] = piece
-    for target in range(N_CHAN):
-        out_ref[target] = wide[target].astype(BF16)
-
-
-def gate_kernel(conv_ref, key_ref, value_ref, gate_ref, skip_ref, out_ref, wide, flat):
+                    row = 24 * upper + 8 * (quad % 3)
+                    wide[quad // 3, row : row + 8, :] = piece
+        if block % 6 == 5:
+            first = N_CHAN // 2 * (block // 6)
+            for target in range(first, first + N_CHAN // 2):
+                out_ref[target] = wide[target].astype(BF16)
+            targets = pl.ds(first, N_CHAN // 2)
+            sends.append(start(pltpu.make_async_copy(out_ref.at[targets], out_far.at[targets], left.at[block // 6])))
+    for send in sends:
+        send.wait()
+
+
+def gate_kernel(conv_ref, key_ref, value_ref, gate_ref, skip_ref, out_far, wide, flat, out_ref, left):
     low = lax.broadcasted_iota(jnp.int32, (8, LANES), 0) < 4
-    for source in range(N_CHAN):
-        wide[source] = conv_ref[source].astype(F32)
+    sends = []
     for block in range(CHANNELS // 8):
         for upper in range(2):
             pieces = []
             for offset in range(2):
                 quad = 2 * block + offset
-                start = 24 * upper + 8 * (quad % 3)
-                pieces.append(wide[quad // 3, start : start + 8, :])
+                row = 24 * upper + 8 * (quad % 3)
+                if row == 0:
+                    wide[quad // 3] = conv_ref[quad // 3].astype(F32)
+                pieces.append(wide[quad // 3, row : row + 8, :])
             first, second = pieces
             flat[8 * block : 8 * block + 8, 256 * upper : 256 * upper + 128] = jnp.where(
                 low, first, pltpu.roll(second, 4, 0)
@@ -94,27 +114,39 @@
             flat[8 * block : 8 * block + 8, 256 * upper + 128 : 256 * upper + 256] = jnp.where(
                 low, pltpu.roll(first, 4, 0), second
             )
-    for block in range(CHANNELS // 16):
-        rows = slice(16 * block, 16 * block + 16)
-        carried = (key_ref[rows, :].astype(F32) * value_ref[rows, :].astype(F32)).astype(BF16).astype(F32)
-        total = flat[rows, :] + skip_ref[rows, :] * carried
-        out_ref[rows, :] = (gate_ref[rows, :].astype(F32) * total).astype(BF16)
-
-
-def fan_out_kernel(in_ref, blocks_ref, out_ref, wide):
+        if block % 2 == 1:
+            rows = slice(8 * block - 8, 8 * block + 8)
+            carried = (key_ref[rows, :].astype(F32) * value_ref[rows, :].astype(F32)).astype(BF16).astype(F32)
+            total = flat[rows, :] + skip_ref[rows, :] * carried
+            out_ref[rows, :] = (gate_ref[rows, :].astype(F32) * total).astype(BF16)
+        if block % 6 == 5:
+            rows = pl.ds(8 * block - 40, 48)
+            sends.append(start(pltpu.make_async_copy(out_ref.at[rows], out_far.at[rows], left.at[block // 6])))
+    for send in sends:
+        send.wait()
+
+
+def fan_out_kernel(in_ref, blocks_ref, out_far, wide, out_ref, left):
     for source in range(N_CHAN):
         wide[48 * source : 48 * source + 48, :] = in_ref[source].astype(F32)
-    for channel, chip in enumerate(CHIPS):
-        first = 8 * (channel // 4) + channel % 4
-        pieces = [wide[pl.ds(first + 4 * quarter, ROWS // 2, stride=24), :] for quarter in range(2)]
-        series = jnp.concatenate(pieces, axis=0).astype(BF16)
-        for core in range(2):
-            out_ref[2 * chip + core, 0:ROWS, :] = series
-            out_ref[2 * chip + core, ROWS : 2 * ROWS, :] = blocks_ref[2 * channel + core]
+    sends = []
     for chip in range(HALF):
-        if chip not in CHIPS:
+        if chip in CHIPS:
+            channel = CHIPS.index(chip)
+            first = 8 * (channel // 4) + channel % 4
+            pieces = [wide[pl.ds(first + 4 * quarter, ROWS // 2, stride=24), :] for quarter in range(2)]
+            series = jnp.concatenate(pieces, axis=0).astype(BF16)
+            for core in range(2):
+                out_ref[2 * chip + core, 0:ROWS, :] = series
+                out_ref[2 * chip + core, ROWS : 2 * ROWS, :] = blocks_ref[2 * channel + core]
+        else:
             for core in range(2):
                 out_ref[2 * chip + core] = jnp.zeros((2 * ROWS, LANES), BF16)
+        if chip % 4 == 3:
+            targets = pl.ds(2 * chip - 6, 8)
+            sends.append(start(pltpu.make_async_copy(out_ref.at[targets], out_far.at[targets], left.at[chip // 4])))
+    for send in sends:
+        send.wait()
 
 
 def join_kernel(in_ref, out_ref, wide):
@@ -151,7 +183,7 @@
     return jnp.dot(a, b, preferred_element_type=F32)
 
 
-def filter_kernel(core_ref, in_ref, block_ref, lane_ref, row_matrix_ref, lane_matrix_ref, out_ref, real, pair):
+def filter_kernel(core_ref, in_ref, block_ref, row_matrix_ref, lane_matrix_ref, out_ref, real, pair):
     sign = jnp.where(core_ref[0] == 0, 1.0, -1.0).astype(F32)
     for index in range(N_CTX):
         real[index] = in_ref[index, 0:ROWS, :].astype(F32)
@@ -174,33 +206,31 @@
             columns = slice(LANES * residue, LANES * residue + LANES)
             pair[row : row + 8, columns] = term[0]
             pair[WORK + row : WORK + row + 8, columns] = term[1]
-    lane_re, lane_im = lane_ref[0], lane_ref[1]
-    for first in range(0, N_CTX, CLASSES):
-        columns = slice(LANES * first, LANES * (first + CLASSES))
-        high, low = split(pair[:, columns])
-        mixed = dot(row_matrix_ref[0], jnp.concatenate([high, low, high], axis=0))
-        turned = []
-        for index in range(CLASSES):
-            lanes = slice(LANES * index, LANES * index + LANES)
-            term = c_mul((mixed[:WORK, lanes], mixed[WORK:, lanes]), lane_re, lane_im)
-            turned.append(jnp.concatenate(term, axis=1))
-        high, low = split(jnp.concatenate(turned, axis=0))
-        spectrum = dot(jnp.concatenate([high, low, high], axis=1), lane_matrix_ref[0])
-        shaped = []
-        for index in range(CLASSES):
-            rows = slice(WORK * index, WORK * index + WORK)
-            response = in_ref[rev5(first + index), ROWS : 2 * ROWS, :].astype(F32)
-            term = c_mul((spectrum[rows, :LANES], spectrum[rows, LANES:]), response[:WORK], response[WORK:])
-            shaped.append(jnp.concatenate(term, axis=1))
-        high, low = split(jnp.concatenate(shaped, axis=0))
-        mixed = dot(jnp.concatenate([high, low, high], axis=1), lane_matrix_ref[1])
-        turned = []
-        for index in range(CLASSES):
-            rows = slice(WORK * index, WORK * index + WORK)
-            term = c_mul((mixed[rows, :LANES], mixed[rows, LANES:]), lane_re, -lane_im)
-            turned.append(jnp.concatenate(term, axis=0))
-        high, low = split(jnp.concatenate(turned, axis=1))
-        pair[:, columns] = dot(row_matrix_ref[1], jnp.concatenate([high, low, high], axis=0))
+    lane_re, lane_im = block_ref[0, N_CTX], block_ref[1, N_CTX]
+    high, low = split(pair[...])
+    mixed = dot(row_matrix_ref[0], jnp.concatenate([high, low, high], axis=0))
+    turned = []
+    for index in range(N_CTX):
+        lanes = slice(LANES * index, LANES * index + LANES)
+        term = c_mul((mixed[:WORK, lanes], mixed[WORK:, lanes]), lane_re, lane_im)
+        turned.append(jnp.concatenate(term, axis=1))
+    high, low = split(jnp.concatenate(turned, axis=0))
+    spectrum = dot(jnp.concatenate([high, low, high], axis=1), lane_matrix_ref[0])
+    shaped = []
+    for index in range(N_CTX):
+        rows = slice(WORK * index, WORK * index + WORK)
+        response = in_ref[rev5(index), ROWS : 2 * ROWS, :].astype(F32)
+        term = c_mul((spectrum[rows, :LANES], spectrum[rows, LANES:]), response[:WORK], response[WORK:])
+        shaped.append(jnp.concatenate(term, axis=1))
+    high, low = split(jnp.concatenate(shaped, axis=0))
+    mixed = dot(jnp.concatenate([high, low, high], axis=1), lane_matrix_ref[1])
+    turned = []
+    for index in range(N_CTX):
+        rows = slice(WORK * index, WORK * index + WORK)
+        term = c_mul((mixed[rows, :LANES], mixed[rows, LANES:]), lane_re, -lane_im)
+        turned.append(jnp.concatenate(term, axis=0))
+    high, low = split(jnp.concatenate(turned, axis=1))
+    pair[...] = dot(row_matrix_ref[1], jnp.concatenate([high, low, high], axis=0))
     for group in range(WORK // 8):
         early, late, row = places(group)
         rows = slice(row, row + 8)
@@ -242,6 +272,7 @@
     frequency = (np.arange(N_CTX)[None, :] + 32 * np.arange(2)[:, None])[:, :, None, None]
     block = np.stack(phases(offset * frequency, LENGTH), axis=1).astype(np.float32)
     lane_phase = np.stack(phases(row[:, None] * lane[None, :], 4096)).astype(np.float32)
+    block = np.concatenate([block, np.stack([lane_phase] * 2)[:, :, None]], axis=2)
 
     def parts(matrix):
         high = matrix.astype(ml_dtypes.bfloat16)
@@ -260,18 +291,19 @@
     for matrix in (forward, inverse):
         high, low = parts(matrix)
         lane_matrices.append(np.concatenate([high, high, low], axis=0))
-    return block, lane_phase, np.stack(row_matrices), np.stack(lane_matrices)
-
-
-def call(kernel, out_shape, scratch, *operands, scalars=0):
+    return block, np.stack(row_matrices), np.stack(lane_matrices)
+
+
+def call(kernel, out_shape, scratch, *operands, scalars=0, far_in=False, far_out=False, limit=VMEM_LIMIT):
+    near_in = pltpu.HBM if far_in else pltpu.VMEM
     return pl.pallas_call(
         kernel,
         out_shape=jax.ShapeDtypeStruct(*out_shape),
         in_specs=[pl.BlockSpec(memory_space=pltpu.SMEM)] * scalars
-        + [pl.BlockSpec(memory_space=pltpu.VMEM)] * (len(operands) - scalars),
-        out_specs=pl.BlockSpec(memory_space=pltpu.VMEM),
-        scratch_shapes=[pltpu.VMEM(shape, F32) for shape in scratch],
-        compiler_params=pltpu.CompilerParams(vmem_limit_bytes=VMEM_LIMIT),
+        + [pl.BlockSpec(memory_space=near_in)] * (len(operands) - scalars),
+        out_specs=pl.BlockSpec(memory_space=pltpu.HBM if far_out else pltpu.VMEM),
+        scratch_shapes=[pltpu.VMEM(shape, F32) if isinstance(shape, tuple) else shape for shape in scratch],
+        compiler_params=pltpu.CompilerParams(vmem_limit_bytes=limit),
     )(*operands)
 
 
@@ -296,7 +328,25 @@
 
 def body(value_branch, key_branch, gate_branch, skip_gain, spectra):
     core = (lax.axis_index("ctx") & 1)[None]
-    packed = call(pack_kernel, ((N_CHAN, 48, LANES), BF16), [(N_CHAN, 48, LANES)], key_branch, value_branch)
+    tokens_shape, message = (CHANNELS, TOKENS), (N_CHAN, 48, LANES)
+    semaphores = pltpu.SemaphoreType.DMA
+    packed = call(
+        pack_kernel,
+        (message, BF16),
+        [
+            pltpu.VMEM(tokens_shape, BF16),
+            pltpu.VMEM(tokens_shape, BF16),
+            message,
+            pltpu.VMEM(message, BF16),
+            semaphores((2, 2)),
+            semaphores((2,)),
+        ],
+        key_branch,
+        value_branch,
+        far_in=True,
+        far_out=True,
+        limit=WHOLE_VMEM,
+    )
     blocks = call(
         spectra_kernel,
         ((2 * GROUP, ROWS, LANES), BF16),
@@ -304,20 +354,29 @@
         spectra.reshape(2, GROUP, ROWS, LANES),
     )
     gathered = exchange(packed, "chan")
-    sent = call(fan_out_kernel, ((N_CTX, 2 * ROWS, LANES), BF16), [(N_CHAN * 48, LANES)], gathered, blocks)
+    blocks_shape = (N_CTX, 2 * ROWS, LANES)
+    sent = call(
+        fan_out_kernel,
+        (blocks_shape, BF16),
+        [(N_CHAN * 48, LANES), pltpu.VMEM(blocks_shape, BF16), semaphores((4,))],
+        gathered,
+        blocks,
+        far_out=True,
+    )
     received = exchange(sent, "ctx")
     parts = exchange(apply_filter(core, received), "ctx")
     joined = call(join_kernel, ((N_CHAN, 48, LANES), BF16), [(N_CHAN * 48, LANES)], parts)
     tokens = exchange(joined, "chan")
     return call(
         gate_kernel,
-        ((CHANNELS, TOKENS), BF16),
-        [(N_CHAN, 48, LANES), (CHANNELS, TOKENS)],
+        (tokens_shape, BF16),
+        [message, tokens_shape, pltpu.VMEM(tokens_shape, BF16), semaphores((4,))],
         tokens,
         key_branch,
         value_branch,
         gate_branch,
         skip_gain[:, None],
+        far_out=True,
     )
 
 

time: 103 us -> 102 us (level)
  local copies, waits for them, and re-layouts: 5.18 us -> 3.42 us
    unnamed x20 -> x14, local copies, waits for them, and re-layouts: 3.76 us -> 1.99 us
where the time goes in v7:
time: 102 us; the launch traced here: 101 us
  waiting for transfers between devices  46 us (45%)
  starting transfers between devices  28.2 us (28%)
  blocking collectives  15.1 us (15%)
  Pallas kernels  8.26 us (8%)
  local copies, waits for them, and re-layouts  3.42 us (3%)
    all_to_all x3, waiting for transfers between devices, exchange(): return lax.all_to_all(x, axis, split_axis=0, concat_axis=0, tiled=True)  46 us
    all_to_all x3, starting transfers between devices, exchange(): return lax.all_to_all(x, axis, split_axis=0, concat_axis=0, tiled=True)  28.2 us
    all_to_all x1, blocking collectives, exchange(): return lax.all_to_all(x, axis, split_axis=0, concat_axis=0, tiled=True)  15.1 us
    pallas_call x6, Pallas kernels, call(): pl.pallas_call(kernel, out_shape=jax.ShapeDtypeStruct(*out_shape), in_spe...  8.26 us
  transfers between devices with their start and end apart: 3, of which 3 were waited for; matrix products, arithmetic and copies ran while one was open for 1% of the time, Pallas kernels for 1%

profile of v7, /device:TPU:32, one launch (start us, length us, event | category | flops | bytes accessed | tf_op | source)
XLA Modules:
  0.0 101.1 jit_solution(16867432392684522473)
XLA Ops:
  0.0 1.8 %shard_map.82 = bf16[16,48,128]{2,1,0:T(8,128)(2,1)} custom-call(bf16[192,512]{1,0:T(8,128)(2,1)} %key_ref.1, bf16[192,512]{1,0:T(8,128)(2,1)} %value_ref.1), custom_call_target="tpu_custom_call" | custom-call | tf_op jit(solution)/shard_map/pallas_call | solution.py:299
  1.8 15.2 %all-to-all-start = ((bf16[16,48,128]{2,1,0:T(8,128)(2,1)}), bf16[16,48,128]{2,1,0:T(8,128)(2,1)S(1)}, u32[]{:S(2)}, u32[]{:S(2)}) async-start(bf16[16,48,128]{2,1,0:T(8,128)(2,1)} %shard_map.82), calls=%async_computation | async-start | bytes 393216 | tf_op jit(solution)/shard_map/all_to_all | solution.py:326
  17.0 0.0 copy-start
  17.0 1.1 %copy-done = f32[2,12,1,8192]{3,2,1,0:T(1,128)S(1)} copy-done((f32[2,12,1,8192]{3,2,1,0:T(1,128)S(1)}, f32[2,12,1,8192]{3,2,1,0:T(1,128)}, u32[]{:S(2)}) %copy-start) | copy-done | bytes 786456
  18.1 0.6 shard_map.83.blocks_ref
  18.8 14.0 %all-to-all-done.in_ref = bf16[16,48,128]{2,1,0:T(8,128)(2,1)S(1)} async-done(((bf16[16,48,128]{2,1,0:T(8,128)(2,1)}), bf16[16,48,128]{2,1,0:T(8,128)(2,1)S(1)}, u32[]{:S(2)}, u32[]{:S(2)}) %all-to-all-start) | async-done | bytes 196640 | tf_op jit(solution)/shard_map/all_to_all | solution.py:326
  32.8 1.1 %shard_map.84 = bf16[32,128,128]{2,1,0:T(8,128)(2,1)} custom-call(bf16[16,48,128]{2,1,0:T(8,128)(2,1)S(1)} %all-to-all-done.in_ref, bf16[24,64,128]{2,1,0:T(8,128)(2,1)S(1)} %shard_map.83.blocks_ref), custom_call_target="tpu_custom_call" | custom-call | tf_op jit(solution)/shard_map/pallas_call | solution.py:299
  33.9 0.0 copy-start.1
  33.9 7.5 %all-to-all-start.1 = ((bf16[32,128,128]{2,1,0:T(8,128)(2,1)}), bf16[32,128,128]{2,1,0:T(8,128)(2,1)S(1)}, u32[]{:S(2)}, u32[]{:S(2)}) async-start(bf16[32,128,128]{2,1,0:T(8,128)(2,1)} %shard_map.84), calls=%async_computation.1 | async-start | bytes 2097152 | tf_op jit(solution)/shard_map/all_to_all | solution.py:326
  41.4 1.3 %dynamic-slice_bitcast_fusion.block_ref = f32[2,33,32,128]{3,2,1,0:T(8,128)S(1)} fusion(f32[2,2,33,32,128]{4,3,2,1,0:T(8,128)} %constant.20.clone, s32[]{:T(128)S(6)} %select_n.4), kind=kLoop, calls=%fused_computation | loop fusion | bytes 2162692 | tf_op jit(solution)/shard_map/jit(dynamic_index_in_dim)/squeeze | solution.py:312
  42.7 16.0 %all-to-all-done.1.in_ref = bf16[32,128,128]{2,1,0:T(8,128)(2,1)S(1)} async-done(((bf16[32,128,128]{2,1,0:T(8,128)(2,1)}), bf16[32,128,128]{2,1,0:T(8,128)(2,1)S(1)}, u32[]{:S(2)}, u32[]{:S(2)}) %all-to-all-start.1) | async-done | bytes 1048608 | tf_op jit(solution)/shard_map/all_to_all | solution.py:326
  58.7 0.0 copy-done.1
  58.7 0.0 copy-start.5
  58.7 0.8 copy-done.5
  59.5 0.0 copy-start.6
  59.5 0.0 copy-start.2
  59.5 0.0 copy-start.3
  59.6 0.0 copy-start.4
  59.6 3.2 %shard_map.85 = bf16[32,64,128]{2,1,0:T(8,128)(2,1)S(1)} custom-call(s32[1]{0:T(128)} %bitcast.core_ref, bf16[32,128,128]{2,1,0:T(8,128)(2,1)S(1)} %all-to-all-done.1.in_ref, f32[2,33,32,128]{3,2,1,0:T(8,128)S(1)} %dynamic-slice_bitcast_fusion.block_ref, bf16[2,64,192]{2,1,0:T(8,128)(2,1)S(1)} %copy-done.5, bf16[2,768,256]{2,1,0:T(8,128)(2,1)S(1)} %copy-done.1), custom_call_target="tpu_custom_call" | custom-call | tf_op jit(solution)/shard_map/pallas_call | solution.py:299
  62.8 15.1 %all_to_all.20.in_ref = bf16[32,64,128]{2,1,0:T(8,128)(2,1)S(1)} all-to-all(bf16[32,64,128]{2,1,0:T(8,128)(2,1)S(1)} %shard_map.85), channel_id=1, replica_groups=mesh['ctx'=32,'chan'=16] {'ctx'}, dimensions={0} | all-to-all | bytes 1048576 | tf_op jit(solution)/shard_map/all_to_all | solution.py:326
  77.9 0.8 shard_map.86
  78.6 5.5 %all-to-all-start.3 = ((bf16[16,48,128]{2,1,0:T(8,128)(2,1)}), bf16[16,48,128]{2,1,0:T(8,128)(2,1)S(1)}, u32[]{:S(2)}, u32[]{:S(2)}) async-start(bf16[16,48,128]{2,1,0:T(8,128)(2,1)} %shard_map.86), calls=%async_computation.3 | async-start | bytes 393216 | tf_op jit(solution)/shard_map/all_to_all | solution.py:326
  84.2 0.0 copy-done.6
  84.2 0.1 copy.9.skip_ref
  84.3 16.0 %all-to-all-done.3.conv_ref = bf16[16,48,128]{2,1,0:T(8,128)(2,1)S(1)} async-done(((bf16[16,48,128]{2,1,0:T(8,128)(2,1)}), bf16[16,48,128]{2,1,0:T(8,128)(2,1)S(1)}, u32[]{:S(2)}, u32[]{:S(2)}) %all-to-all-start.3) | async-done | bytes 196640 | tf_op jit(solution)/shard_map/all_to_all | solution.py:326
  100.3 0.0 copy-done.2
  100.3 0.0 copy-done.3
  100.3 0.0 copy-done.4
  100.3 0.8 shard_map.87
Async XLA Ops:
  1.8 31.0 %all-to-all-start = ((bf16[16,48,128]{2,1,0:T(8,128)(2,1)}), bf16[16,48,128]{2,1,0:T(8,128)(2,1)S(1)}, u32[]{:S(2)}, u32[]{:S(2)}) async-start(bf16[16,48,128]{2,1,0:T(8,128)(2,1)} %shard_map.82), calls=%async_computation | async-start | bytes 393216 | tf_op jit(solution)/shard_map/all_to_all | solution.py:326
  17.0 1.1 %copy-start = (f32[2,12,1,8192]{3,2,1,0:T(1,128)S(1)}, f32[2,12,1,8192]{3,2,1,0:T(1,128)}, u32[]{:S(2)}) copy-start(f32[2,12,1,8192]{3,2,1,0:T(1,128)} %param.12) | copy-start | bytes 2359300
  33.9 24.8 %copy-start.1 = (bf16[2,768,256]{2,1,0:T(8,128)(2,1)S(1)}, bf16[2,768,256]{2,1,0:T(8,128)(2,1)}, u32[]{:S(2)}) copy-start(bf16[2,768,256]{2,1,0:T(8,128)(2,1)} %constant.22.clone.lane_matrix_ref) | copy-start | bytes 2359300
  33.9 24.8 %all-to-all-start.1 = ((bf16[32,128,128]{2,1,0:T(8,128)(2,1)}), bf16[32,128,128]{2,1,0:T(8,128)(2,1)S(1)}, u32[]{:S(2)}, u32[]{:S(2)}) async-start(bf16[32,128,128]{2,1,0:T(8,128)(2,1)} %shard_map.84), calls=%async_computation.1 | async-start | bytes 2097152 | tf_op jit(solution)/shard_map/all_to_all | solution.py:326
  58.7 0.8 copy-start.5
  59.5 24.6 %copy-start.6 = (f32[192]{0:T(256)S(1)}, f32[192]{0:T(256)}, u32[]{:S(2)}) copy-start(f32[192]{0:T(256)} %param.11) | copy-start | bytes 2308
  59.5 40.7 %copy-start.2 = (bf16[192,512]{1,0:T(8,128)(2,1)S(1)}, bf16[192,512]{1,0:T(8,128)(2,1)}, u32[]{:S(2)}) copy-start(bf16[192,512]{1,0:T(8,128)(2,1)} %key_ref.1) | copy-start | bytes 589828
  59.5 40.7 %copy-start.3 = (bf16[192,512]{1,0:T(8,128)(2,1)S(1)}, bf16[192,512]{1,0:T(8,128)(2,1)}, u32[]{:S(2)}) copy-start(bf16[192,512]{1,0:T(8,128)(2,1)} %value_ref.1) | copy-start | bytes 589828
  59.6 40.7 %copy-start.4 = (bf16[192,512]{1,0:T(8,128)(2,1)S(1)}, bf16[192,512]{1,0:T(8,128)(2,1)}, u32[]{:S(2)}) copy-start(bf16[192,512]{1,0:T(8,128)(2,1)} %gate_ref.1) | copy-start | bytes 589828
  78.6 21.6 %all-to-all-start.3 = ((bf16[16,48,128]{2,1,0:T(8,128)(2,1)}), bf16[16,48,128]{2,1,0:T(8,128)(2,1)S(1)}, u32[]{:S(2)}, u32[]{:S(2)}) async-start(bf16[16,48,128]{2,1,0:T(8,128)(2,1)} %shard_map.86), calls=%async_computation.3 | async-start | bytes 393216 | tf_op jit(solution)/shard_map/all_to_all | solution.py:326

commit v8 on v7

--- a/solution.py
+++ b/solution.py
@@ -183,7 +183,7 @@
     return jnp.dot(a, b, preferred_element_type=F32)
 
 
-def filter_kernel(core_ref, in_ref, block_ref, row_matrix_ref, lane_matrix_ref, out_ref, real, pair):
+def filter_kernel(core_ref, in_ref, block_ref, matrix_ref, out_ref, real, pair):
     sign = jnp.where(core_ref[0] == 0, 1.0, -1.0).astype(F32)
     for index in range(N_CTX):
         real[index] = in_ref[index, 0:ROWS, :].astype(F32)
@@ -208,14 +208,14 @@
             pair[WORK + row : WORK + row + 8, columns] = term[1]
     lane_re, lane_im = block_ref[0, N_CTX], block_ref[1, N_CTX]
     high, low = split(pair[...])
-    mixed = dot(row_matrix_ref[0], jnp.concatenate([high, low, high], axis=0))
+    mixed = dot(matrix_ref[0, 6 * LANES :, : 3 * ROWS], jnp.concatenate([high, low, high], axis=0))
     turned = []
     for index in range(N_CTX):
         lanes = slice(LANES * index, LANES * index + LANES)
         term = c_mul((mixed[:WORK, lanes], mixed[WORK:, lanes]), lane_re, lane_im)
         turned.append(jnp.concatenate(term, axis=1))
     high, low = split(jnp.concatenate(turned, axis=0))
-    spectrum = dot(jnp.concatenate([high, low, high], axis=1), lane_matrix_ref[0])
+    spectrum = dot(jnp.concatenate([high, low, high], axis=1), matrix_ref[0, : 6 * LANES, :])
     shaped = []
     for index in range(N_CTX):
         rows = slice(WORK * index, WORK * index + WORK)
@@ -223,14 +223,14 @@
         term = c_mul((spectrum[rows, :LANES], spectrum[rows, LANES:]), response[:WORK], response[WORK:])
         shaped.append(jnp.concatenate(term, axis=1))
     high, low = split(jnp.concatenate(shaped, axis=0))
-    mixed = dot(jnp.concatenate([high, low, high], axis=1), lane_matrix_ref[1])
+    mixed = dot(jnp.concatenate([high, low, high], axis=1), matrix_ref[1, : 6 * LANES, :])
     turned = []
     for index in range(N_CTX):
         rows = slice(WORK * index, WORK * index + WORK)
         term = c_mul((mixed[rows, :LANES], mixed[rows, LANES:]), lane_re, -lane_im)
         turned.append(jnp.concatenate(term, axis=0))
     high, low = split(jnp.concatenate(turned, axis=1))
-    pair[...] = dot(row_matrix_ref[1], jnp.concatenate([high, low, high], axis=0))
+    pair[...] = dot(matrix_ref[1, 6 * LANES :, : 3 * ROWS], jnp.concatenate([high, low, high], axis=0))
     for group in range(WORK // 8):
         early, late, row = places(group)
         rows = slice(row, row + 8)
@@ -291,7 +291,10 @@
     for matrix in (forward, inverse):
         high, low = parts(matrix)
         lane_matrices.append(np.concatenate([high, high, low], axis=0))
-    return block, np.stack(row_matrices), np.stack(lane_matrices)
+    matrices = np.zeros((2, 6 * LANES + ROWS, 2 * LANES), ml_dtypes.bfloat16)
+    matrices[:, : 6 * LANES] = np.stack(lane_matrices)
+    matrices[:, 6 * LANES :, : 3 * ROWS] = np.stack(row_matrices)
+    return block, matrices
 
 
 def call(kernel, out_shape, scratch, *operands, scalars=0, far_in=False, far_out=False, limit=VMEM_LIMIT):
@@ -308,7 +311,7 @@
 
 
 def apply_filter(core, received):
-    block, *others = (jnp.asarray(table) for table in tables())
+    block, matrices = (jnp.asarray(table) for table in tables())
     block = lax.dynamic_index_in_dim(block, core[0], 0, keepdims=False)
     return call(
         filter_kernel,
@@ -317,7 +320,7 @@
         core,
         received,
         block,
-        *others,
+        matrices,
         scalars=1,
     )
 

time: 102 us -> 101 us (level)
  no operation moved by 1% of the time
where the time goes in v8:
time: 101 us; the launch traced here: 100 us
  waiting for transfers between devices  46 us (46%)
  starting transfers between devices  28.2 us (28%)
  blocking collectives  15.2 us (15%)
  Pallas kernels  8.26 us (8%)
  local copies, waits for them, and re-layouts  2.58 us (3%)
    all_to_all x3, waiting for transfers between devices, exchange(): return lax.all_to_all(x, axis, split_axis=0, concat_axis=0, tiled=True)  46 us
    all_to_all x3, starting transfers between devices, exchange(): return lax.all_to_all(x, axis, split_axis=0, concat_axis=0, tiled=True)  28.2 us
    all_to_all x1, blocking collectives, exchange(): return lax.all_to_all(x, axis, split_axis=0, concat_axis=0, tiled=True)  15.2 us
    pallas_call x6, Pallas kernels, call(): pl.pallas_call(kernel, out_shape=jax.ShapeDtypeStruct(*out_shape), in_spe...  8.26 us
  transfers between devices with their start and end apart: 3, of which 3 were waited for; matrix products, arithmetic and copies ran while one was open for 1% of the time, Pallas kernels for 1%

profile of v8, /device:TPU:32, one launch (start us, length us, event | category | flops | bytes accessed | tf_op | source)
XLA Modules:
  0.0 100.4 jit_solution(5981398725289204148)
XLA Ops:
  0.0 1.8 %shard_map.73 = bf16[16,48,128]{2,1,0:T(8,128)(2,1)} custom-call(bf16[192,512]{1,0:T(8,128)(2,1)} %key_ref.1, bf16[192,512]{1,0:T(8,128)(2,1)} %value_ref.1), custom_call_target="tpu_custom_call" | custom-call | tf_op jit(solution)/shard_map/pallas_call | solution.py:302
  1.8 15.2 %all-to-all-start = ((bf16[16,48,128]{2,1,0:T(8,128)(2,1)}), bf16[16,48,128]{2,1,0:T(8,128)(2,1)S(1)}, u32[]{:S(2)}, u32[]{:S(2)}) async-start(bf16[16,48,128]{2,1,0:T(8,128)(2,1)} %shard_map.73), calls=%async_computation | async-start | bytes 393216 | tf_op jit(solution)/shard_map/all_to_all | solution.py:329
  17.0 0.0 copy-start.1
  17.0 1.1 %copy-done.1 = f32[2,12,1,8192]{3,2,1,0:T(1,128)S(1)} copy-done((f32[2,12,1,8192]{3,2,1,0:T(1,128)S(1)}, f32[2,12,1,8192]{3,2,1,0:T(1,128)}, u32[]{:S(2)}) %copy-start.1) | copy-done | bytes 786456
  18.1 0.6 shard_map.74.blocks_ref
  18.8 14.0 %all-to-all-done.in_ref = bf16[16,48,128]{2,1,0:T(8,128)(2,1)S(1)} async-done(((bf16[16,48,128]{2,1,0:T(8,128)(2,1)}), bf16[16,48,128]{2,1,0:T(8,128)(2,1)S(1)}, u32[]{:S(2)}, u32[]{:S(2)}) %all-to-all-start) | async-done | bytes 196640 | tf_op jit(solution)/shard_map/all_to_all | solution.py:329
  32.8 1.1 %shard_map.75 = bf16[32,128,128]{2,1,0:T(8,128)(2,1)} custom-call(bf16[16,48,128]{2,1,0:T(8,128)(2,1)S(1)} %all-to-all-done.in_ref, bf16[24,64,128]{2,1,0:T(8,128)(2,1)S(1)} %shard_map.74.blocks_ref), custom_call_target="tpu_custom_call" | custom-call | tf_op jit(solution)/shard_map/pallas_call | solution.py:302
  33.9 0.0 copy-start
  33.9 7.5 %all-to-all-start.1 = ((bf16[32,128,128]{2,1,0:T(8,128)(2,1)}), bf16[32,128,128]{2,1,0:T(8,128)(2,1)S(1)}, u32[]{:S(2)}, u32[]{:S(2)}) async-start(bf16[32,128,128]{2,1,0:T(8,128)(2,1)} %shard_map.75), calls=%async_computation.1 | async-start | bytes 2097152 | tf_op jit(solution)/shard_map/all_to_all | solution.py:329
  41.4 1.3 %dynamic-slice_bitcast_fusion.block_ref = f32[2,33,32,128]{3,2,1,0:T(8,128)S(1)} fusion(f32[2,2,33,32,128]{4,3,2,1,0:T(8,128)} %constant.18.clone, s32[]{:T(128)S(6)} %select_n.4), kind=kLoop, calls=%fused_computation | loop fusion | bytes 2162692 | tf_op jit(solution)/shard_map/jit(dynamic_index_in_dim)/squeeze | solution.py:315
  42.7 16.0 %all-to-all-done.1.in_ref = bf16[32,128,128]{2,1,0:T(8,128)(2,1)S(1)} async-done(((bf16[32,128,128]{2,1,0:T(8,128)(2,1)}), bf16[32,128,128]{2,1,0:T(8,128)(2,1)S(1)}, u32[]{:S(2)}, u32[]{:S(2)}) %all-to-all-start.1) | async-done | bytes 1048608 | tf_op jit(solution)/shard_map/all_to_all | solution.py:329
  58.7 0.0 copy-done
  58.7 0.0 copy-start.5
  58.7 0.0 copy-start.2
  58.7 0.0 copy-start.3
  58.7 3.2 %shard_map.76 = bf16[32,64,128]{2,1,0:T(8,128)(2,1)S(1)} custom-call(s32[1]{0:T(128)} %bitcast.core_ref, bf16[32,128,128]{2,1,0:T(8,128)(2,1)S(1)} %all-to-all-done.1.in_ref, f32[2,33,32,128]{3,2,1,0:T(8,128)S(1)} %dynamic-slice_bitcast_fusion.block_ref, bf16[2,832,256]{2,1,0:T(8,128)(2,1)S(1)} %copy-done), custom_call_target="tpu_custom_call" | custom-call | tf_op jit(solution)/shard_map/pallas_call | solution.py:302
  61.9 0.0 copy-start.4
  61.9 15.2 %all_to_all.20.in_ref = bf16[32,64,128]{2,1,0:T(8,128)(2,1)S(1)} all-to-all(bf16[32,64,128]{2,1,0:T(8,128)(2,1)S(1)} %shard_map.76), channel_id=1, replica_groups=mesh['ctx'=32,'chan'=16] {'ctx'}, dimensions={0} | all-to-all | bytes 1048576 | tf_op jit(solution)/shard_map/all_to_all | solution.py:329
  77.2 0.8 shard_map.77
  77.9 5.5 %all-to-all-start.3 = ((bf16[16,48,128]{2,1,0:T(8,128)(2,1)}), bf16[16,48,128]{2,1,0:T(8,128)(2,1)S(1)}, u32[]{:S(2)}, u32[]{:S(2)}) async-start(bf16[16,48,128]{2,1,0:T(8,128)(2,1)} %shard_map.77), calls=%async_computation.3 | async-start | bytes 393216 | tf_op jit(solution)/shard_map/all_to_all | solution.py:329
  83.5 0.0 copy-done.5
  83.5 0.1 copy.8.skip_ref
  83.6 16.0 %all-to-all-done.3.conv_ref = bf16[16,48,128]{2,1,0:T(8,128)(2,1)S(1)} async-done(((bf16[16,48,128]{2,1,0:T(8,128)(2,1)}), bf16[16,48,128]{2,1,0:T(8,128)(2,1)S(1)}, u32[]{:S(2)}, u32[]{:S(2)}) %all-to-all-start.3) | async-done | bytes 196640 | tf_op jit(solution)/shard_map/all_to_all | solution.py:329
  99.6 0.0 copy-done.2
  99.6 0.0 copy-done.3
  99.6 0.0 copy-done.4
  99.6 0.8 shard_map.78
Async XLA Ops:
  1.8 31.0 %all-to-all-start = ((bf16[16,48,128]{2,1,0:T(8,128)(2,1)}), bf16[16,48,128]{2,1,0:T(8,128)(2,1)S(1)}, u32[]{:S(2)}, u32[]{:S(2)}) async-start(bf16[16,48,128]{2,1,0:T(8,128)(2,1)} %shard_map.73), calls=%async_computation | async-start | bytes 393216 | tf_op jit(solution)/shard_map/all_to_all | solution.py:329
  17.0 1.1 %copy-start.1 = (f32[2,12,1,8192]{3,2,1,0:T(1,128)S(1)}, f32[2,12,1,8192]{3,2,1,0:T(1,128)}, u32[]{:S(2)}) copy-start(f32[2,12,1,8192]{3,2,1,0:T(1,128)} %param.11) | copy-start | bytes 2359300
  33.9 24.8 %copy-start = (bf16[2,832,256]{2,1,0:T(8,128)(2,1)S(1)}, bf16[2,832,256]{2,1,0:T(8,128)(2,1)}, u32[]{:S(2)}) copy-start(bf16[2,832,256]{2,1,0:T(8,128)(2,1)} %constant.19.clone.matrix_ref) | copy-start | bytes 2555908
  33.9 24.8 %all-to-all-start.1 = ((bf16[32,128,128]{2,1,0:T(8,128)(2,1)}), bf16[32,128,128]{2,1,0:T(8,128)(2,1)S(1)}, u32[]{:S(2)}, u32[]{:S(2)}) async-start(bf16[32,128,128]{2,1,0:T(8,128)(2,1)} %shard_map.75), calls=%async_computation.1 | async-start | bytes 2097152 | tf_op jit(solution)/shard_map/all_to_all | solution.py:329
  58.7 24.8 %copy-start.5 = (f32[192]{0:T(256)S(1)}, f32[192]{0:T(256)}, u32[]{:S(2)}) copy-start(f32[192]{0:T(256)} %param.10) | copy-start | bytes 2308
  58.7 40.9 %copy-start.2 = (bf16[192,512]{1,0:T(8,128)(2,1)S(1)}, bf16[192,512]{1,0:T(8,128)(2,1)}, u32[]{:S(2)}) copy-start(bf16[192,512]{1,0:T(8,128)(2,1)} %key_ref.1) | copy-start | bytes 589828
  58.7 40.9 %copy-start.3 = (bf16[192,512]{1,0:T(8,128)(2,1)S(1)}, bf16[192,512]{1,0:T(8,128)(2,1)}, u32[]{:S(2)}) copy-start(bf16[192,512]{1,0:T(8,128)(2,1)} %value_ref.1) | copy-start | bytes 589828
  61.9 37.7 %copy-start.4 = (bf16[192,512]{1,0:T(8,128)(2,1)S(1)}, bf16[192,512]{1,0:T(8,128)(2,1)}, u32[]{:S(2)}) copy-start(bf16[192,512]{1,0:T(8,128)(2,1)} %gate_ref.1) | copy-start | bytes 589828
  77.9 21.6 %all-to-all-start.3 = ((bf16[16,48,128]{2,1,0:T(8,128)(2,1)}), bf16[16,48,128]{2,1,0:T(8,128)(2,1)S(1)}, u32[]{:S(2)}, u32[]{:S(2)}) async-start(bf16[16,48,128]{2,1,0:T(8,128)(2,1)} %shard_map.77), calls=%async_computation.3 | async-start | bytes 393216 | tf_op jit(solution)/shard_map/all_to_all | solution.py:329
